TPU v7x, 128 devices: a whole 4x4x4 slice. The times are simulated.
128 devices in a mesh: expert: 16 (over y, x), cuts: 8 (over z, core).
Axes of the slice: x: 4, y: 4, z: 4, core: 2. Of those that a mesh axis runs over, the one named last changes fastest.
Arguments:
- tokens: bfloat16 [16384, 7168], P(('expert', 'cuts')), may hold values from -130 to 130
- out_grad: bfloat16 [16384, 7168], P(('expert', 'cuts')), may hold values from -130 to 130
- combine: float32 [16384, 8], P(('expert', 'cuts')), may hold values from 0.1 to 1
- expert_ids: int32 [16384, 8], P(('expert', 'cuts')), may hold values from 0 to 383, all different within a row; in each aligned block of 128 rows (0 to 127, 128 to 255, ...) at most 4 rows name the same one
- expert_rank: int32 [384], replicated, may hold values from 0 to 383, each once
- gate_weight: bfloat16 [16, 7168, 2048], P('expert', None, 'cuts'), may hold values from -0.0625 to 0.0625
- up_weight: bfloat16 [16, 7168, 2048], P('expert', None, 'cuts'), may hold values from -0.0625 to 0.0625
- down_weight: bfloat16 [16, 2048, 7168], P('expert', 'cuts'), may hold values from -1 to 1
Outputs:
- updates: bfloat16 [16, 3, 7168, 2048], P('expert', None, 'cuts')
Inputs may be any that keep to these rules, and one draw needn't show every extreme that they name: `expert_ids`: each row names 8 different experts; among the rows of one device no expert is named more than 4 times. `expert_rank`: A permutation; the experts of rank under 16 are the hot ones.
All inputs are finite; a program needn't handle non-finite values.
Results may differ from a plain program's by a relative error of at most 0.0058.
Values may be sent and summed in bfloat16 or wider, within the bound.
No kernel may reach another device: no remote copies, remote signals or barrier semaphores. Data moves between devices by JAX's collectives and lax.ppermute only.
A program may use at most 128 MiB of HBM per device.

v0:
```python
import jax
import jax.numpy as jnp
from jax import lax
from jax.sharding import PartitionSpec as P

CAP = 4


EPSILON = 1e-06
ROW_DIMS = (((0,), (0,)), ((), ()))


def dispatch_rows(tokens, out_grad, combine, expert_ids, expert_rank, hot_count, capacity):
    tok_count = expert_ids.shape[0]
    routed = expert_rank.shape[0]
    id_match = (expert_ids[:, :, None] == jnp.arange(routed, dtype=jnp.int32)).astype(jnp.int32)
    rank_of = jnp.sum(id_match * expert_rank, axis=2)
    hot_hits = (rank_of[:, :, None] == jnp.arange(hot_count, dtype=jnp.int32)).astype(jnp.int32)
    flat_hits = hot_hits.reshape(-1, hot_count)
    before = jnp.cumsum(flat_hits, axis=0) - flat_hits
    slot_index = jnp.sum(before * flat_hits, axis=1).reshape(tok_count, -1)
    placed = (slot_index[:, :, None] == jnp.arange(capacity, dtype=jnp.int32)).astype(jnp.float32)
    hot_float = hot_hits.astype(jnp.float32)
    select = jnp.einsum("tkh,tkc->hct", hot_float, placed)
    scaled = jnp.einsum(
        "tkh,tkc,tk->hct", hot_float, placed, combine, precision=lax.Precision.HIGHEST
    )
    width = tokens.shape[1]
    tok_rows = jnp.dot(
        select.reshape(hot_count * capacity, tok_count).astype(jnp.bfloat16),
        tokens,
        preferred_element_type=jnp.float32,
    ).astype(jnp.bfloat16)
    grad_rows = jnp.dot(
        scaled.reshape(hot_count * capacity, tok_count),
        out_grad.astype(jnp.float32),
        precision=lax.Precision.HIGHEST,
    ).astype(jnp.bfloat16)
    return (
        tok_rows.reshape(hot_count, capacity, width),
        grad_rows.reshape(hot_count, capacity, width),
    )


def expert_acts(x_rows, g_rows, w_gate, w_up, w_down):
    gate_act = jnp.dot(x_rows, w_gate, preferred_element_type=jnp.float32)
    up_act = jnp.dot(x_rows, w_up, preferred_element_type=jnp.float32)
    sigmoid_gate = jax.nn.sigmoid(gate_act)
    hidden = (gate_act * sigmoid_gate * up_act).astype(jnp.bfloat16)
    act_grad = lax.dot_general(
        g_rows, w_down, (((1,), (1,)), ((), ())), preferred_element_type=jnp.float32
    )
    gate_grad = (act_grad * up_act * sigmoid_gate * (1.0 + gate_act * (1.0 - sigmoid_gate))).astype(
        jnp.bfloat16
    )
    up_grad = (act_grad * gate_act * sigmoid_gate).astype(jnp.bfloat16)
    return jnp.stack([gate_grad, up_grad, hidden])


def weight_products(x_rows, g_rows, stacked):
    return jnp.stack(
        [
            lax.dot_general(x_rows, stacked[0], ROW_DIMS, preferred_element_type=jnp.float32),
            lax.dot_general(x_rows, stacked[1], ROW_DIMS, preferred_element_type=jnp.float32),
            lax.dot_general(g_rows, stacked[2], ROW_DIMS, preferred_element_type=jnp.float32),
        ]
    )


def norm_factor(values, entry_count):
    local_squares = jnp.sum(values * values, axis=(1, 2))
    total = lax.psum(local_squares, "cuts")
    return lax.rsqrt(total / entry_count + EPSILON)


def body(tokens, out_grad, combine, expert_ids, expert_rank, gate_weight, up_weight, down_weight):
    hot_count = lax.axis_size("expert")
    cut_count = lax.axis_size("cuts")
    width = tokens.shape[1]
    columns = gate_weight.shape[2]
    full_hidden = columns * cut_count
    tok_rows, grad_rows = dispatch_rows(
        tokens, out_grad, combine, expert_ids, expert_rank, hot_count, CAP
    )
    w_gate = gate_weight[0]
    w_up = up_weight[0]
    w_down = down_weight[0]
    send_tok = jnp.repeat(tok_rows, cut_count, axis=0)
    send_grad = jnp.repeat(grad_rows, cut_count, axis=0)
    got_tok, got_grad = (
        lax.all_to_all(send_tok, ("expert", "cuts"), split_axis=0, concat_axis=0, tiled=True),
        lax.all_to_all(send_grad, ("expert", "cuts"), split_axis=0, concat_axis=0, tiled=True),
    )
    x_all = got_tok.reshape(-1, width)
    g_all = got_grad.reshape(-1, width)
    stacked = expert_acts(x_all, g_all, w_gate, w_up, w_down)
    gradients = weight_products(x_all, g_all, stacked)
    factor = norm_factor(gradients, width * full_hidden)
    normalized = (gradients * factor[:, None, None]).astype(jnp.bfloat16)
    owned = lax.all_to_all(normalized, "cuts", split_axis=1, concat_axis=2, tiled=True)
    return owned[None]


def solution(mesh):
    return jax.shard_map(
        body,
        mesh=mesh,
        in_specs=(
            P(("expert", "cuts"), None),
            P(("expert", "cuts"), None),
            P(("expert", "cuts"), None),
            P(("expert", "cuts"), None),
            P(),
            P("expert", None, "cuts"),
            P("expert", None, "cuts"),
            P("expert", "cuts", None),
        ),
        out_specs=P("expert", None, "cuts", None),
        check_vma=False,
    )
```

profile of v0, /device:TPU:1, one launch (start us, length us, event | category | flops | bytes accessed | tf_op | source)
XLA Modules:
  0.0 487.5 jit_solution(7493327397267218885)
XLA Ops:
  0.0 0.0 copy-start
  0.0 0.9 copy.29
  0.9 3.1 select_reduce_fusion
  4.0 0.1 eq.67
  4.1 0.1 eq.63
  4.2 4.5 reduce-window.6
  8.7 0.1 slice.8
  8.8 0.1 copy.30
  9.0 0.1 copy.31
  9.0 0.1 broadcast_add_fusion
  9.2 0.1 eq.71
  9.3 0.3 fusion.6
  9.6 0.1 copy.32
  9.7 0.0 copy-done
  9.7 0.4 convolution_convert_fusion.1
  10.1 0.3 reshape.47
  10.5 5.3 %broadcast_in_dim.6 = bf16[16,8,4,7168]{3,2,1,0:T(4,128)(2,1)} broadcast(bf16[16,4,7168]{2,1,0:T(4,128)(2,1)S(1)} %reshape.47), dimensions={0,2,3} | broadcast | bytes 8257536 | tf_op jit(solution)/shard_map/broadcast_in_dim | solution.py:88
  15.7 11.9 %all-to-all-start = ((bf16[128,4,7168]{2,1,0:T(4,128)(2,1)}), bf16[128,4,7168]{2,1,0:T(4,128)(2,1)}, u32[]{:S(2)}, u32[]{:S(2)}) async-start(bf16[128,4,7168]{2,1,0:T(4,128)(2,1)} %bitcast.57), calls=%async_computation | async-start | bytes 14680064 | tf_op jit(solution)/shard_map/all_to_all | solution.py:91
  27.6 0.1 copy.33
  27.7 1.0 convolution_bitcast_fusion.3
  28.8 0.1 copy.34
  28.9 2.4 convolution_convert_fusion
  31.3 0.3 reshape.51
  31.6 85.8 %all-to-all-done = bf16[128,4,7168]{2,1,0:T(4,128)(2,1)} async-done(((bf16[128,4,7168]{2,1,0:T(4,128)(2,1)}), bf16[128,4,7168]{2,1,0:T(4,128)(2,1)}, u32[]{:S(2)}, u32[]{:S(2)}) %all-to-all-start) | async-done | bytes 7340064 | tf_op jit(solution)/shard_map/all_to_all | solution.py:91
  117.4 5.3 %broadcast_in_dim.7 = bf16[16,8,4,7168]{3,2,1,0:T(4,128)(2,1)} broadcast(bf16[16,4,7168]{2,1,0:T(4,128)(2,1)S(1)} %reshape.51), dimensions={0,2,3} | broadcast | bytes 8257536 | tf_op jit(solution)/shard_map/broadcast_in_dim | solution.py:89
  122.7 7.3 %all-to-all-start.1 = ((bf16[128,4,7168]{2,1,0:T(4,128)(2,1)}), bf16[128,4,7168]{2,1,0:T(4,128)(2,1)}, u32[]{:S(2)}, u32[]{:S(2)}) async-start(bf16[128,4,7168]{2,1,0:T(4,128)(2,1)} %bitcast.58), calls=%async_computation.1 | async-start | bytes 14680064 | tf_op jit(solution)/shard_map/all_to_all | solution.py:92
  130.0 12.1 %reshape.49 = bf16[512,7168]{1,0:T(8,128)(2,1)} reshape(bf16[128,4,7168]{2,1,0:T(4,128)(2,1)} %all-to-all-done) | data formatting | bytes 14680064 | tf_op jit(solution)/shard_map/reshape | solution.py:94
  142.1 6.3 %fusion = f32[512,256]{1,0:T(8,128)S(1)} fusion(bf16[512,7168]{1,0:T(8,128)(2,1)} %reshape.49, bf16[1,7168,256]{2,1,0:T(8,128)(2,1)} %param.13), kind=kOutput, calls=%fused_computation.8 | convolution fusion | flops 1879048192 | bytes 11534336 | tf_op jit(solution)/shard_map/dot_general | solution.py:46
  148.5 0.0 copy-done.5
  148.5 0.9 copy-done.8
  149.4 2.1 fusion.2
  151.4 68.3 %all-to-all-done.1 = bf16[128,4,7168]{2,1,0:T(4,128)(2,1)} async-done(((bf16[128,4,7168]{2,1,0:T(4,128)(2,1)}), bf16[128,4,7168]{2,1,0:T(4,128)(2,1)}, u32[]{:S(2)}, u32[]{:S(2)}) %all-to-all-start.1) | async-done | bytes 7340064 | tf_op jit(solution)/shard_map/all_to_all | solution.py:92
  219.8 12.1 %reshape.53 = bf16[512,7168]{1,0:T(8,128)(2,1)} reshape(bf16[128,4,7168]{2,1,0:T(4,128)(2,1)} %all-to-all-done.1) | data formatting | bytes 14680064 | tf_op jit(solution)/shard_map/reshape | solution.py:95
  231.9 6.4 %fusion.4 = f32[512,256]{1,0:T(8,128)S(1)} fusion(bf16[512,7168]{1,0:T(8,128)(2,1)} %reshape.53, bf16[1,256,7168]{2,1,0:T(8,128)(2,1)} %param.15), kind=kOutput, calls=%fused_computation.12 | convolution fusion | flops 1879048192 | bytes 11534336 | tf_op jit(solution)/shard_map/dot_general | solution.py:50
  238.2 0.0 slice-start.1
  238.2 2.3 convolution_bitcast_fusion
  240.6 2.3 convolution_bitcast_fusion.2
  242.9 2.2 convolution_bitcast_fusion.1
  245.1 0.0 copy-done.2
  245.1 0.7 copy-done.3
  245.8 3.0 copy-done.4
  248.8 2.5 multiply_reduce_fusion
  251.3 11.7 %psum.7 = f32[3]{0:T(128)S(1)} all-reduce(f32[3]{0:T(128)S(1)} %multiply_reduce_fusion), channel_id=1, replica_groups=mesh['expert'=16,'cuts'=8] {'cuts'}, use_global_device_ids=true, to_apply=%region_5.6 | all-reduce | flops 3 | bytes 24 | tf_op jit(solution)/shard_map/psum | solution.py:72
  263.1 12.4 %multiply_convert_fusion = bf16[3,7168,256]{2,1,0:T(8,128)(2,1)} fusion(f32[1,7168,256]{2,1,0:T(8,128)} %copy-done.2, f32[1,7168,256]{2,1,0:T(8,128)} %copy-done.4, f32[1,7168,256]{2,1,0:T(8,128)} %copy-done.3, f32[3]{0:T(128)S(1)} %add_rsqrt_fusion), kind=kLoop, calls=%fused_computation.1 | loop fusion | flops 22020096 | bytes 33030156 | tf_op jit(solution)/shard_map/convert_element_type | solution.py:99
  275.5 15.8 %copy.35 = bf16[3,7168,256]{2,0,1:T(4,128)(2,1)S(1)} copy(bf16[3,7168,256]{2,1,0:T(8,128)(2,1)} %multiply_convert_fusion) | data formatting | bytes 22020096 | tf_op jit(solution)/shard_map/convert_element_type | solution.py:99
  291.3 168.2 %all_to_all.25 = bf16[3,7168,256]{2,0,1:T(4,128)(2,1)S(1)} all-to-all(bf16[3,7168,256]{2,0,1:T(4,128)(2,1)S(1)} %copy.35), channel_id=1, replica_groups=mesh['expert'=16,'cuts'=8] {'cuts'}, dimensions={1} | all-to-all | bytes 22020096 | tf_op jit(solution)/shard_map/all_to_all | solution.py:100
  459.5 10.6 %copy.36 = bf16[3,896,8,256]{3,2,1,0:T(8,128)(2,1)} copy(bf16[3,896,8,256]{3,0,1,2:T(4,128)(2,1)S(1)} %bitcast.56) | data formatting | bytes 22020096 | tf_op jit(solution)/shard_map/all_to_all | solution.py:100
  470.1 17.4 %broadcast_in_dim.8 = bf16[1,3,896,2048]{3,2,1,0:T(8,128)(2,1)} reshape(bf16[3,896,8,256]{3,2,1,0:T(8,128)(2,1)} %copy.36) | data formatting | bytes 22020096 | tf_op jit(solution)/shard_map/broadcast_in_dim | solution.py:101
  (20 shorter events, 0.1 us)
Async XLA Ops:
  0.0 9.7 %copy-start = (bf16[128,7168]{1,0:T(8,128)(2,1)S(1)}, bf16[128,7168]{1,0:T(8,128)(2,1)}, u32[]{:S(2)}) copy-start(bf16[128,7168]{1,0:T(8,128)(2,1)} %param.8) | copy-start | bytes 5505028
  15.7 11.9 %copy-start.7 = (f32[128,8]{0,1:T(8,128)S(1)}, f32[128,8]{0,1:T(8,128)}, u32[]{:S(2)}) copy-start(f32[128,8]{0,1:T(8,128)} %param.10) | copy-start | bytes 12292
  15.7 101.7 %all-to-all-start = ((bf16[128,4,7168]{2,1,0:T(4,128)(2,1)}), bf16[128,4,7168]{2,1,0:T(4,128)(2,1)}, u32[]{:S(2)}, u32[]{:S(2)}) async-start(bf16[128,4,7168]{2,1,0:T(4,128)(2,1)} %bitcast.57), calls=%async_computation | async-start | bytes 14680064 | tf_op jit(solution)/shard_map/all_to_all | solution.py:91
  122.7 97.1 %all-to-all-start.1 = ((bf16[128,4,7168]{2,1,0:T(4,128)(2,1)}), bf16[128,4,7168]{2,1,0:T(4,128)(2,1)}, u32[]{:S(2)}, u32[]{:S(2)}) async-start(bf16[128,4,7168]{2,1,0:T(4,128)(2,1)} %bitcast.58), calls=%async_computation.1 | async-start | bytes 14680064 | tf_op jit(solution)/shard_map/all_to_all | solution.py:92
  142.1 6.3 %copy-start.5 = (bf16[512,7168]{1,0:T(8,128)(2,1)S(1)}, bf16[512,7168]{1,0:T(8,128)(2,1)}, u32[]{:S(2)}) copy-start(bf16[512,7168]{1,0:T(8,128)(2,1)} %reshape.49) | copy-start | bytes 22020100
  142.1 7.3 %copy-start.8 = (bf16[1,7168,256]{2,1,0:T(8,128)(2,1)S(1)}, bf16[1,7168,256]{2,1,0:T(8,128)(2,1)}, u32[]{:S(2)}) copy-start(bf16[1,7168,256]{2,1,0:T(8,128)(2,1)} %param.14) | copy-start | bytes 11010052
  231.8 6.4 %copy-start.6 = (bf16[512,7168]{1,0:T(8,128)(2,1)S(1)}, bf16[512,7168]{1,0:T(8,128)(2,1)}, u32[]{:S(2)}) copy-start(bf16[512,7168]{1,0:T(8,128)(2,1)} %reshape.53) | copy-start | bytes 22020100
  231.9 8.7 %slice-start = ((s8[7340032]{0:T(1024)(128)(4,1)}), s8[4194304]{0:T(1024)(128)(4,1)S(1)}, s32[]{:S(2)}) async-start(s8[7340032]{0:T(1024)(128)(4,1)} %bitcast.59), calls=%async_computation.3 | async-start | bytes 8388608
  238.2 2.3 slice-start.1
  240.5 4.6 copy-start.2
  242.9 2.9 copy-start.3
  245.8 3.0 copy-start.4
  459.5 28.0 %copy-start.1 = (bf16[128,7168]{1,0:T(8,128)(2,1)S(1)}, bf16[128,7168]{1,0:T(8,128)(2,1)}, u32[]{:S(2)}) copy-start(bf16[128,7168]{1,0:T(8,128)(2,1)} %param.8) | copy-start | bytes 5505028
where the time goes:
time: 489 us; the launch traced here: 488 us
  blocking collectives  180 us (37%)
  waiting for transfers between devices  154 us (31%)
  local copies, waits for them, and re-layouts  85.6 us (18%)
  matrix products  25.7 us (5%)
  other arithmetic  22.7 us (5%)
  starting transfers between devices  19.2 us (4%)
    all_to_all x1, blocking collectives, body(): lax.all_to_all(normalized, 'cuts', split_axis=1, concat_axis=2, tiled=True)  168 us
    all_to_all x1, waiting for transfers between devices, body(): lax.all_to_all(send_tok, ('expert', 'cuts'), split_axis=0, concat_axis=0,...  85.8 us
    all_to_all x1, waiting for transfers between devices, body(): lax.all_to_all(send_grad, ('expert', 'cuts'), split_axis=0, concat_axis=0...  68.3 us
    broadcast_in_dim x1, local copies, waits for them, and re-layouts, body(): return owned[None]  17.4 us
    convert_element_type x1, local copies, waits for them, and re-layouts, body(): normalized = (gradients * factor[:, None, None]).astype(jnp.bfloat16)  15.8 us
    convert_element_type x1, other arithmetic, body(): normalized = (gradients * factor[:, None, None]).astype(jnp.bfloat16)  12.4 us
    reshape x1, local copies, waits for them, and re-layouts, body(): x_all = got_tok.reshape(-1, width)  12.1 us
    reshape x1, local copies, waits for them, and re-layouts, body(): g_all = got_grad.reshape(-1, width)  12.1 us
  transfers between devices with their start and end apart: 2, of which 2 were waited for; matrix products, arithmetic and copies ran while one was open for 5% of the time, Pallas kernels for 0%

commit v1 on v0

v1 whole, which is shorter than its diff:
```python
import functools

import jax
import jax.numpy as jnp
from jax import lax
from jax.experimental import pallas as pl
from jax.experimental.pallas import tpu as pltpu
from jax.sharding import Mesh
from jax.sharding import PartitionSpec as P

CAP = 4
EPSILON = 1e-06
TILE = 896
F32 = jnp.float32
BF16 = jnp.bfloat16
ANY = pl.BlockSpec(memory_space=pl.ANY)
VMEM = pl.BlockSpec(memory_space=pltpu.VMEM)
SMEM = pl.BlockSpec(memory_space=pltpu.SMEM)


def params(mib):
    return pltpu.CompilerParams(vmem_limit_bytes=mib * 1024 * 1024)


def iota(shape, dim):
    return lax.broadcasted_iota(jnp.int32, shape, dim)


def dispatch_kernel(ids_ref, comb_ref, rank_ref, tok_ref, grad_ref, out_ref, sel_ref, scale_ref):
    rows = out_ref.shape[0]
    toks = tok_ref.shape[0]

    @pl.when(pl.program_id(0) == 0)
    def _():
        ranks = rank_ref[...]
        routed = ranks.shape[1]
        expert_row = iota((rows, routed), 0) // (2 * CAP)
        ident = jnp.sum(
            jnp.where(ranks == expert_row, iota((rows, routed), 1), 0), axis=1, keepdims=True
        )
        hit = jnp.zeros((rows, toks), F32)
        comb = jnp.zeros((rows, toks), F32)
        for k in range(ids_ref.shape[0]):
            same = ids_ref[k : k + 1, :] == ident
            hit = jnp.where(same, 1.0, hit)
            comb = jnp.where(same, comb_ref[k : k + 1, :], comb)
        earlier = (iota((toks, toks), 0) < iota((toks, toks), 1)).astype(BF16)
        slot = jnp.dot(hit.astype(BF16), earlier, preferred_element_type=F32)
        row = iota((rows, toks), 0)
        want = (row % CAP).astype(F32)
        is_grad = (row // CAP) % 2 == 1
        sel = jnp.where(slot == want, hit, 0.0)
        sel_ref[:, :toks] = jnp.where(is_grad, 0.0, sel).astype(BF16)
        sel_ref[:, toks:] = jnp.where(is_grad, sel, 0.0).astype(BF16)
        weight = jnp.sum(sel * comb, axis=1, keepdims=True)
        scale_ref[...] = jnp.where(is_grad, weight, 1.0)

    both = jnp.concatenate([tok_ref[...], grad_ref[...]], axis=0)
    picked = jnp.dot(sel_ref[...], both, preferred_element_type=F32)
    out_ref[...] = (picked * scale_ref[:, :1]).astype(BF16)


def dispatch(ids, comb, ranks, tokens, out_grad, first, tiles, rows):
    toks = tokens.shape[0]
    whole = lambda j: (0, 0)
    piece = lambda j: (0, j + first)
    return pl.pallas_call(
        dispatch_kernel,
        grid=(tiles,),
        in_specs=[
            pl.BlockSpec(ids.shape, whole),
            pl.BlockSpec(comb.shape, whole),
            pl.BlockSpec(ranks.shape, whole),
            pl.BlockSpec((toks, TILE), piece),
            pl.BlockSpec((toks, TILE), piece),
        ],
        out_specs=pl.BlockSpec((rows, TILE), lambda j: (0, j)),
        out_shape=jax.ShapeDtypeStruct((rows, tiles * TILE), BF16),
        scratch_shapes=[pltpu.VMEM((rows, 2 * toks), BF16), pltpu.VMEM((rows, toks), F32)],
        compiler_params=params(16),
        name="dispatch",
    )(ids, comb, ranks, tokens, out_grad)


def split_kernel(in_ref, out_ref):
    rows = in_ref.shape[0]
    half = rows // 2
    r, c = iota((rows, rows), 0), iota((rows, rows), 1)
    group = r % half
    source = (group // CAP) * (2 * CAP) + (r // half) * CAP + group % CAP
    perm = (c == source).astype(BF16)
    out_ref[...] = jnp.dot(perm, in_ref[...], preferred_element_type=F32).astype(BF16)


def split_rows(block):
    rows, width = block.shape
    spec = pl.BlockSpec((rows, TILE), lambda j: (0, j))
    return pl.pallas_call(
        split_kernel,
        grid=(width // TILE,),
        in_specs=[spec],
        out_specs=spec,
        out_shape=jax.ShapeDtypeStruct(block.shape, BF16),
        compiler_params=params(16),
        name="split_rows",
    )(block)


def shift(n, k):
    return [(i, (i + k) % n) for i in range(n)]


def gather_z(block, half):
    up = lax.ppermute(block, "z", shift(4, 1))
    down = lax.ppermute(block, "z", shift(4, 3))
    far_a = lax.ppermute(up[:half], "z", shift(4, 1))
    far_b = lax.ppermute(down[half:], "z", shift(4, 3))
    return [block, up, down, far_a, far_b]


def gather_cuts(block, half):
    mine = gather_z(block, half)
    other = [lax.ppermute(t, "core", shift(2, 1)) for t in mine]
    return mine + other


def canon_blocks():
    z, c = lax.axis_index("z"), lax.axis_index("core")
    out = []
    for core in (c, 1 - c):
        for dz in (0, 3, 1, 2):
            out.append(((z + dz) % 4) * 2 + core)
    return jnp.stack(out).astype(jnp.int32)


def fetch_rows(order_ref, blocks, x_s, g_s, column, width, x_sem, g_sem):
    span = pl.ds(column, width)
    n = x_s.shape[0] // 8
    for i in range(8):
        own, up, down, far_a, far_b = blocks[5 * (i // 4) : 5 * (i // 4) + 5]
        at = pl.ds(pl.multiple_of(order_ref[i] * n, n), n)
        kind = i % 4
        if kind < 3:
            ref = (own, up, down)[kind]
            xs, gs = ref.at[pl.ds(0, n), span], ref.at[pl.ds(n, n), span]
        else:
            xs, gs = far_a.at[:, span], far_b.at[:, span]
        pltpu.make_async_copy(xs, x_s.at[at, :], x_sem).start()
        pltpu.make_async_copy(gs, g_s.at[at, :], g_sem).start()


def act_dots(x_s, g_s, wg_s, wu_s, wd_s, gate, up, act):
    gate[...] += jnp.dot(x_s[...], wg_s[...], preferred_element_type=F32)
    up[...] += jnp.dot(x_s[...], wu_s[...], preferred_element_type=F32)
    act[...] += lax.dot_general(
        g_s[...], wd_s[...], (((1,), (1,)), ((), ())), preferred_element_type=F32
    )


def acts_kernel(first, tiles, last, order_ref, *refs):
    blocks = refs[:10]
    wg, wu, wd = refs[10:13]
    refs = refs[13:]
    if last:
        before, out_ref = refs[0], refs[1]
        x_s, g_s, wg_s, wu_s, wd_s, acc, sems = refs[2:]
    else:
        acc = refs[0]
        x_s, g_s, wg_s, wu_s, wd_s, sems = refs[1:]
    for j in range(tiles):
        rows = pl.ds((first + j) * TILE, TILE)
        fetch_rows(
            order_ref, blocks, x_s.at[j], g_s.at[j], j * TILE, TILE, sems.at[0, j], sems.at[1, j]
        )
        pltpu.make_async_copy(wg.at[rows, :], wg_s.at[j], sems.at[2, j]).start()
        pltpu.make_async_copy(wu.at[rows, :], wu_s.at[j], sems.at[3, j]).start()
        pltpu.make_async_copy(wd.at[:, rows], wd_s.at[j], sems.at[4, j]).start()
    if last:
        acc[...] = before[...]
    else:
        acc[...] = jnp.zeros_like(acc)

    @pl.loop(0, tiles)
    def _(j):
        for k, ref in enumerate((x_s, g_s, wg_s, wu_s, wd_s)):
            pltpu.make_async_copy(ref.at[j], ref.at[j], sems.at[k, j]).wait()
        act_dots(
            x_s.at[j], g_s.at[j], wg_s.at[j], wu_s.at[j], wd_s.at[j],
            acc.at[0], acc.at[1], acc.at[2],
        )

    if last:
        n = acc.shape[2]
        step = 64

        @pl.loop(0, acc.shape[1] // step)
        def _(i):
            at = pl.ds(i * step, step)
            gate, up, act = acc[0, at, :], acc[1, at, :], acc[2, at, :]
            sig = jax.nn.sigmoid(gate)
            out_ref[at, 0:n] = (act * up * sig * (1.0 + gate * (1.0 - sig))).astype(BF16)
            out_ref[at, n : 2 * n] = (act * gate * sig).astype(BF16)
            out_ref[at, 2 * n : 3 * n] = (gate * sig * up).astype(BF16)


def acts(order, blocks, wg, wu, wd, first, before):
    n = wg.shape[1]
    tiles = blocks[0].shape[1] // TILE
    rows = 4 * blocks[0].shape[0]
    last = before is not None
    scratch = [
        pltpu.VMEM((tiles, rows, TILE), BF16),
        pltpu.VMEM((tiles, rows, TILE), BF16),
        pltpu.VMEM((tiles, TILE, n), BF16),
        pltpu.VMEM((tiles, TILE, n), BF16),
        pltpu.VMEM((tiles, n, TILE), BF16),
    ]
    if last:
        scratch.append(pltpu.VMEM((3, rows, n), F32))
        out = jax.ShapeDtypeStruct((rows, 3 * n), BF16)
    else:
        out = jax.ShapeDtypeStruct((3, rows, n), F32)
    scratch.append(pltpu.SemaphoreType.DMA((5, tiles)))
    return pl.pallas_call(
        functools.partial(acts_kernel, first, tiles, last),
        in_specs=[SMEM] + [ANY] * 13 + ([VMEM] if last else []),
        out_specs=VMEM,
        out_shape=out,
        scratch_shapes=scratch,
        compiler_params=params(40),
        cost_estimate=pl.CostEstimate(
            flops=6 * rows * tiles * TILE * n,
            bytes_accessed=4 * rows * tiles * TILE + 6 * n * tiles * TILE,
            transcendentals=0,
        ),
        name="acts",
    )(order, *blocks, wg, wu, wd, *([before] if last else []))


def squares_kernel(tiles_a, tiles, order_ref, *refs):
    blocks_a, blocks_b, hid = refs[:10], refs[10:20], refs[20]
    sums_ref, xt_ref, gt_ref = refs[21:24]
    x_s, g_s, hid_t, parts, sems = refs[24:]
    for j in range(tiles):
        blocks, column = (blocks_a, j) if j < tiles_a else (blocks_b, j - tiles_a)
        fetch_rows(
            order_ref, blocks, x_s.at[j], g_s.at[j], column * TILE, TILE, sems.at[0, j], sems.at[1, j]
        )
    n = hid.shape[1] // 3
    hid_t[...] = hid[...].T
    parts[...] = jnp.zeros_like(parts)

    @pl.loop(0, tiles)
    def _(j):
        for k, ref in enumerate((x_s, g_s)):
            pltpu.make_async_copy(ref.at[j], ref.at[j], sems.at[k, j]).wait()

        @pl.when(j == order_ref[0])
        def _():
            xt_ref[...] = x_s[j].T
            gt_ref[...] = g_s[j].T

        for m in range(3):
            src = g_s if m == 2 else x_s
            for h in range(0, n, 128):
                grads = jnp.dot(
                    hid_t[m * n + h : m * n + h + 128, :], src[j], preferred_element_type=F32
                )
                sq = grads * grads
                parts[m] += jnp.sum(sq.reshape(16, 8, TILE), axis=0)

    row = iota((8, 128), 0)
    result = jnp.zeros((8, 128), F32)
    for m in range(3):
        result = jnp.where(row == m, jnp.sum(parts[m]), result)
    sums_ref[...] = result


def squares(order, blocks_a, blocks_b, hid):
    tiles_a = blocks_a[0].shape[1] // TILE
    tiles = tiles_a + blocks_b[0].shape[1] // TILE
    rows = hid.shape[0]
    return pl.pallas_call(
        functools.partial(squares_kernel, tiles_a, tiles),
        in_specs=[SMEM] + [ANY] * 20 + [VMEM],
        out_specs=(VMEM, VMEM, VMEM),
        out_shape=(
            jax.ShapeDtypeStruct((8, 128), F32),
            jax.ShapeDtypeStruct((TILE, rows), BF16),
            jax.ShapeDtypeStruct((TILE, rows), BF16),
        ),
        scratch_shapes=[
            pltpu.VMEM((tiles, rows, TILE), BF16),
            pltpu.VMEM((tiles, rows, TILE), BF16),
            pltpu.VMEM((hid.shape[1], rows), BF16),
            pltpu.VMEM((3, 8, TILE), F32),
            pltpu.SemaphoreType.DMA((2, tiles)),
        ],
        compiler_params=params(32),
        cost_estimate=pl.CostEstimate(
            flops=2 * rows * tiles * TILE * hid.shape[1],
            bytes_accessed=4 * rows * tiles * TILE,
            transcendentals=0,
        ),
        name="squares",
    )(order, *blocks_a, *blocks_b, hid)


def final_kernel(entries, order_ref, *refs):
    blocks = refs[:10]
    xt_ref, gt_ref, total_ref, out_ref, hid, stage, in_sems, out_sems = refs[10:]
    half = hid.shape[1] // 2
    for i in range(8):
        own = blocks[5 * (i // 4) : 5 * (i // 4) + 5]
        kind = i % 4
        if kind < 3:
            pltpu.make_async_copy(own[kind], hid.at[i], in_sems.at[i]).start()
        else:
            pltpu.make_async_copy(own[3], hid.at[i, pl.ds(0, half), :], in_sems.at[i]).start()
            pltpu.make_async_copy(own[4], hid.at[i, pl.ds(half, half), :], in_sems.at[i]).start()
    n = hid.shape[2] // 3
    factors = [lax.rsqrt(total_ref[m : m + 1, 0:1] / entries + EPSILON) for m in range(3)]

    def store(slot, i):
        at = pl.ds(pl.multiple_of(order_ref[i] * n, n), n)
        return pltpu.make_async_copy(stage.at[slot], out_ref.at[:, :, at], out_sems.at[slot])

    @pl.loop(0, 8)
    def _(i):
        slot = i % 2
        pltpu.make_async_copy(hid.at[i], hid.at[i], in_sems.at[i]).wait()

        @pl.when(i >= 2)
        def _():
            store(slot, i - 2).wait()

        for m in range(3):
            lhs = gt_ref if m == 2 else xt_ref
            grads = jnp.dot(
                lhs[...], hid[i, :, m * n : (m + 1) * n], preferred_element_type=F32
            )
            stage[slot, m] = (grads * factors[m]).astype(BF16)
        store(slot, i).start()

    store(0, 6).wait()
    store(1, 7).wait()


def final(order, hid_blocks, xt, gt, total, entries):
    rows, width = hid_blocks[0].shape
    n = width // 3
    return pl.pallas_call(
        functools.partial(final_kernel, entries),
        in_specs=[SMEM] + [ANY] * 10 + [VMEM] * 3,
        out_specs=ANY,
        out_shape=jax.ShapeDtypeStruct((3, TILE, 8 * n), BF16),
        scratch_shapes=[
            pltpu.VMEM((8, rows, width), BF16),
            pltpu.VMEM((2, 3, TILE, n), BF16),
            pltpu.SemaphoreType.DMA((8,)),
            pltpu.SemaphoreType.DMA((2,)),
        ],
        compiler_params=params(32),
        name="final",
    )(order, *hid_blocks, xt, gt, total)


def body(tokens, out_grad, combine, expert_ids, expert_rank, gate_weight, up_weight, down_weight):
    width = tokens.shape[1]
    hot = lax.axis_size(("y", "x"))
    rows = hot * 2 * CAP
    ids, comb, ranks = expert_ids.T, combine.T, expert_rank[None]
    wg, wu, wd = gate_weight[0], up_weight[0], down_weight[0]
    order = canon_blocks()
    tiles = width // TILE
    split = 3
    gathered = []
    for first, count in ((0, split), (split, tiles - split)):
        sent = dispatch(ids, comb, ranks, tokens, out_grad, first, count, rows)
        sent = sent.reshape(hot, 2 * CAP, count * TILE)
        got = lax.all_to_all(sent, ("y", "x"), split_axis=0, concat_axis=0, tiled=True)
        block = split_rows(got.reshape(rows, count * TILE))
        gathered.append(gather_cuts(block, rows // 2))
    part = acts(order, gathered[0], wg, wu, wd, 0, None)
    hid = acts(order, gathered[1], wg, wu, wd, split, part)
    hid_blocks = gather_cuts(hid, hid.shape[0] // 2)
    sums, xt, gt = squares(order, gathered[0], gathered[1], hid)
    total = lax.psum(sums, ("z", "core"))
    entries = width * wg.shape[1] * 8
    return final(order, hid_blocks, xt, gt, total, entries)[None]


def solution(mesh):
    fine = Mesh(mesh.devices.reshape(4, 4, 4, 2), ("y", "x", "z", "core"))
    expert, cuts = ("y", "x"), ("z", "core")
    tokens = P(expert + cuts, None)
    return jax.shard_map(
        body,
        mesh=fine,
        in_specs=(
            tokens,
            tokens,
            tokens,
            tokens,
            P(),
            P(expert, None, cuts),
            P(expert, None, cuts),
            P(expert, cuts, None),
        ),
        out_specs=P(expert, None, cuts, None),
        check_vma=False,
    )
```

time: 489 us -> 208 us (0.43)
  blocking collectives: 180 us -> 11.8 us
  waiting for transfers between devices: 154 us -> 73.6 us
  local copies, waits for them, and re-layouts: 85.6 us -> 28.5 us
  Pallas kernels: 0 us -> 43.9 us
  starting transfers between devices: 19.2 us -> 48.3 us
  matrix products: 25.7 us -> 0 us
  other arithmetic: 22.7 us -> 0 us
    all_to_all x1 -> x0, blocking collectives: 168 us -> none  [body(): lax.all_to_all(normalized, 'cuts', split_axis=1, concat_axis=2, tiled=True)]
    all_to_all x2, waiting for transfers between devices: 154 us -> 17.8 us  [body(): lax.all_to_all(sent, ('y', 'x'), split_axis=0, concat_axis=0, tiled=True)]
    ppermute x0 -> x27, waiting for transfers between devices: none -> 55.9 us  [the longest x3 34.3 us: gather_z(): far_b = lax.ppermute(down[half:], 'z', shift(4, 3))]
    pallas_call x0 -> x8, Pallas kernels: none -> 43.9 us  [the longest x2 14.3 us: acts(): pl.pallas_call(functools.partial(acts_kernel, first, tiles, last), in_spe...]
    ppermute x0 -> x27, starting transfers between devices: none -> 36.6 us  [the longest x15 21.4 us: gather_cuts(): other = [lax.ppermute(t, 'core', shift(2, 1)) for t in mine]]
    broadcast_in_dim x3 -> x1, local copies, waits for them, and re-layouts: 27.9 us -> 0.68 us  [body(): ids, comb, ranks = (expert_ids.T, combine.T, expert_rank[None])]
    dot_general x10 -> x0, matrix products: 25.7 us -> none  [the longest x1 6.37 us: expert_acts(): lax.dot_general(g_rows, w_down, (((1,), (1,)), ((), ())), preferred_eleme...]
    reshape x4 -> x0, local copies, waits for them, and re-layouts: 24.9 us -> none  [the longest x1 12.1 us: body(): x_all = got_tok.reshape(-1, width)]
  transfers between devices with their start and end apart: 2 -> 29, of which waited for: 2 -> 9; matrix products, arithmetic and copies ran while one was open for 5% -> 3% of each run, Pallas kernels for 0% -> 12%
where the time goes in v1:
time: 208 us; the launch traced here: 207 us
  waiting for transfers between devices  73.6 us (35%)
  starting transfers between devices  48.3 us (23%)
  Pallas kernels  43.9 us (21%)
  local copies, waits for them, and re-layouts  28.5 us (14%)
  blocking collectives  11.8 us (6%)
    ppermute x3, waiting for transfers between devices, gather_z(): far_b = lax.ppermute(down[half:], 'z', shift(4, 3))  34.3 us
    unnamed x66, local copies, waits for them, and re-layouts  22.5 us
    ppermute x15, starting transfers between devices, gather_cuts(): other = [lax.ppermute(t, 'core', shift(2, 1)) for t in mine]  21.4 us
    ppermute x3, waiting for transfers between devices, gather_z(): down = lax.ppermute(block, 'z', shift(4, 3))  17.8 us
    all_to_all x2, waiting for transfers between devices, body(): lax.all_to_all(sent, ('y', 'x'), split_axis=0, concat_axis=0, tiled=True)  17.8 us
    pallas_call x2, Pallas kernels, acts(): pl.pallas_call(functools.partial(acts_kernel, first, tiles, last), in_spe...  14.3 us
    psum x1, blocking collectives, body(): total = lax.psum(sums, ('z', 'core'))  11.8 us
    all_to_all x2, starting transfers between devices, body(): lax.all_to_all(sent, ('y', 'x'), split_axis=0, concat_axis=0, tiled=True)  11.7 us
  transfers between devices with their start and end apart: 29, of which 9 were waited for; matrix products, arithmetic and copies ran while one was open for 3% of the time, Pallas kernels for 12%

profile of v1, /device:TPU:1, one launch (start us, length us, event | category | flops | bytes accessed | tf_op | source)
XLA Modules:
  0.0 206.5 jit_solution(7417252769973109864)
XLA Ops:
  0.7 1.5 copy-done.2
  2.2 1.5 copy-done.4
  5.1 2.4 %dispatch.3 = bf16[128,2688]{1,0:T(8,128)(2,1)} custom-call(s32[8,128]{1,0:T(8,128)S(1)} %bitcast.24, f32[8,128]{1,0:T(8,128)S(1)} %bitcast.26, s32[1,384]{1,0:T(1,128)S(1)} %broadcast_in_dim.6.rank_ref, bf16[128,7168]{1,0:T(8,128)(2,1)S(1)} %copy-done.2, bf16[128,7168]{1,0:T(8,128)(2,1)S(1)} %copy-done.4), custom_call_target="tpu_custom_call" | custom-call | tf_op jit(solution)/shard_map/dispatch/pallas_call | solution.py:67
  7.4 7.7 %all-to-all-start.1 = ((bf16[16,8,2688]{2,1,0:T(8,128)(2,1)}), bf16[16,8,2688]{2,1,0:T(8,128)(2,1)S(1)}, u32[]{:S(2)}, u32[]{:S(2)}) async-start(bf16[16,8,2688]{2,1,0:T(8,128)(2,1)} %bitcast.15), calls=%async_computation.1 | async-start | bytes 1376256 | tf_op jit(solution)/shard_map/all_to_all | solution.py:381
  15.2 1.5 copy-done.5
  16.7 3.3 %dispatch.2 = bf16[128,4480]{1,0:T(8,128)(2,1)} custom-call(s32[8,128]{1,0:T(8,128)S(1)} %bitcast.25, f32[8,128]{1,0:T(8,128)S(1)} %bitcast.27, s32[1,384]{1,0:T(1,128)S(1)} %broadcast_in_dim.6.rank_ref, bf16[128,7168]{1,0:T(8,128)(2,1)S(1)} %copy-done.3, bf16[128,7168]{1,0:T(8,128)(2,1)S(1)} %copy-done.5), custom_call_target="tpu_custom_call" | custom-call | tf_op jit(solution)/shard_map/dispatch/pallas_call | solution.py:67
  20.0 7.3 %all-to-all-done.1 = bf16[16,8,2688]{2,1,0:T(8,128)(2,1)S(1)} async-done(((bf16[16,8,2688]{2,1,0:T(8,128)(2,1)}), bf16[16,8,2688]{2,1,0:T(8,128)(2,1)S(1)}, u32[]{:S(2)}, u32[]{:S(2)}) %all-to-all-start.1) | async-done | bytes 688160 | tf_op jit(solution)/shard_map/all_to_all | solution.py:381
  27.3 3.9 %all-to-all-start = ((bf16[16,8,4480]{2,1,0:T(8,128)(2,1)}), bf16[16,8,4480]{2,1,0:T(8,128)(2,1)S(1)}, u32[]{:S(2)}, u32[]{:S(2)}) async-start(bf16[16,8,4480]{2,1,0:T(8,128)(2,1)} %bitcast.10), calls=%async_computation | async-start | bytes 2293760 | tf_op jit(solution)/shard_map/all_to_all | solution.py:381
  31.2 1.9 split_rows.3.refs_0_
  33.2 3.8 %collective-permute-start.10 = (bf16[128,2688]{1,0:T(8,128)(2,1)}, bf16[128,2688]{1,0:T(8,128)(2,1)}, u32[]{:S(2)}, u32[]{:S(2)}) collective-permute-start(bf16[128,2688]{1,0:T(8,128)(2,1)} %split_rows.3.refs_0_), channel_id=1, source_target_pairs={{0,6},{2,0},{4,2},{6,4},{1,7},{3,1},{5,3},{7,5},{8,14},{10,8},{12,... | collective-permute-start | bytes 2064392 | tf_op jit(solution)/shard_map/ppermute | solution.py:115
  36.9 10.5 %all-to-all-done = bf16[16,8,4480]{2,1,0:T(8,128)(2,1)S(1)} async-done(((bf16[16,8,4480]{2,1,0:T(8,128)(2,1)}), bf16[16,8,4480]{2,1,0:T(8,128)(2,1)S(1)}, u32[]{:S(2)}, u32[]{:S(2)}) %all-to-all-start) | async-done | bytes 1146912 | tf_op jit(solution)/shard_map/all_to_all | solution.py:381
  47.4 1.3 split_rows.2.refs_0_.refs_10_
  48.7 3.8 %collective-permute-start.1 = (bf16[128,4480]{1,0:T(8,128)(2,1)S(1)}, bf16[128,4480]{1,0:T(8,128)(2,1)S(1)}, u32[]{:S(2)}, u32[]{:S(2)}) collective-permute-start(bf16[128,4480]{1,0:T(8,128)(2,1)S(1)} %split_rows.2.refs_0_.refs_10_), channel_id=1, source_target_pairs={{0,6},{2,0},{4,2},{6,4},{1,7},{3,1},{5,3},{7,5},{8,14},{10,8},{12,... | collective-permute-start | bytes 3440648 | tf_op jit(solution)/shard_map/ppermute | solution.py:115
  52.5 1.0 slice.27
  53.6 2.7 %collective-permute-start.12 = (bf16[64,2688]{1,0:T(8,128)(2,1)S(1)}, bf16[64,2688]{1,0:T(8,128)(2,1)S(1)}, u32[]{:S(2)}, u32[]{:S(2)}) collective-permute-start(bf16[64,2688]{1,0:T(8,128)(2,1)S(1)} %slice.27), channel_id=1, source_target_pairs={{0,6},{2,0},{4,2},{6,4},{1,7},{3,1},{5,3},{7,5},{8,14},{10,8},{12,... | collective-permute-start | bytes 1032200 | tf_op jit(solution)/shard_map/ppermute | solution.py:117
  56.3 1.0 slice.26
  57.4 4.2 %collective-permute-start.13 = (bf16[128,2688]{1,0:T(8,128)(2,1)}, bf16[128,2688]{1,0:T(8,128)(2,1)S(1)}, u32[]{:S(2)}, u32[]{:S(2)}) collective-permute-start(bf16[128,2688]{1,0:T(8,128)(2,1)} %split_rows.3.refs_0_), channel_id=1, source_target_pairs={{0,1},{1,0},{2,3},{3,2},{4,5},{5,4},{6,7},{7,6},{8,9},{9,8},{10,11... | collective-permute-start | bytes 2064392 | tf_op jit(solution)/shard_map/ppermute | solution.py:123
  61.6 19.5 %collective-permute-done.12.refs_4_ = bf16[64,2688]{1,0:T(8,128)(2,1)S(1)} collective-permute-done((bf16[64,2688]{1,0:T(8,128)(2,1)S(1)}, bf16[64,2688]{1,0:T(8,128)(2,1)S(1)}, u32[]{:S(2)}, u32[]{:S(2)}) %collective-permute-start.12) | collective-permute-done | bytes 344096 | tf_op jit(solution)/shard_map/ppermute | solution.py:117
  81.1 4.3 %collective-permute-start.15 = (bf16[128,2688]{1,0:T(8,128)(2,1)}, bf16[128,2688]{1,0:T(8,128)(2,1)S(1)}, u32[]{:S(2)}, u32[]{:S(2)}) collective-permute-start(bf16[128,2688]{1,0:T(8,128)(2,1)} %collective-permute-done.10.refs_2_), channel_id=1, source_target_pairs={{0,1},{1,0},{2,3},{3,2},{4,5},{5,4},{6,7},{7,6},{8,9},{9,8},{10,11... | collective-permute-start | bytes 2064392 | tf_op jit(solution)/shard_map/ppermute | solution.py:123
  85.4 3.4 %collective-permute-start.14 = (bf16[128,2688]{1,0:T(8,128)(2,1)}, bf16[128,2688]{1,0:T(8,128)(2,1)S(1)}, u32[]{:S(2)}, u32[]{:S(2)}) collective-permute-start(bf16[128,2688]{1,0:T(8,128)(2,1)} %collective-permute-done.9.refs_1_), channel_id=1, source_target_pairs={{0,1},{1,0},{2,3},{3,2},{4,5},{5,4},{6,7},{7,6},{8,9},{9,8},{10,11... | collective-permute-start | bytes 2064392 | tf_op jit(solution)/shard_map/ppermute | solution.py:123
  89.4 1.1 slice.24
  96.7 9.4 %collective-permute-done.3.refs_4_.refs_14_ = bf16[64,4480]{1,0:T(8,128)(2,1)} collective-permute-done((bf16[64,4480]{1,0:T(8,128)(2,1)S(1)}, bf16[64,4480]{1,0:T(8,128)(2,1)}, u32[]{:S(2)}, u32[]{:S(2)}) %collective-permute-start.3) | collective-permute-done | bytes 573472 | tf_op jit(solution)/shard_map/ppermute | solution.py:117
  106.1 1.2 collective-permute-start.8
  107.3 1.0 collective-permute-done.2.refs_3_.refs_13_
  108.3 1.5 collective-permute-start.7
  110.0 2.0 copy-done
  112.0 2.0 copy-done.1
  114.0 1.1 copy-done.13
  115.1 1.1 copy-done.16
  116.2 1.0 copy-done.21
  117.2 1.0 copy-done.24
  119.2 6.4 %acts.2.refs_13_ = f32[3,512,256]{2,1,0:T(8,128)S(1)} custom-call(s32[8]{0:T(128)S(1)} %stack.35.order_ref, bf16[128,2688]{1,0:T(8,128)(2,1)} %split_rows.3.refs_0_, bf16[128,2688]{1,0:T(8,128)(2,1)} %collective-permute-done.9.refs_1_, bf16[128,2688]{1,0:T(8,128)(2,1)} %collective-permute-done.10.refs_2_, bf16[64,2688]{1,0:T(8,128)(2,1)S(1)} %copy-done.21, ...), custom_call_target="tpu_custom_call" | custom-call | flops 2113929216 | bytes 9633792 | tf_op jit(solution)/shard_map/acts/pallas_call | solution.py:224
  125.7 7.9 %acts.3.refs_20_.refs_0_ = bf16[512,768]{1,0:T(8,128)(2,1)S(1)} custom-call(s32[8]{0:T(128)S(1)} %stack.35.order_ref, bf16[128,4480]{1,0:T(8,128)(2,1)S(1)} %split_rows.2.refs_0_.refs_10_, bf16[128,4480]{1,0:T(8,128)(2,1)} %collective-permute-done.refs_1_.refs_11_, bf16[128,4480]{1,0:T(8,128)(2,1)S(1)} %collective-permute-done.1.refs_2_.refs_12_, ...), custom_call_target="tpu_custom_call" | custom-call | flops 3523215360 | bytes 16056320 | tf_op jit(solution)/shard_map/acts/pallas_call | solution.py:224
  133.7 1.5 collective-permute-start.18
  135.2 17.8 %collective-permute-done.19.refs_2_ = bf16[512,768]{1,0:T(8,128)(2,1)} collective-permute-done((bf16[512,768]{1,0:T(8,128)(2,1)S(1)}, bf16[512,768]{1,0:T(8,128)(2,1)}, u32[]{:S(2)}, u32[]{:S(2)}) %collective-permute-start.19) | collective-permute-done | bytes 786464 | tf_op jit(solution)/shard_map/ppermute | solution.py:115
  153.0 1.0 slice.29
  154.0 1.5 collective-permute-start.21
  155.5 1.0 slice.28
  156.8 1.3 collective-permute-start.22
  158.7 5.4 %collective-permute-done.21.refs_4_ = bf16[256,768]{1,0:T(8,128)(2,1)S(1)} collective-permute-done((bf16[256,768]{1,0:T(8,128)(2,1)S(1)}, bf16[256,768]{1,0:T(8,128)(2,1)S(1)}, u32[]{:S(2)}, u32[]{:S(2)}) %collective-permute-start.21) | collective-permute-done | bytes 393248 | tf_op jit(solution)/shard_map/ppermute | solution.py:117
  164.0 1.6 collective-permute-start.26
  165.6 2.3 %collective-permute-done.20.refs_3_ = bf16[256,768]{1,0:T(8,128)(2,1)} collective-permute-done((bf16[256,768]{1,0:T(8,128)(2,1)S(1)}, bf16[256,768]{1,0:T(8,128)(2,1)}, u32[]{:S(2)}, u32[]{:S(2)}) %collective-permute-start.20) | collective-permute-done | bytes 393248 | tf_op jit(solution)/shard_map/ppermute | solution.py:116
  167.8 1.8 collective-permute-start.25
  169.7 11.0 %squares.1 = (f32[8,128]{1,0:T(8,128)S(1)}, bf16[896,512]{1,0:T(8,128)(2,1)S(1)}, bf16[896,512]{1,0:T(8,128)(2,1)S(1)}) custom-call(s32[8]{0:T(128)S(1)} %stack.35.order_ref, bf16[128,2688]{1,0:T(8,128)(2,1)} %split_rows.3.refs_0_, bf16[128,2688]{1,0:T(8,128)(2,1)} %collective-permute-done.9.refs_1_, bf16[128,2688]{1,0:T(8,128)(2,1)} %collective-permute-done.10.refs_2_, ...), custom_call_target="tpu_custom_call" | custom-call | flops 5637144576 | bytes 14680064 | tf_op jit(solution)/shard_map/squares/pallas_call | solution.py:283
  182.5 11.8 %psum.7.refs_12_ = f32[8,128]{1,0:T(8,128)S(1)} all-reduce(f32[8,128]{1,0:T(8,128)S(1)} %get-tuple-element.10), channel_id=1, replica_groups=mesh['y'=4,'x'=4,'z'=4,'core'=2] {'z','core'}, use_global_device_ids=true, to_apply=%region_0.1 | all-reduce | flops 1024 | bytes 8192 | tf_op jit(solution)/shard_map/psum | solution.py:388
  194.4 1.2 copy-done.7
  195.5 1.2 copy-done.9
  196.7 9.7 %final.1 = bf16[3,896,2048]{2,1,0:T(8,128)(2,1)} custom-call(s32[8]{0:T(128)S(1)} %stack.35.order_ref, bf16[512,768]{1,0:T(8,128)(2,1)S(1)} %acts.3.refs_20_.refs_0_, bf16[512,768]{1,0:T(8,128)(2,1)} %collective-permute-done.18.refs_1_, bf16[512,768]{1,0:T(8,128)(2,1)} %collective-permute-done.19.refs_2_, bf16[256,768]{1,0:T(8,128)(2,1)} %collective-permute-done.20.refs_3_, ...), custom_call_target="tpu_custom_call" | custom-call | tf_op jit(solution)/shard_map/final/pallas_call | solution.py:352
  (93 shorter events, 12.8 us)
Async XLA Ops:
  0.7 1.5 copy-start.2
  2.2 1.5 copy-start.4
  5.1 10.1 %copy-start.3 = (bf16[128,7168]{1,0:T(8,128)(2,1)S(1)}, bf16[128,7168]{1,0:T(8,128)(2,1)}, u32[]{:S(2)}) copy-start(bf16[128,7168]{1,0:T(8,128)(2,1)} %tok_ref.3) | copy-start | bytes 5505028
  7.4 7.7 %copy-start.30 = (s32[128,8]{0,1:T(8,128)S(1)}, s32[128,8]{0,1:T(8,128)}, u32[]{:S(2)}) copy-start(s32[128,8]{0,1:T(8,128)} %param.11) | copy-start | bytes 12292
  7.4 7.8 %copy-start.32 = (f32[128,8]{0,1:T(8,128)S(1)}, f32[128,8]{0,1:T(8,128)}, u32[]{:S(2)}) copy-start(f32[128,8]{0,1:T(8,128)} %param.10) | copy-start | bytes 12292
  7.4 19.9 %all-to-all-start.1 = ((bf16[16,8,2688]{2,1,0:T(8,128)(2,1)}), bf16[16,8,2688]{2,1,0:T(8,128)(2,1)S(1)}, u32[]{:S(2)}, u32[]{:S(2)}) async-start(bf16[16,8,2688]{2,1,0:T(8,128)(2,1)} %bitcast.15), calls=%async_computation.1 | async-start | bytes 1376256 | tf_op jit(solution)/shard_map/all_to_all | solution.py:381
  15.2 1.5 copy-start.5
  27.3 20.1 %all-to-all-start = ((bf16[16,8,4480]{2,1,0:T(8,128)(2,1)}), bf16[16,8,4480]{2,1,0:T(8,128)(2,1)S(1)}, u32[]{:S(2)}, u32[]{:S(2)}) async-start(bf16[16,8,4480]{2,1,0:T(8,128)(2,1)} %bitcast.10), calls=%async_computation | async-start | bytes 2293760 | tf_op jit(solution)/shard_map/all_to_all | solution.py:381
  33.2 19.4 %collective-permute-start.10 = (bf16[128,2688]{1,0:T(8,128)(2,1)}, bf16[128,2688]{1,0:T(8,128)(2,1)}, u32[]{:S(2)}, u32[]{:S(2)}) collective-permute-start(bf16[128,2688]{1,0:T(8,128)(2,1)} %split_rows.3.refs_0_), channel_id=1, source_target_pairs={{0,6},{2,0},{4,2},{6,4},{1,7},{3,1},{5,3},{7,5},{8,14},{10,8},{12,... | collective-permute-start | bytes 2064392 | tf_op jit(solution)/shard_map/ppermute | solution.py:115
  36.9 19.4 %collective-permute-start.9 = (bf16[128,2688]{1,0:T(8,128)(2,1)}, bf16[128,2688]{1,0:T(8,128)(2,1)}, u32[]{:S(2)}, u32[]{:S(2)}) collective-permute-start(bf16[128,2688]{1,0:T(8,128)(2,1)} %split_rows.3.refs_0_), channel_id=1, source_target_pairs={{0,2},{2,4},{4,6},{6,0},{1,3},{3,5},{5,7},{7,1},{8,10},{10,12},{12... | collective-permute-start | bytes 2064392 | tf_op jit(solution)/shard_map/ppermute | solution.py:114
  48.7 40.1 %collective-permute-start.1 = (bf16[128,4480]{1,0:T(8,128)(2,1)S(1)}, bf16[128,4480]{1,0:T(8,128)(2,1)S(1)}, u32[]{:S(2)}, u32[]{:S(2)}) collective-permute-start(bf16[128,4480]{1,0:T(8,128)(2,1)S(1)} %split_rows.2.refs_0_.refs_10_), channel_id=1, source_target_pairs={{0,6},{2,0},{4,2},{6,4},{1,7},{3,1},{5,3},{7,5},{8,14},{10,8},{12,... | collective-permute-start | bytes 3440648 | tf_op jit(solution)/shard_map/ppermute | solution.py:115
  52.5 36.4 %collective-permute-start = (bf16[128,4480]{1,0:T(8,128)(2,1)S(1)}, bf16[128,4480]{1,0:T(8,128)(2,1)}, u32[]{:S(2)}, u32[]{:S(2)}) collective-permute-start(bf16[128,4480]{1,0:T(8,128)(2,1)S(1)} %split_rows.2.refs_0_.refs_10_), channel_id=1, source_target_pairs={{0,2},{2,4},{4,6},{6,0},{1,3},{3,5},{5,7},{7,1},{8,10},{10,12},{12... | collective-permute-start | bytes 3440648 | tf_op jit(solution)/shard_map/ppermute | solution.py:114
  53.6 27.6 %collective-permute-start.12 = (bf16[64,2688]{1,0:T(8,128)(2,1)S(1)}, bf16[64,2688]{1,0:T(8,128)(2,1)S(1)}, u32[]{:S(2)}, u32[]{:S(2)}) collective-permute-start(bf16[64,2688]{1,0:T(8,128)(2,1)S(1)} %slice.27), channel_id=1, source_target_pairs={{0,6},{2,0},{4,2},{6,4},{1,7},{3,1},{5,3},{7,5},{8,14},{10,8},{12,... | collective-permute-start | bytes 1032200 | tf_op jit(solution)/shard_map/ppermute | solution.py:117
  57.3 28.1 %collective-permute-start.11 = (bf16[64,2688]{1,0:T(8,128)(2,1)S(1)}, bf16[64,2688]{1,0:T(8,128)(2,1)S(1)}, u32[]{:S(2)}, u32[]{:S(2)}) collective-permute-start(bf16[64,2688]{1,0:T(8,128)(2,1)S(1)} %slice.26), channel_id=1, source_target_pairs={{0,2},{2,4},{4,6},{6,0},{1,3},{3,5},{5,7},{7,1},{8,10},{10,12},{12... | collective-permute-start | bytes 1032200 | tf_op jit(solution)/shard_map/ppermute | solution.py:116
  57.4 33.1 %collective-permute-start.13 = (bf16[128,2688]{1,0:T(8,128)(2,1)}, bf16[128,2688]{1,0:T(8,128)(2,1)S(1)}, u32[]{:S(2)}, u32[]{:S(2)}) collective-permute-start(bf16[128,2688]{1,0:T(8,128)(2,1)} %split_rows.3.refs_0_), channel_id=1, source_target_pairs={{0,1},{1,0},{2,3},{3,2},{4,5},{5,4},{6,7},{7,6},{8,9},{9,8},{10,11... | collective-permute-start | bytes 2064392 | tf_op jit(solution)/shard_map/ppermute | solution.py:123
  81.1 28.8 %copy-start.18 = (bf16[64,2688]{1,0:T(8,128)(2,1)}, bf16[64,2688]{1,0:T(8,128)(2,1)S(1)}, u32[]{:S(2)}) copy-start(bf16[64,2688]{1,0:T(8,128)(2,1)S(1)} %collective-permute-done.12.refs_4_) | copy-start | bytes 1032196
  81.1 11.2 %collective-permute-start.15 = (bf16[128,2688]{1,0:T(8,128)(2,1)}, bf16[128,2688]{1,0:T(8,128)(2,1)S(1)}, u32[]{:S(2)}, u32[]{:S(2)}) collective-permute-start(bf16[128,2688]{1,0:T(8,128)(2,1)} %collective-permute-done.10.refs_2_), channel_id=1, source_target_pairs={{0,1},{1,0},{2,3},{3,2},{4,5},{5,4},{6,7},{7,6},{8,9},{9,8},{10,11... | collective-permute-start | bytes 2064392 | tf_op jit(solution)/shard_map/ppermute | solution.py:123
  85.4 5.1 %copy-start.20 = (bf16[64,2688]{1,0:T(8,128)(2,1)}, bf16[64,2688]{1,0:T(8,128)(2,1)S(1)}, u32[]{:S(2)}) copy-start(bf16[64,2688]{1,0:T(8,128)(2,1)S(1)} %collective-permute-done.11.refs_3_) | copy-start | bytes 1032196
  85.4 10.4 %collective-permute-start.14 = (bf16[128,2688]{1,0:T(8,128)(2,1)}, bf16[128,2688]{1,0:T(8,128)(2,1)S(1)}, u32[]{:S(2)}, u32[]{:S(2)}) collective-permute-start(bf16[128,2688]{1,0:T(8,128)(2,1)} %collective-permute-done.9.refs_1_), channel_id=1, source_target_pairs={{0,1},{1,0},{2,3},{3,2},{4,5},{5,4},{6,7},{7,6},{8,9},{9,8},{10,11... | collective-permute-start | bytes 2064392 | tf_op jit(solution)/shard_map/ppermute | solution.py:123
  88.8 2.3 %collective-permute-start.17 = (bf16[64,2688]{1,0:T(8,128)(2,1)S(1)}, bf16[64,2688]{1,0:T(8,128)(2,1)S(1)}, u32[]{:S(2)}, u32[]{:S(2)}) collective-permute-start(bf16[64,2688]{1,0:T(8,128)(2,1)S(1)} %collective-permute-done.12.refs_4_), channel_id=1, source_target_pairs={{0,1},{1,0},{2,3},{3,2},{4,5},{5,4},{6,7},{7,6},{8,9},{9,8},{10,11... | collective-permute-start | bytes 1032200 | tf_op jit(solution)/shard_map/ppermute | solution.py:123
  88.9 5.2 %collective-permute-start.16 = (bf16[64,2688]{1,0:T(8,128)(2,1)S(1)}, bf16[64,2688]{1,0:T(8,128)(2,1)S(1)}, u32[]{:S(2)}, u32[]{:S(2)}) collective-permute-start(bf16[64,2688]{1,0:T(8,128)(2,1)S(1)} %collective-permute-done.11.refs_3_), channel_id=1, source_target_pairs={{0,1},{1,0},{2,3},{3,2},{4,5},{5,4},{6,7},{7,6},{8,9},{9,8},{10,11... | collective-permute-start | bytes 1032200 | tf_op jit(solution)/shard_map/ppermute | solution.py:123
  90.5 35.1 %copy-start.10 = (bf16[128,2688]{1,0:T(8,128)(2,1)}, bf16[128,2688]{1,0:T(8,128)(2,1)S(1)}, u32[]{:S(2)}) copy-start(bf16[128,2688]{1,0:T(8,128)(2,1)S(1)} %collective-permute-done.13.refs_5_) | copy-start | bytes 2064388
  90.5 35.1 %collective-permute-start.4 = (bf16[128,4480]{1,0:T(8,128)(2,1)S(1)}, bf16[128,4480]{1,0:T(8,128)(2,1)}, u32[]{:S(2)}, u32[]{:S(2)}) collective-permute-start(bf16[128,4480]{1,0:T(8,128)(2,1)S(1)} %split_rows.2.refs_0_.refs_10_), channel_id=1, source_target_pairs={{0,1},{1,0},{2,3},{3,2},{4,5},{5,4},{6,7},{7,6},{8,9},{9,8},{10,11... | collective-permute-start | bytes 3440648 | tf_op jit(solution)/shard_map/ppermute | solution.py:123
  91.8 14.3 %collective-permute-start.3 = (bf16[64,4480]{1,0:T(8,128)(2,1)S(1)}, bf16[64,4480]{1,0:T(8,128)(2,1)}, u32[]{:S(2)}, u32[]{:S(2)}) collective-permute-start(bf16[64,4480]{1,0:T(8,128)(2,1)S(1)} %slice.25), channel_id=1, source_target_pairs={{0,6},{2,0},{4,2},{6,4},{1,7},{3,1},{5,3},{7,5},{8,14},{10,8},{12,... | collective-permute-start | bytes 1720328 | tf_op jit(solution)/shard_map/ppermute | solution.py:117
  93.2 15.2 %collective-permute-start.2 = (bf16[64,4480]{1,0:T(8,128)(2,1)S(1)}, bf16[64,4480]{1,0:T(8,128)(2,1)}, u32[]{:S(2)}, u32[]{:S(2)}) collective-permute-start(bf16[64,4480]{1,0:T(8,128)(2,1)S(1)} %slice.24), channel_id=1, source_target_pairs={{0,2},{2,4},{4,6},{6,0},{1,3},{3,5},{5,7},{7,1},{8,10},{10,12},{12... | collective-permute-start | bytes 1720328 | tf_op jit(solution)/shard_map/ppermute | solution.py:116
  94.9 30.7 %collective-permute-start.6 = (bf16[128,4480]{1,0:T(8,128)(2,1)S(1)}, bf16[128,4480]{1,0:T(8,128)(2,1)}, u32[]{:S(2)}, u32[]{:S(2)}) collective-permute-start(bf16[128,4480]{1,0:T(8,128)(2,1)S(1)} %collective-permute-done.1.refs_2_.refs_12_), channel_id=1, source_target_pairs={{0,1},{1,0},{2,3},{3,2},{4,5},{5,4},{6,7},{7,6},{8,9},{9,8},{10,11... | collective-permute-start | bytes 3440648 | tf_op jit(solution)/shard_map/ppermute | solution.py:123
  96.7 29.0 %collective-permute-start.5 = (bf16[128,4480]{1,0:T(8,128)(2,1)}, bf16[128,4480]{1,0:T(8,128)(2,1)}, u32[]{:S(2)}, u32[]{:S(2)}) collective-permute-start(bf16[128,4480]{1,0:T(8,128)(2,1)} %collective-permute-done.refs_1_.refs_11_), channel_id=1, source_target_pairs={{0,1},{1,0},{2,3},{3,2},{4,5},{5,4},{6,7},{7,6},{8,9},{9,8},{10,11... | collective-permute-start | bytes 3440648 | tf_op jit(solution)/shard_map/ppermute | solution.py:123
  106.1 19.5 %collective-permute-start.8 = (bf16[64,4480]{1,0:T(8,128)(2,1)}, bf16[64,4480]{1,0:T(8,128)(2,1)}, u32[]{:S(2)}, u32[]{:S(2)}) collective-permute-start(bf16[64,4480]{1,0:T(8,128)(2,1)} %collective-permute-done.3.refs_4_.refs_14_), channel_id=1, source_target_pairs={{0,1},{1,0},{2,3},{3,2},{4,5},{5,4},{6,7},{7,6},{8,9},{9,8},{10,11... | collective-permute-start | bytes 1720328 | tf_op jit(solution)/shard_map/ppermute | solution.py:123
  108.3 17.3 %collective-permute-start.7 = (bf16[64,4480]{1,0:T(8,128)(2,1)}, bf16[64,4480]{1,0:T(8,128)(2,1)}, u32[]{:S(2)}, u32[]{:S(2)}) collective-permute-start(bf16[64,4480]{1,0:T(8,128)(2,1)} %collective-permute-done.2.refs_3_.refs_13_), channel_id=1, source_target_pairs={{0,1},{1,0},{2,3},{3,2},{4,5},{5,4},{6,7},{7,6},{8,9},{9,8},{10,11... | collective-permute-start | bytes 1720328 | tf_op jit(solution)/shard_map/ppermute | solution.py:123
  110.0 2.0 copy-start
  112.0 2.0 copy-start.1
  125.6 44.0 %copy-start.17 = (bf16[128,2688]{1,0:T(8,128)(2,1)S(1)}, bf16[128,2688]{1,0:T(8,128)(2,1)}, u32[]{:S(2)}) copy-start(bf16[128,2688]{1,0:T(8,128)(2,1)} %copy-done.15) | copy-start | bytes 2064388
  125.6 44.0 %copy-start.19 = (bf16[64,2688]{1,0:T(8,128)(2,1)S(1)}, bf16[64,2688]{1,0:T(8,128)(2,1)}, u32[]{:S(2)}) copy-start(bf16[64,2688]{1,0:T(8,128)(2,1)} %copy-done.18) | copy-start | bytes 1032196
  125.6 44.0 %copy-start.22 = (bf16[64,2688]{1,0:T(8,128)(2,1)S(1)}, bf16[64,2688]{1,0:T(8,128)(2,1)}, u32[]{:S(2)}) copy-start(bf16[64,2688]{1,0:T(8,128)(2,1)} %copy-done.20) | copy-start | bytes 1032196
  125.7 44.0 %copy-start.25 = (bf16[64,2688]{1,0:T(8,128)(2,1)S(1)}, bf16[64,2688]{1,0:T(8,128)(2,1)}, u32[]{:S(2)}) copy-start(bf16[64,2688]{1,0:T(8,128)(2,1)} %copy-done.23) | copy-start | bytes 1032196
  125.7 44.0 %copy-start.28 = (bf16[64,2688]{1,0:T(8,128)(2,1)S(1)}, bf16[64,2688]{1,0:T(8,128)(2,1)}, u32[]{:S(2)}) copy-start(bf16[64,2688]{1,0:T(8,128)(2,1)} %copy-done.26) | copy-start | bytes 1032196
  133.6 36.0 %copy-start.11 = (bf16[128,2688]{1,0:T(8,128)(2,1)S(1)}, bf16[128,2688]{1,0:T(8,128)(2,1)}, u32[]{:S(2)}) copy-start(bf16[128,2688]{1,0:T(8,128)(2,1)} %copy-done.10) | copy-start | bytes 2064388
  133.6 36.0 %copy-start.14 = (bf16[128,2688]{1,0:T(8,128)(2,1)S(1)}, bf16[128,2688]{1,0:T(8,128)(2,1)}, u32[]{:S(2)}) copy-start(bf16[128,2688]{1,0:T(8,128)(2,1)} %copy-done.12) | copy-start | bytes 2064388
  133.6 19.3 %collective-permute-start.19 = (bf16[512,768]{1,0:T(8,128)(2,1)S(1)}, bf16[512,768]{1,0:T(8,128)(2,1)}, u32[]{:S(2)}, u32[]{:S(2)}) collective-permute-start(bf16[512,768]{1,0:T(8,128)(2,1)S(1)} %acts.3.refs_20_.refs_0_), channel_id=1, source_target_pairs={{0,6},{2,0},{4,2},{6,4},{1,7},{3,1},{5,3},{7,5},{8,14},{10,8},{12,... | collective-permute-start | bytes 2359304 | tf_op jit(solution)/shard_map/ppermute | solution.py:115
  133.7 21.8 %collective-permute-start.18 = (bf16[512,768]{1,0:T(8,128)(2,1)S(1)}, bf16[512,768]{1,0:T(8,128)(2,1)}, u32[]{:S(2)}, u32[]{:S(2)}) collective-permute-start(bf16[512,768]{1,0:T(8,128)(2,1)S(1)} %acts.3.refs_20_.refs_0_), channel_id=1, source_target_pairs={{0,2},{2,4},{4,6},{6,0},{1,3},{3,5},{5,7},{7,1},{8,10},{10,12},{12... | collective-permute-start | bytes 2359304 | tf_op jit(solution)/shard_map/ppermute | solution.py:114
  154.0 10.0 %collective-permute-start.21 = (bf16[256,768]{1,0:T(8,128)(2,1)S(1)}, bf16[256,768]{1,0:T(8,128)(2,1)S(1)}, u32[]{:S(2)}, u32[]{:S(2)}) collective-permute-start(bf16[256,768]{1,0:T(8,128)(2,1)S(1)} %slice.29), channel_id=1, source_target_pairs={{0,6},{2,0},{4,2},{6,4},{1,7},{3,1},{5,3},{7,5},{8,14},{10,8},{12,... | collective-permute-start | bytes 1179656 | tf_op jit(solution)/shard_map/ppermute | solution.py:117
  156.5 11.3 %collective-permute-start.20 = (bf16[256,768]{1,0:T(8,128)(2,1)S(1)}, bf16[256,768]{1,0:T(8,128)(2,1)}, u32[]{:S(2)}, u32[]{:S(2)}) collective-permute-start(bf16[256,768]{1,0:T(8,128)(2,1)S(1)} %slice.28), channel_id=1, source_target_pairs={{0,2},{2,4},{4,6},{6,0},{1,3},{3,5},{5,7},{7,1},{8,10},{10,12},{12... | collective-permute-start | bytes 1179656 | tf_op jit(solution)/shard_map/ppermute | solution.py:116
  156.8 37.5 %collective-permute-start.22 = (bf16[512,768]{1,0:T(8,128)(2,1)S(1)}, bf16[512,768]{1,0:T(8,128)(2,1)}, u32[]{:S(2)}, u32[]{:S(2)}) collective-permute-start(bf16[512,768]{1,0:T(8,128)(2,1)S(1)} %acts.3.refs_20_.refs_0_), channel_id=1, source_target_pairs={{0,1},{1,0},{2,3},{3,2},{4,5},{5,4},{6,7},{7,6},{8,9},{9,8},{10,11... | collective-permute-start | bytes 2359304 | tf_op jit(solution)/shard_map/ppermute | solution.py:123
  158.2 36.2 %collective-permute-start.24 = (bf16[512,768]{1,0:T(8,128)(2,1)}, bf16[512,768]{1,0:T(8,128)(2,1)}, u32[]{:S(2)}, u32[]{:S(2)}) collective-permute-start(bf16[512,768]{1,0:T(8,128)(2,1)} %collective-permute-done.19.refs_2_), channel_id=1, source_target_pairs={{0,1},{1,0},{2,3},{3,2},{4,5},{5,4},{6,7},{7,6},{8,9},{9,8},{10,11... | collective-permute-start | bytes 2359304 | tf_op jit(solution)/shard_map/ppermute | solution.py:123
  158.2 36.2 %collective-permute-start.23 = (bf16[512,768]{1,0:T(8,128)(2,1)}, bf16[512,768]{1,0:T(8,128)(2,1)}, u32[]{:S(2)}, u32[]{:S(2)}) collective-permute-start(bf16[512,768]{1,0:T(8,128)(2,1)} %collective-permute-done.18.refs_1_), channel_id=1, source_target_pairs={{0,1},{1,0},{2,3},{3,2},{4,5},{5,4},{6,7},{7,6},{8,9},{9,8},{10,11... | collective-permute-start | bytes 2359304 | tf_op jit(solution)/shard_map/ppermute | solution.py:123
  164.0 30.3 %collective-permute-start.26 = (bf16[256,768]{1,0:T(8,128)(2,1)S(1)}, bf16[256,768]{1,0:T(8,128)(2,1)}, u32[]{:S(2)}, u32[]{:S(2)}) collective-permute-start(bf16[256,768]{1,0:T(8,128)(2,1)S(1)} %collective-permute-done.21.refs_4_), channel_id=1, source_target_pairs={{0,1},{1,0},{2,3},{3,2},{4,5},{5,4},{6,7},{7,6},{8,9},{9,8},{10,11... | collective-permute-start | bytes 1179656 | tf_op jit(solution)/shard_map/ppermute | solution.py:123
  167.8 26.5 %collective-permute-start.25 = (bf16[256,768]{1,0:T(8,128)(2,1)}, bf16[256,768]{1,0:T(8,128)(2,1)}, u32[]{:S(2)}, u32[]{:S(2)}) collective-permute-start(bf16[256,768]{1,0:T(8,128)(2,1)} %collective-permute-done.20.refs_3_), channel_id=1, source_target_pairs={{0,1},{1,0},{2,3},{3,2},{4,5},{5,4},{6,7},{7,6},{8,9},{9,8},{10,11... | collective-permute-start | bytes 1179656 | tf_op jit(solution)/shard_map/ppermute | solution.py:123
  194.4 1.2 copy-start.7
  (14 other events, 12.7 us)

commit v2 on v0

v2 whole, which is shorter than its diff:
```python
import functools

import jax
import jax.numpy as jnp
from jax import lax
from jax.experimental import pallas as pl
from jax.experimental.pallas import tpu as pltpu
from jax.sharding import Mesh
from jax.sharding import PartitionSpec as P

CAP = 4
ROW_BITS = 3
EPSILON = 1e-06
TILE = 896
AHEAD = 3
EARLY = 2
F32 = jnp.float32
BF16 = jnp.bfloat16
ANY = pl.BlockSpec(memory_space=pl.ANY)
HBM = pl.BlockSpec(memory_space=pltpu.HBM)
VMEM = pl.BlockSpec(memory_space=pltpu.VMEM)


def params(mib):
    return pltpu.CompilerParams(vmem_limit_bytes=mib * 1024 * 1024)


NEAR_Z = (0, 3, 1)


def in_hbm(*arrays):
    return [pltpu.with_memory_space_constraint(t, pltpu.HBM) for t in arrays]


def in_vmem(*shapes):
    return tuple(pltpu.VMEM(shape, dtype) for shape, dtype in shapes)


def iota(shape, dim):
    return lax.broadcasted_iota(jnp.int32, shape, dim)


def dispatch_kernel(first, tiles, ids_ref, comb_ref, rank_ref, tok, grad, out_ref, both, sems):
    rows = out_ref.shape[0]
    toks = tok.shape[0]
    for j in range(tiles):
        span = pl.ds((first + j) * TILE, TILE)
        pltpu.make_async_copy(tok.at[:, span], both.at[j, pl.ds(0, toks), :], sems.at[j]).start()
        pltpu.make_async_copy(grad.at[:, span], both.at[j, pl.ds(toks, toks), :], sems.at[j]).start()
    routed = rank_ref.shape[0]
    ranks = rank_ref[...].reshape(1, routed)
    expert_row = iota((rows, routed), 0) >> ROW_BITS
    ident = jnp.sum(
        jnp.where(ranks == expert_row, iota((rows, routed), 1), 0), axis=1, keepdims=True
    )
    hit = jnp.zeros((rows, toks), F32)
    comb = jnp.zeros((rows, toks), F32)
    for k in range(ids_ref.shape[0]):
        same = ids_ref[k : k + 1, :] == ident
        hit = jnp.where(same, 1.0, hit)
        comb = jnp.where(same, comb_ref[k : k + 1, :], comb)
    earlier = (iota((toks, toks), 0) < iota((toks, toks), 1)).astype(BF16)
    slot = jnp.dot(hit.astype(BF16), earlier, preferred_element_type=F32)
    row = iota((rows, toks), 0)
    want = (row & (CAP - 1)).astype(F32)
    is_grad = (row & CAP) != 0
    sel = jnp.where(slot == want, hit, 0.0)
    select = jnp.concatenate(
        [jnp.where(is_grad, 0.0, sel), jnp.where(is_grad, sel, 0.0)], axis=1
    ).astype(BF16)
    weight = jnp.sum(sel * comb, axis=1, keepdims=True)
    scale = jnp.where(is_grad[:, :1], weight, 1.0)
    for j in range(tiles):
        pltpu.make_async_copy(both.at[j], both.at[j], sems.at[j]).wait()
        picked = jnp.dot(select, both[j], preferred_element_type=F32)
        out_ref[:, j * TILE : (j + 1) * TILE] = (picked * scale).astype(BF16)


def dispatch(ids, comb, ranks, tokens, out_grad, first, tiles, rows):
    toks = tokens.shape[0]
    return pl.pallas_call(
        functools.partial(dispatch_kernel, first, tiles),
        in_specs=[VMEM, VMEM, VMEM, HBM, HBM],
        out_specs=VMEM,
        out_shape=jax.ShapeDtypeStruct((rows, tiles * TILE), BF16),
        scratch_shapes=[
            pltpu.VMEM((tiles, 2 * toks, TILE), BF16),
            pltpu.SemaphoreType.DMA((tiles,)),
        ],
        compiler_params=params(20),
        cost_estimate=pl.CostEstimate(
            flops=tiles * 8 * toks * rows * TILE, bytes_accessed=tiles * 6 * toks * TILE, transcendentals=0
        ),
        name="dispatch",
    )(ids, comb, ranks, *in_hbm(tokens, out_grad))


def split_kernel(order, in_ref, out_ref):
    source_count, width = in_ref.shape[0], in_ref.shape[2]
    rows = source_count * 2 * CAP
    half = rows // 2
    r, c = iota((rows, rows), 0), iota((rows, rows), 1)
    group = r & (half - 1)
    source = (group & -CAP) * 2 + jnp.where(r >= half, CAP, 0) + (group & (CAP - 1))
    perm = (c == source).astype(BF16)
    for i, place in enumerate(order):
        block = in_ref[:, i * 2 * CAP : (i + 1) * 2 * CAP, :].reshape(rows, width)
        out_ref[place * rows : (place + 1) * rows, :] = jnp.dot(
            perm, block, preferred_element_type=F32
        ).astype(BF16)


def split_rows(block, order):
    rows = block.shape[0] * block.shape[1]
    return pl.pallas_call(
        functools.partial(split_kernel, order),
        in_specs=[VMEM],
        out_specs=VMEM,
        out_shape=jax.ShapeDtypeStruct((rows, block.shape[2]), BF16),
        compiler_params=params(16),
        name="split_rows",
    )(block)


def shift(n, k):
    return [(i, (i + k) % n) for i in range(n)]


def along(x, k):
    return lax.ppermute(x, "z", shift(4, k))


def swap(x):
    return lax.ppermute(x, "core", shift(2, 1))


def after(x, dep):
    return lax.optimization_barrier((x, dep))[0]


def near_z(block):
    return [block, along(block, 1), along(block, 3)]


def far_z(up, down, half):
    return [along(up[:half], 1), along(down[half:], 3)]


def with_other(mine):
    return list(mine) + [swap(t) for t in mine]


def position(dc, dz):
    z = lax.rem(lax.axis_index("z") + dz, 4)
    return z * 2 + lax.rem(lax.axis_index("core") + dc, 2)


class Rows:
    def __init__(self, first, arrays, kind, groups):
        self.first, self.arrays, self.kind, self.groups = first, arrays, kind, groups
        self.width = arrays[0].shape[1]

    def sources(self, refs, a, n):
        refs = refs[a * len(refs) // 2 : (a + 1) * len(refs) // 2]
        out = []
        for group in self.groups:
            if self.kind == "whole":
                out.append((group, refs[0], 2 * n * group, refs[0], 2 * n * group + n))
            elif group < 3:
                ref = refs[(1, 0, 2)[group]]
                out.append((group, ref, 0, ref, n))
            else:
                out.append((group, refs[-2], 0, refs[-1], 0))
        return out

    def start(self, refs, x_s, g_s, column, width, x_sem, g_sem):
        span = pl.ds(column, width)
        n = x_s.shape[0] // (2 * len(self.groups))
        core = lax.axis_index("core")
        for a in range(2):
            here = core if a == 0 else 1 - core
            for group, x, x_row, g, g_row in self.sources(refs, a, n):
                at = pl.multiple_of((group - self.groups[0]) * 2 * n + here * n, n)
                at = pl.ds(at, n)
                pltpu.make_async_copy(x.at[pl.ds(x_row, n), span], x_s.at[at, :], x_sem).start()
                pltpu.make_async_copy(g.at[pl.ds(g_row, n), span], g_s.at[at, :], g_sem).start()


def acts_kernel(rows_of, skip, last, keep, given, *refs):
    blocks, refs = refs[: len(rows_of.arrays)], refs[len(rows_of.arrays) :]
    weights, refs = refs[:3], refs[3:]
    if skip is not None:
        before, refs = refs[0], refs[1:]
    out_ref, x_s, g_s = refs[:3]
    refs = refs[3:]
    if given:
        held = weights
    else:
        held, refs = refs[:3], refs[3:]
    sems, acc_sem = refs[:2]
    acc = refs[2] if last else out_ref
    rows = acc.shape[1]
    count = rows_of.width // TILE
    if skip is not None:
        pltpu.make_async_copy(before.at[:, pl.ds(skip, rows), :], acc, acc_sem).start()

    def views(j):
        span = pl.ds(j * TILE, TILE)
        return (
            x_s.at[:, span], g_s.at[:, span], held[0].at[span, :], held[1].at[span, :], held[2].at[:, span]
        )

    def start(j):
        x, g, wg, wu, wd = views(j)
        span = pl.ds(rows_of.first + j * TILE, TILE)
        if not given:
            pltpu.make_async_copy(weights[0].at[span, :], wg, sems.at[2, j]).start()
            pltpu.make_async_copy(weights[1].at[span, :], wu, sems.at[3, j]).start()
        rows_of.start(blocks, x, g, j * TILE, TILE, sems.at[0, j], sems.at[1, j])
        if not given:
            pltpu.make_async_copy(weights[2].at[:, span], wd, sems.at[4, j]).start()

    for j in range(min(AHEAD, count)):
        start(j)
    if skip is not None:
        pltpu.make_async_copy(acc, acc, acc_sem).wait()
    for j in range(count):
        x, g, wg, wu, wd = views(j)
        for k, ref in enumerate((x, g) if given else (x, g, wg, wu, wd)):
            pltpu.make_async_copy(ref, ref, sems.at[k, j]).wait()
        if j + AHEAD < count:
            start(j + AHEAD)
        new = (
            jnp.dot(x[...], wg[...], preferred_element_type=F32),
            jnp.dot(x[...], wu[...], preferred_element_type=F32),
            lax.dot_general(
                g[...], wd[...], (((1,), (1,)), ((), ())), preferred_element_type=F32
            ),
        )
        for k in range(3):
            if j == 0 and skip is None:
                acc[k] = new[k]
            else:
                acc[k] += new[k]

    if last:
        m = acc.shape[2]
        step = 64

        @pl.loop(0, rows // step)
        def _(i):
            at = pl.ds(pl.multiple_of(i * step, step), step)
            gate, up, act = acc[0, at, :], acc[1, at, :], acc[2, at, :]
            sig = jax.nn.sigmoid(gate)
            out_ref[at, 0:m] = (act * up * sig * (1.0 + gate * (1.0 - sig))).astype(BF16)
            out_ref[at, m : 2 * m] = (act * gate * sig).astype(BF16)
            out_ref[at, 2 * m : 3 * m] = (gate * sig * up).astype(BF16)


def acts(rows_of, n, weights, last, mib, before=None, skip=None, keep=False, given=False):
    m = weights[2].shape[0]
    rows = 2 * n * len(rows_of.groups)
    width = rows_of.width
    out = ((rows, 3 * m), BF16) if last else ((3, rows, m), F32)
    outs = [out, ((rows, width), BF16), ((rows, width), BF16)]
    held = [((width, m), BF16), ((width, m), BF16), ((m, width), BF16)]
    scratch = []
    if keep:
        outs += held
    elif not given:
        scratch += [pltpu.VMEM(*shape) for shape in held]
    scratch += [pltpu.SemaphoreType.DMA((5, width // TILE)), pltpu.SemaphoreType.DMA(())]
    if last:
        scratch.append(pltpu.VMEM((3, rows, m), F32))
    extra = [] if before is None else [before]
    return pl.pallas_call(
        functools.partial(acts_kernel, rows_of, skip, last, keep, given),
        in_specs=[HBM] * len(rows_of.arrays) + [VMEM if given else HBM] * 3 + [VMEM] * len(extra),
        out_specs=(VMEM,) * len(outs),
        out_shape=in_vmem(*outs),
        scratch_shapes=scratch,
        compiler_params=params(mib),
        cost_estimate=pl.CostEstimate(
            flops=6 * rows * width * m,
            bytes_accessed=4 * rows * width + 6 * m * width,
            transcendentals=0,
        ),
        name="acts",
    )(*in_hbm(*rows_of.arrays), *(weights if given else in_hbm(*weights)), *extra)


def squares_kernel(x0, g0, xa, ga, xb, gb, hid_a, hid_b, last_ref, xt_ref, gt_ref, hid_t, parts):
    m = hid_a.shape[1] // 3
    rows_a = hid_a.shape[0]
    hid_t[:, :rows_a] = hid_a[...].T
    hid_t[:, rows_a:] = hid_b[...].T
    parts[...] = jnp.zeros_like(parts)
    mine = position(0, 0)

    def tile(j, x, g):
        @pl.when(j == mine)
        def _():
            xt_ref[...] = x.T
            gt_ref[...] = g.T

        both = jnp.dot(hid_t[: 2 * m, :], x, preferred_element_type=F32)
        down = jnp.dot(hid_t[2 * m :, :], g, preferred_element_type=F32)
        for i, grads in enumerate((both[:m], both[m:], down)):
            parts[i] += jnp.sum((grads * grads).reshape(m // 8, 8, TILE), axis=0)

    early = x0.shape[1] // TILE

    @pl.loop(0, early)
    def _(j):
        span = pl.ds(pl.multiple_of(j * TILE, TILE), TILE)
        tile(j, x0[:, span], g0[:, span])

    @pl.loop(0, xa.shape[1] // TILE)
    def _(j):
        span = pl.ds(pl.multiple_of(j * TILE, TILE), TILE)
        x = jnp.concatenate([xa[:, span], xb[:, span]], axis=0)
        g = jnp.concatenate([ga[:, span], gb[:, span]], axis=0)
        tile(j + early, x, g)

    rows_b = hid_b.shape[0]
    last_ref[:rows_b, :] = hid_b[...]
    row = iota((16, last_ref.shape[1]), 0)
    coded = jnp.zeros(row.shape, F32)
    for i in range(3):
        rest = jnp.broadcast_to(jnp.sum(parts[i], keepdims=True), row.shape)
        for k in range(3):
            piece = rest.astype(BF16).astype(F32)
            coded = jnp.where(row == 3 * i + k, piece, coded)
            rest = rest - piece
    last_ref[rows_b:, :] = coded.astype(BF16)


def squares(rows_of_x, hid_a, hid_b):
    rows = hid_a.shape[0] + hid_b.shape[0]
    cols = hid_a.shape[1]
    width = rows_of_x[0].shape[1] + rows_of_x[2].shape[1]
    return pl.pallas_call(
        squares_kernel,
        in_specs=[VMEM] * 8,
        out_specs=(VMEM,) * 3,
        out_shape=in_vmem(
            ((hid_b.shape[0] + 16, cols), BF16), ((TILE, rows), BF16), ((TILE, rows), BF16)
        ),
        scratch_shapes=[pltpu.VMEM((cols, rows), BF16), pltpu.VMEM((3, 8, TILE), F32)],
        compiler_params=params(20),
        cost_estimate=pl.CostEstimate(
            flops=2 * rows * width * cols, bytes_accessed=4 * rows * width, transcendentals=0
        ),
        name="squares",
    )(*rows_of_x, hid_a, hid_b)


def final_kernel(entries, copies, sums, *refs):
    arrays, refs = refs[: -8], refs[-8:]
    xt_ref, gt_ref, out_ref, hid, coded, stage, in_sems, out_sems = refs
    for k, (i, row) in enumerate(sums):
        pltpu.make_async_copy(
            arrays[i].at[pl.ds(row, 16), pl.ds(0, 128)], coded.at[k], in_sems.at[8]
        ).start()

    def start(source):
        for owner, i, row, at, n in copies:
            if owner == source:
                pltpu.make_async_copy(
                    arrays[i].at[pl.ds(row, n), :],
                    hid.at[source, pl.ds(at, n), :],
                    in_sems.at[source],
                ).start()

    start(0)
    start(1)
    m = hid.shape[2] // 3
    pltpu.make_async_copy(coded, coded, in_sems.at[8]).wait()
    pieces = jnp.sum(coded[...].astype(F32), axis=0)
    factors = []
    for i in range(3):
        total = jnp.sum(pieces[3 * i : 3 * i + 3, :], axis=0, keepdims=True)
        factors.append(lax.rsqrt(total[:, 0:1] / entries + EPSILON))

    def store(slot, i):
        dz = jnp.where(i % 4 == 1, 3, jnp.where(i % 4 == 2, 1, jnp.where(i % 4 == 3, 2, 0)))
        at = pl.ds(pl.multiple_of(position(i // 4, dz) * m, m), m)
        return pltpu.make_async_copy(stage.at[slot], out_ref.at[:, :, at], out_sems.at[slot])

    @pl.loop(0, 8)
    def _(i):
        slot = i % 2
        pltpu.make_async_copy(hid.at[i], hid.at[i], in_sems.at[i]).wait()

        @pl.when(i == 0)
        def _():
            for source in range(2, 8):
                start(source)

        @pl.when(i >= 2)
        def _():
            store(slot, i - 2).wait()

        for k in range(3):
            lhs = gt_ref if k == 2 else xt_ref
            grads = jnp.dot(
                lhs[...], hid[i, :, k * m : (k + 1) * m], preferred_element_type=F32
            )
            stage[slot, k] = (grads * factors[k]).astype(BF16)
        store(slot, i).start()

    store(0, 6).wait()
    store(1, 7).wait()


def final(copies, sums, arrays, xt, gt, entries):
    rows = xt.shape[1]
    width = arrays[0].shape[1]
    m = width // 3
    return pl.pallas_call(
        functools.partial(final_kernel, entries, copies, sums),
        in_specs=[ANY] * len(arrays) + [VMEM] * 2,
        out_specs=HBM,
        out_shape=jax.ShapeDtypeStruct((3, TILE, 8 * m), BF16),
        scratch_shapes=[
            pltpu.VMEM((8, rows, width), BF16),
            pltpu.VMEM((8, 16, 128), BF16),
            pltpu.VMEM((2, 3, TILE, m), BF16),
            pltpu.SemaphoreType.DMA((9,)),
            pltpu.SemaphoreType.DMA((2,)),
        ],
        compiler_params=params(16),
        cost_estimate=pl.CostEstimate(
            flops=2 * rows * TILE * width * 8,
            bytes_accessed=4 * TILE * width * 8,
            transcendentals=0,
        ),
        name="final",
    )(*arrays, xt, gt)


def placed(source, array, row, group, offset, count, z, size):
    out = []
    while count:
        step = min(count, size - offset)
        out.append((source, array, row, ((group + z) % 4) * size + offset, step))
        row, count, group, offset = row + step, count - step, group + 1, 0
    merged = [out[0]]
    for item in out[1:]:
        s, a, r, at, c = merged[-1]
        if at + c == item[3]:
            merged[-1] = (s, a, r, at, c + item[4])
        else:
            merged.append(item)
    return merged


def cut(width, step):
    return tuple((at, min(step, width - at)) for at in range(0, width, step))


def body(tokens, out_grad, combine, expert_ids, expert_rank, gate_weight, up_weight, down_weight):
    width = tokens.shape[1]
    expert = ("y", "x")
    hot = lax.axis_size(expert)
    rows = hot * 2 * CAP
    n = rows // 2
    weights = (gate_weight[0], up_weight[0], down_weight[0])
    ids, comb = expert_ids.T, combine.T
    tiles = width // TILE
    sent = dispatch(ids, comb, expert_rank, tokens, out_grad, 0, EARLY, rows)
    ranks = after(expert_rank, sent)
    sent_rest = dispatch(ids, comb, ranks, tokens, out_grad, EARLY, tiles - EARLY, rows)
    early = EARLY * TILE

    near = near_z(sent)
    got = lax.all_to_all(
        sent_rest.reshape(hot, 2 * CAP, width - early), expert, split_axis=0, concat_axis=0, tiled=True
    )
    block = split_rows(got, (0,))
    far = far_z(near[1], near[2], n)
    block = after(block, far)
    four = [t.reshape(hot, 2 * CAP, early) for t in near + [jnp.concatenate(far)]]
    got = lax.all_to_all(
        jnp.concatenate(four, axis=1), expert, split_axis=0, concat_axis=0, tiled=True
    )
    whole = with_other([split_rows(got, (1, 0, 2, 3))])

    near = near_z(block)
    far = far_z(near[1], near[2], n)
    part, *x0 = acts(Rows(0, whole, "whole", (0, 1, 2, 3)), n, weights, False, 20)
    near = with_other(near)
    hid_a, xa, ga, *held = acts(
        Rows(early, near, "parts", (0, 1, 2)), n, weights, True, 20, part, 0, keep=True
    )
    far = with_other(after(tuple(far), hid_a))
    hid_b, xb, gb = acts(
        Rows(early, far, "parts", (3,)), n, held, True, 16, part, 6 * n, given=True
    )

    near_a = near_z(hid_a)
    hid_b, xt, gt = squares((*x0, xa, ga, xb, gb), hid_a, hid_b)
    half = hid_a.shape[0] // 2
    up_a, down_a = after((near_a[1], near_a[2]), hid_b)
    last = [
        hid_b,
        along(jnp.concatenate([up_a[:half], hid_b]), 1),
        along(jnp.concatenate([down_a[half:], hid_b]), 3),
        along(hid_b, 2),
    ]
    near_a = with_other(near_a)
    last = with_other(last)

    size = 2 * n
    copies, sums = [], []
    for a in range(2):
        for k, z in enumerate(NEAR_Z):
            copies += placed(4 * a + k, 3 * a + k, 0, 0, 0, 3 * size, z, size)
        mine, up, down, other = range(6 + 4 * a, 10 + 4 * a)
        copies += placed(4 * a, mine, 0, 3, 0, size, 0, size)
        copies += placed(4 * a + 1, up, half, 3, 0, size, 3, size)
        copies += placed(4 * a + 2, down, half, 3, 0, size, 1, size)
        copies += placed(4 * a + 3, up, 0, 0, 0, half, 2, size)
        copies += placed(4 * a + 3, down, 0, half // size, half % size, half, 2, size)
        copies += placed(4 * a + 3, other, 0, 3, 0, size, 2, size)
        sums += [(mine, size), (up, half + size), (down, half + size), (other, size)]
    entries = width * weights[0].shape[1] * 8
    return final(copies, sums, near_a + last, xt, gt, entries)[None]


def solution(mesh):
    fine = Mesh(mesh.devices.reshape(4, 4, 4, 2), ("y", "x", "z", "core"))
    expert, cuts = ("y", "x"), ("z", "core")
    tokens = P(expert + cuts, None)
    return jax.shard_map(
        body,
        mesh=fine,
        in_specs=(
            tokens,
            tokens,
            tokens,
            tokens,
            P(),
            P(expert, None, cuts),
            P(expert, None, cuts),
            P(expert, cuts, None),
        ),
        out_specs=P(expert, None, cuts, None),
        check_vma=False,
    )
```

time: 489 us -> 155 us (0.32)
  blocking collectives: 180 us -> 0 us
  waiting for transfers between devices: 154 us -> 50.7 us
  local copies, waits for them, and re-layouts: 85.6 us -> 6.34 us
  Pallas kernels: 0 us -> 46.9 us
  starting transfers between devices: 19.2 us -> 48.7 us
  matrix products: 25.7 us -> 0 us
  other arithmetic: 22.7 us -> 1.53 us
    all_to_all x1 -> x0, blocking collectives: 168 us -> none  [body(): lax.all_to_all(normalized, 'cuts', split_axis=1, concat_axis=2, tiled=True)]
    all_to_all x2, waiting for transfers between devices: 154 us -> 18.1 us  [the longest x1 18.1 us: body(): lax.all_to_all(jnp.concatenate(four, axis=1), expert, split_axis=0, conca...]
    pallas_call x0 -> x9, Pallas kernels: none -> 46.9 us  [the longest x3 16.3 us: acts(): pl.pallas_call(functools.partial(acts_kernel, rows_of, skip, last, keep,...]
    ppermute x0 -> x26, starting transfers between devices: none -> 35.1 us  [the longest x13 18.8 us: along(): return lax.ppermute(x, 'z', shift(4, k))]
    ppermute x0 -> x26, waiting for transfers between devices: none -> 32.5 us  [the longest x13 30.3 us: along(): return lax.ppermute(x, 'z', shift(4, k))]
    broadcast_in_dim x3 -> x0, local copies, waits for them, and re-layouts: 27.9 us -> none  [the longest x1 17.4 us: body(): return owned[None]]
    dot_general x10 -> x0, matrix products: 25.7 us -> none  [the longest x1 6.37 us: expert_acts(): lax.dot_general(g_rows, w_down, (((1,), (1,)), ((), ())), preferred_eleme...]
    reshape x4 -> x0, local copies, waits for them, and re-layouts: 24.9 us -> none  [the longest x1 12.1 us: body(): x_all = got_tok.reshape(-1, width)]
  transfers between devices with their start and end apart: 2 -> 28, of which waited for: 2 -> 9; matrix products, arithmetic and copies ran while one was open for 5% -> 2% of each run, Pallas kernels for 0% -> 18%
where the time goes in v2:
time: 155 us
  waiting for transfers between devices  50.7 us (33%)
  starting transfers between devices  48.7 us (31%)
  Pallas kernels  46.9 us (30%)
  local copies, waits for them, and re-layouts  6.34 us (4%)
    ppermute x13, waiting for transfers between devices, along(): return lax.ppermute(x, 'z', shift(4, k))  30.3 us
    ppermute x13, starting transfers between devices, along(): return lax.ppermute(x, 'z', shift(4, k))  18.8 us
    all_to_all x1, waiting for transfers between devices, body(): lax.all_to_all(jnp.concatenate(four, axis=1), expert, split_axis=0, conca...  18.1 us
    pallas_call x3, Pallas kernels, acts(): pl.pallas_call(functools.partial(acts_kernel, rows_of, skip, last, keep,...  16.3 us
    ppermute x13, starting transfers between devices, swap(): return lax.ppermute(x, 'core', shift(2, 1))  16.3 us
    pallas_call x1, Pallas kernels, final(): pl.pallas_call(functools.partial(final_kernel, entries, copies, sums), in...  13.1 us
    pallas_call x1, Pallas kernels, squares(): pl.pallas_call(squares_kernel, in_specs=[VMEM] * 8, out_specs=(VMEM,) * 3...  9.82 us
    all_to_all x1, starting transfers between devices, body(): lax.all_to_all(sent_rest.reshape(hot, 2 * CAP, width - early), expert, sp...  7.6 us
  transfers between devices with their start and end apart: 28, of which 9 were waited for; matrix products, arithmetic and copies ran while one was open for 2% of the time, Pallas kernels for 18%

profile of v2, /device:TPU:1, one launch (start us, length us, event | category | flops | bytes accessed | tf_op | source)
XLA Modules:
  0.0 154.6 jit_solution(14560536931707980100)
XLA Ops:
  0.0 0.7 copy-done.1
  0.7 0.7 copy-done.2
  1.4 0.7 copy-done.3
  2.1 1.7 %dispatch.2 = bf16[128,1792]{1,0:T(8,128)(2,1)S(1)} custom-call(s32[8,128]{1,0:T(8,128)S(1)} %bitcast.13, f32[8,128]{1,0:T(8,128)S(1)} %bitcast.15, s32[384]{0:T(512)S(1)} %copy-done.3, bf16[128,7168]{1,0:T(8,128)(2,1)} %tok.3, bf16[128,7168]{1,0:T(8,128)(2,1)} %grad.3), custom_call_target="tpu_custom_call" | custom-call | flops 234881024 | bytes 1376256 | tf_op jit(solution)/shard_map/dispatch/pallas_call | solution.py:81
  3.7 3.7 %dispatch.3 = bf16[128,5376]{1,0:T(8,128)(2,1)} custom-call(s32[8,128]{1,0:T(8,128)S(1)} %bitcast.14, f32[8,128]{1,0:T(8,128)S(1)} %bitcast.16, s32[384]{0:T(512)S(1)} %copy-done.3, bf16[128,7168]{1,0:T(8,128)(2,1)} %tok.3, bf16[128,7168]{1,0:T(8,128)(2,1)} %grad.3), custom_call_target="tpu_custom_call" | custom-call | flops 704643072 | bytes 4128768 | tf_op jit(solution)/shard_map/dispatch/pallas_call | solution.py:81
  7.4 7.6 %all-to-all-start = ((bf16[16,8,5376]{2,1,0:T(8,128)(2,1)}), bf16[16,8,5376]{2,1,0:T(8,128)(2,1)S(1)}, u32[]{:S(2)}, u32[]{:S(2)}) async-start(bf16[16,8,5376]{2,1,0:T(8,128)(2,1)} %bitcast.2), calls=%async_computation | async-start | bytes 2752512 | tf_op jit(solution)/shard_map/all_to_all | solution.py:477
  15.0 1.7 %collective-permute-start = (bf16[128,1792]{1,0:T(8,128)(2,1)S(1)}, bf16[128,1792]{1,0:T(8,128)(2,1)S(1)}, u32[]{:S(2)}, u32[]{:S(2)}) collective-permute-start(bf16[128,1792]{1,0:T(8,128)(2,1)S(1)} %dispatch.2), channel_id=1, source_target_pairs={{0,2},{2,4},{4,6},{6,0},{1,3},{3,5},{5,7},{7,1},{8,10},{10,12},{12... | collective-permute-start | bytes 1376264 | tf_op jit(solution)/shard_map/ppermute | solution.py:130
  16.7 2.2 %collective-permute-start.2 = (bf16[128,1792]{1,0:T(8,128)(2,1)S(1)}, bf16[128,1792]{1,0:T(8,128)(2,1)S(1)}, u32[]{:S(2)}, u32[]{:S(2)}) collective-permute-start(bf16[128,1792]{1,0:T(8,128)(2,1)S(1)} %dispatch.2), channel_id=1, source_target_pairs={{0,6},{2,0},{4,2},{6,4},{1,7},{3,1},{5,3},{7,5},{8,14},{10,8},{12,... | collective-permute-start | bytes 1376264 | tf_op jit(solution)/shard_map/ppermute | solution.py:130
  18.9 9.8 %collective-permute-done = bf16[128,1792]{1,0:T(8,128)(2,1)S(1)} collective-permute-done((bf16[128,1792]{1,0:T(8,128)(2,1)S(1)}, bf16[128,1792]{1,0:T(8,128)(2,1)S(1)}, u32[]{:S(2)}, u32[]{:S(2)}) %collective-permute-start) | collective-permute-done | bytes 458784 | tf_op jit(solution)/shard_map/ppermute | solution.py:130
  28.9 2.7 %collective-permute-start.3 = (bf16[64,1792]{1,0:T(8,128)(2,1)S(1)}, bf16[64,1792]{1,0:T(8,128)(2,1)S(1)}, u32[]{:S(2)}, u32[]{:S(2)}) collective-permute-start(bf16[64,1792]{1,0:T(8,128)(2,1)S(1)} %slice.25), channel_id=1, source_target_pairs={{0,6},{2,0},{4,2},{6,4},{1,7},{3,1},{5,3},{7,5},{8,14},{10,8},{12,... | collective-permute-start | bytes 688136 | tf_op jit(solution)/shard_map/ppermute | solution.py:130
  31.6 4.0 %collective-permute-done.1 = bf16[64,1792]{1,0:T(8,128)(2,1)S(1)} collective-permute-done((bf16[64,1792]{1,0:T(8,128)(2,1)S(1)}, bf16[64,1792]{1,0:T(8,128)(2,1)S(1)}, u32[]{:S(2)}, u32[]{:S(2)}) %collective-permute-start.1) | collective-permute-done | bytes 229408 | tf_op jit(solution)/shard_map/ppermute | solution.py:130
  35.7 1.4 pad_maximum_fusion
  37.1 6.0 %all-to-all-start.1 = ((bf16[16,32,1792]{2,1,0:T(8,128)(2,1)}), bf16[16,32,1792]{2,1,0:T(8,128)(2,1)S(1)}, u32[]{:S(2)}, u32[]{:S(2)}) async-start(bf16[16,32,1792]{2,1,0:T(8,128)(2,1)} %pad_maximum_fusion), calls=%async_computation.1 | async-start | bytes 3670016 | tf_op jit(solution)/shard_map/all_to_all | solution.py:484
  43.1 1.6 %split_rows.2.refs_0_ = bf16[128,5376]{1,0:T(8,128)(2,1)} custom-call(bf16[16,8,5376]{2,1,0:T(8,128)(2,1)S(1)} %all-to-all-done.in_ref), custom_call_target="tpu_custom_call" | custom-call | tf_op jit(solution)/shard_map/split_rows/pallas_call | solution.py:115
  44.7 2.7 %collective-permute-start.5 = (bf16[128,5376]{1,0:T(8,128)(2,1)}, bf16[128,5376]{1,0:T(8,128)(2,1)}, u32[]{:S(2)}, u32[]{:S(2)}) collective-permute-start(bf16[128,5376]{1,0:T(8,128)(2,1)} %split_rows.2.refs_0_), channel_id=1, source_target_pairs={{0,6},{2,0},{4,2},{6,4},{1,7},{3,1},{5,3},{7,5},{8,14},{10,8},{12,... | collective-permute-start | bytes 4128776 | tf_op jit(solution)/shard_map/ppermute | solution.py:130
  47.4 18.1 %all-to-all-done.1.in_ref = bf16[16,32,1792]{2,1,0:T(8,128)(2,1)S(1)} async-done(((bf16[16,32,1792]{2,1,0:T(8,128)(2,1)}), bf16[16,32,1792]{2,1,0:T(8,128)(2,1)S(1)}, u32[]{:S(2)}, u32[]{:S(2)}) %all-to-all-start.1) | async-done | bytes 1835040 | tf_op jit(solution)/shard_map/all_to_all | solution.py:484
  65.5 0.6 split_rows.3.refs_0_
  66.1 5.3 %collective-permute-start.9 = (bf16[512,1792]{1,0:T(8,128)(2,1)S(1)}, bf16[512,1792]{1,0:T(8,128)(2,1)S(1)}, u32[]{:S(2)}, u32[]{:S(2)}) collective-permute-start(bf16[512,1792]{1,0:T(8,128)(2,1)S(1)} %split_rows.3.refs_0_), channel_id=1, source_target_pairs={{0,1},{1,0},{2,3},{3,2},{4,5},{5,4},{6,7},{7,6},{8,9},{9,8},{10,11... | collective-permute-start | bytes 5505032 | tf_op jit(solution)/shard_map/ppermute | solution.py:134
  71.6 3.2 %collective-permute-done.4.refs_1_ = bf16[128,5376]{1,0:T(8,128)(2,1)S(1)} collective-permute-done((bf16[128,5376]{1,0:T(8,128)(2,1)}, bf16[128,5376]{1,0:T(8,128)(2,1)S(1)}, u32[]{:S(2)}, u32[]{:S(2)}) %collective-permute-start.4) | collective-permute-done | bytes 1376288 | tf_op jit(solution)/shard_map/ppermute | solution.py:130
  74.7 4.0 %collective-permute-start.7 = (bf16[128,5376]{1,0:T(8,128)(2,1)S(1)}, bf16[128,5376]{1,0:T(8,128)(2,1)S(1)}, u32[]{:S(2)}, u32[]{:S(2)}) collective-permute-start(bf16[128,5376]{1,0:T(8,128)(2,1)S(1)} %collective-permute-done.4.refs_1_), channel_id=1, source_target_pairs={{0,1},{1,0},{2,3},{3,2},{4,5},{5,4},{6,7},{7,6},{8,9},{9,8},{10,11... | collective-permute-start | bytes 4128776 | tf_op jit(solution)/shard_map/ppermute | solution.py:134
  78.8 0.7 collective-permute-start.15
  79.6 1.1 slice.27
  80.7 2.3 %collective-permute-start.16 = (bf16[64,5376]{1,0:T(8,128)(2,1)S(1)}, bf16[64,5376]{1,0:T(8,128)(2,1)S(1)}, u32[]{:S(2)}, u32[]{:S(2)}) collective-permute-start(bf16[64,5376]{1,0:T(8,128)(2,1)S(1)} %slice.27), channel_id=1, source_target_pairs={{0,6},{2,0},{4,2},{6,4},{1,7},{3,1},{5,3},{7,5},{8,14},{10,8},{12,... | collective-permute-start | bytes 2064392 | tf_op jit(solution)/shard_map/ppermute | solution.py:130
  83.0 4.1 %acts.3 = (f32[3,512,256]{2,1,0:T(8,128)S(1)}, bf16[512,1792]{1,0:T(8,128)(2,1)S(1)}, bf16[512,1792]{1,0:T(8,128)(2,1)S(1)}) custom-call(bf16[512,1792]{1,0:T(8,128)(2,1)} %copy-done, bf16[512,1792]{1,0:T(8,128)(2,1)} %copy-done.5, bf16[7168,256]{1,0:T(8,128)(2,1)} %bitcast.17, bf16[7168,256]{1,0:T(8,128)(2,1)} %bitcast.19, bf16[256,7168]{1,0:T(8,128)(2,1)} %bitcast.21), custom_call_target="tpu_custom_call" | custom-call | flops 1409286144 | bytes 6422528 | tf_op jit(solution)/shard_map/acts/pallas_call | solution.py:276
  87.2 1.0 copy-done.6
  88.2 0.5 copy-done.7
  88.7 0.4 copy-done.8
  89.1 7.9 %acts.4 = (bf16[384,768]{1,0:T(8,128)(2,1)S(1)}, bf16[384,5376]{1,0:T(8,128)(2,1)S(1)}, bf16[384,5376]{1,0:T(8,128)(2,1)S(1)}, bf16[5376,256]{1,0:T(8,128)(2,1)S...) custom-call(bf16[128,5376]{1,0:T(8,128)(2,1)} %split_rows.2.refs_0_, bf16[128,5376]{1,0:T(8,128)(2,1)} %copy-done.4, ...), custom_call_target="tpu_custom_call" | custom-call | flops 3170893824 | bytes 16515072 | tf_op jit(solution)/shard_map/acts/pallas_call | solution.py:276
  97.1 0.7 collective-permute-done.16.refs_1_
  97.7 1.1 collective-permute-start.17
  98.8 1.4 collective-permute-start.10
  100.3 1.8 %collective-permute-start.11 = (bf16[384,768]{1,0:T(8,128)(2,1)S(1)}, bf16[384,768]{1,0:T(8,128)(2,1)S(1)}, u32[]{:S(2)}, u32[]{:S(2)}) collective-permute-start(bf16[384,768]{1,0:T(8,128)(2,1)S(1)} %get-tuple-element.29.hid_a.refs_0_), channel_id=1, source_target_pairs={{0,6},{2,0},{4,2},{6,4},{1,7},{3,1},{5,3},{7,5},{8,14},{10,8},{12,... | collective-permute-start | bytes 1769480 | tf_op jit(solution)/shard_map/ppermute | solution.py:130
  102.1 0.8 collective-permute-start.12
  102.9 0.8 copy-done.11
  104.0 4.3 %acts.5 = (bf16[128,768]{1,0:T(8,128)(2,1)S(1)}, bf16[128,5376]{1,0:T(8,128)(2,1)S(1)}, bf16[128,5376]{1,0:T(8,128)(2,1)S(1)}) custom-call(bf16[64,5376]{1,0:T(8,128)(2,1)} %copy-done.9, bf16[64,5376]{1,0:T(8,128)(2,1)} %copy-done.10, bf16[64,5376]{1,0:T(8,128)(2,1)} %copy-done.11, bf16[64,5376]{1,0:T(8,128)(2,1)} %copy-done.12, ...), custom_call_target="tpu_custom_call" | custom-call | flops 1056964608 | bytes 11010048 | tf_op jit(solution)/shard_map/acts/pallas_call | solution.py:276
  108.3 9.8 %squares.1 = (bf16[144,768]{1,0:T(8,128)(2,1)S(1)}, bf16[896,512]{1,0:T(8,128)(2,1)S(1)}, bf16[896,512]{1,0:T(8,128)(2,1)S(1)}) custom-call(bf16[512,1792]{1,0:T(8,128)(2,1)S(1)} %get-tuple-element.30.x0, bf16[512,1792]{1,0:T(8,128)(2,1)S(1)} %get-tuple-element.31.g0, bf16[384,5376]{1,0:T(8,128)(2,1)S(1)} %get-tuple-element.32.xa, ...), custom_call_target="tpu_custom_call" | custom-call | flops 5637144576 | bytes 14680064 | tf_op jit(solution)/shard_map/squares/pallas_call | solution.py:342
  118.4 2.7 %collective-permute-start.20 = (bf16[336,768]{1,0:T(8,128)(2,1)S(1)}, bf16[336,768]{1,0:T(8,128)(2,1)S(1)}, u32[]{:S(2)}, u32[]{:S(2)}) collective-permute-start(bf16[336,768]{1,0:T(8,128)(2,1)S(1)} %get-tuple-element.47), channel_id=1, source_target_pairs={{0,6},{2,0},{4,2},{6,4},{1,7},{3,1},{5,3},{7,5},{8,14},{10,8},{12,... | collective-permute-start | bytes 1548296 | tf_op jit(solution)/shard_map/ppermute | solution.py:130
  121.1 0.4 collective-permute-start.21
  121.5 1.2 collective-permute-start.13
  122.7 10.5 %collective-permute-done.19.refs_7_ = bf16[336,768]{1,0:T(8,128)(2,1)S(1)} collective-permute-done((bf16[336,768]{1,0:T(8,128)(2,1)S(1)}, bf16[336,768]{1,0:T(8,128)(2,1)S(1)}, u32[]{:S(2)}, u32[]{:S(2)}) %collective-permute-start.19) | collective-permute-done | bytes 516128 | tf_op jit(solution)/shard_map/ppermute | solution.py:130
  133.2 1.2 collective-permute-start.23
  134.4 2.2 %collective-permute-done.20.refs_8_ = bf16[336,768]{1,0:T(8,128)(2,1)S(1)} collective-permute-done((bf16[336,768]{1,0:T(8,128)(2,1)S(1)}, bf16[336,768]{1,0:T(8,128)(2,1)S(1)}, u32[]{:S(2)}, u32[]{:S(2)}) %collective-permute-start.20) | collective-permute-done | bytes 516128 | tf_op jit(solution)/shard_map/ppermute | solution.py:130
  136.5 1.2 collective-permute-start.24
  137.8 0.9 collective-permute-start.22
  138.7 1.1 collective-permute-done.22.refs_10_
  139.8 0.4 collective-permute-start.25
  140.2 1.1 collective-permute-done.25.refs_13_
  141.3 13.1 %final.1 = bf16[3,896,2048]{2,1,0:T(8,128)(2,1)} custom-call(bf16[384,768]{1,0:T(8,128)(2,1)S(1)} %get-tuple-element.29.hid_a.refs_0_, bf16[384,768]{1,0:T(8,128)(2,1)S(1)} %collective-permute-done.10.refs_1_, bf16[384,768]{1,0:T(8,128)(2,1)S(1)} %collective-permute-done.11.refs_2_, bf16[384,768]{1,0:T(8,128)(2,1)S(1)} %collective-permute-done.12.refs_3_, ...), custom_call_target="tpu_custom_call" | custom-call | flops 5637144576 | bytes 22020096 | tf_op jit(solution)/shard_map/final/pallas_call | solution.py:420
  (52 shorter events, 0.9 us)
Async XLA Ops:
  0.0 0.7 copy-start.1
  0.7 0.7 copy-start.2
  1.4 0.7 copy-start.3
  7.4 29.7 %all-to-all-start = ((bf16[16,8,5376]{2,1,0:T(8,128)(2,1)}), bf16[16,8,5376]{2,1,0:T(8,128)(2,1)S(1)}, u32[]{:S(2)}, u32[]{:S(2)}) async-start(bf16[16,8,5376]{2,1,0:T(8,128)(2,1)} %bitcast.2), calls=%async_computation | async-start | bytes 2752512 | tf_op jit(solution)/shard_map/all_to_all | solution.py:477
  15.0 13.7 %collective-permute-start = (bf16[128,1792]{1,0:T(8,128)(2,1)S(1)}, bf16[128,1792]{1,0:T(8,128)(2,1)S(1)}, u32[]{:S(2)}, u32[]{:S(2)}) collective-permute-start(bf16[128,1792]{1,0:T(8,128)(2,1)S(1)} %dispatch.2), channel_id=1, source_target_pairs={{0,2},{2,4},{4,6},{6,0},{1,3},{3,5},{5,7},{7,1},{8,10},{10,12},{12... | collective-permute-start | bytes 1376264 | tf_op jit(solution)/shard_map/ppermute | solution.py:130
  16.7 12.1 %collective-permute-start.2 = (bf16[128,1792]{1,0:T(8,128)(2,1)S(1)}, bf16[128,1792]{1,0:T(8,128)(2,1)S(1)}, u32[]{:S(2)}, u32[]{:S(2)}) collective-permute-start(bf16[128,1792]{1,0:T(8,128)(2,1)S(1)} %dispatch.2), channel_id=1, source_target_pairs={{0,6},{2,0},{4,2},{6,4},{1,7},{3,1},{5,3},{7,5},{8,14},{10,8},{12,... | collective-permute-start | bytes 1376264 | tf_op jit(solution)/shard_map/ppermute | solution.py:130
  28.8 6.8 %collective-permute-start.1 = (bf16[64,1792]{1,0:T(8,128)(2,1)S(1)}, bf16[64,1792]{1,0:T(8,128)(2,1)S(1)}, u32[]{:S(2)}, u32[]{:S(2)}) collective-permute-start(bf16[64,1792]{1,0:T(8,128)(2,1)S(1)} %slice.24), channel_id=1, source_target_pairs={{0,2},{2,4},{4,6},{6,0},{1,3},{3,5},{5,7},{7,1},{8,10},{10,12},{12... | collective-permute-start | bytes 688136 | tf_op jit(solution)/shard_map/ppermute | solution.py:130
  28.9 6.7 %collective-permute-start.3 = (bf16[64,1792]{1,0:T(8,128)(2,1)S(1)}, bf16[64,1792]{1,0:T(8,128)(2,1)S(1)}, u32[]{:S(2)}, u32[]{:S(2)}) collective-permute-start(bf16[64,1792]{1,0:T(8,128)(2,1)S(1)} %slice.25), channel_id=1, source_target_pairs={{0,6},{2,0},{4,2},{6,4},{1,7},{3,1},{5,3},{7,5},{8,14},{10,8},{12,... | collective-permute-start | bytes 688136 | tf_op jit(solution)/shard_map/ppermute | solution.py:130
  37.1 28.4 %all-to-all-start.1 = ((bf16[16,32,1792]{2,1,0:T(8,128)(2,1)}), bf16[16,32,1792]{2,1,0:T(8,128)(2,1)S(1)}, u32[]{:S(2)}, u32[]{:S(2)}) async-start(bf16[16,32,1792]{2,1,0:T(8,128)(2,1)} %pad_maximum_fusion), calls=%async_computation.1 | async-start | bytes 3670016 | tf_op jit(solution)/shard_map/all_to_all | solution.py:484
  44.7 30.0 %collective-permute-start.4 = (bf16[128,5376]{1,0:T(8,128)(2,1)}, bf16[128,5376]{1,0:T(8,128)(2,1)S(1)}, u32[]{:S(2)}, u32[]{:S(2)}) collective-permute-start(bf16[128,5376]{1,0:T(8,128)(2,1)} %split_rows.2.refs_0_), channel_id=1, source_target_pairs={{0,2},{2,4},{4,6},{6,0},{1,3},{3,5},{5,7},{7,1},{8,10},{10,12},{12... | collective-permute-start | bytes 4128776 | tf_op jit(solution)/shard_map/ppermute | solution.py:130
  44.7 34.0 %collective-permute-start.5 = (bf16[128,5376]{1,0:T(8,128)(2,1)}, bf16[128,5376]{1,0:T(8,128)(2,1)}, u32[]{:S(2)}, u32[]{:S(2)}) collective-permute-start(bf16[128,5376]{1,0:T(8,128)(2,1)} %split_rows.2.refs_0_), channel_id=1, source_target_pairs={{0,6},{2,0},{4,2},{6,4},{1,7},{3,1},{5,3},{7,5},{8,14},{10,8},{12,... | collective-permute-start | bytes 4128776 | tf_op jit(solution)/shard_map/ppermute | solution.py:130
  66.1 16.9 %copy-start = (bf16[512,1792]{1,0:T(8,128)(2,1)}, bf16[512,1792]{1,0:T(8,128)(2,1)S(1)}, u32[]{:S(2)}) copy-start(bf16[512,1792]{1,0:T(8,128)(2,1)S(1)} %split_rows.3.refs_0_) | copy-start | bytes 5505028
  66.1 14.6 %collective-permute-start.9 = (bf16[512,1792]{1,0:T(8,128)(2,1)S(1)}, bf16[512,1792]{1,0:T(8,128)(2,1)S(1)}, u32[]{:S(2)}, u32[]{:S(2)}) collective-permute-start(bf16[512,1792]{1,0:T(8,128)(2,1)S(1)} %split_rows.3.refs_0_), channel_id=1, source_target_pairs={{0,1},{1,0},{2,3},{3,2},{4,5},{5,4},{6,7},{7,6},{8,9},{9,8},{10,11... | collective-permute-start | bytes 5505032 | tf_op jit(solution)/shard_map/ppermute | solution.py:134
  71.5 15.7 %collective-permute-start.6 = (bf16[128,5376]{1,0:T(8,128)(2,1)}, bf16[128,5376]{1,0:T(8,128)(2,1)S(1)}, u32[]{:S(2)}, u32[]{:S(2)}) collective-permute-start(bf16[128,5376]{1,0:T(8,128)(2,1)} %split_rows.2.refs_0_), channel_id=1, source_target_pairs={{0,1},{1,0},{2,3},{3,2},{4,5},{5,4},{6,7},{7,6},{8,9},{9,8},{10,11... | collective-permute-start | bytes 4128776 | tf_op jit(solution)/shard_map/ppermute | solution.py:134
  74.7 12.4 %copy-start.4 = (bf16[128,5376]{1,0:T(8,128)(2,1)}, bf16[128,5376]{1,0:T(8,128)(2,1)S(1)}, u32[]{:S(2)}) copy-start(bf16[128,5376]{1,0:T(8,128)(2,1)S(1)} %collective-permute-done.4.refs_1_) | copy-start | bytes 4128772
  74.7 12.4 %collective-permute-start.7 = (bf16[128,5376]{1,0:T(8,128)(2,1)S(1)}, bf16[128,5376]{1,0:T(8,128)(2,1)S(1)}, u32[]{:S(2)}, u32[]{:S(2)}) collective-permute-start(bf16[128,5376]{1,0:T(8,128)(2,1)S(1)} %collective-permute-done.4.refs_1_), channel_id=1, source_target_pairs={{0,1},{1,0},{2,3},{3,2},{4,5},{5,4},{6,7},{7,6},{8,9},{9,8},{10,11... | collective-permute-start | bytes 4128776 | tf_op jit(solution)/shard_map/ppermute | solution.py:134
  78.7 8.5 %collective-permute-start.8 = (bf16[128,5376]{1,0:T(8,128)(2,1)}, bf16[128,5376]{1,0:T(8,128)(2,1)S(1)}, u32[]{:S(2)}, u32[]{:S(2)}) collective-permute-start(bf16[128,5376]{1,0:T(8,128)(2,1)} %collective-permute-done.5.refs_2_), channel_id=1, source_target_pairs={{0,1},{1,0},{2,3},{3,2},{4,5},{5,4},{6,7},{7,6},{8,9},{9,8},{10,11... | collective-permute-start | bytes 4128776 | tf_op jit(solution)/shard_map/ppermute | solution.py:134
  78.8 18.2 %collective-permute-start.15 = (bf16[64,5376]{1,0:T(8,128)(2,1)S(1)}, bf16[64,5376]{1,0:T(8,128)(2,1)S(1)}, u32[]{:S(2)}, u32[]{:S(2)}) collective-permute-start(bf16[64,5376]{1,0:T(8,128)(2,1)S(1)} %slice.26), channel_id=1, source_target_pairs={{0,2},{2,4},{4,6},{6,0},{1,3},{3,5},{5,7},{7,1},{8,10},{10,12},{12... | collective-permute-start | bytes 2064392 | tf_op jit(solution)/shard_map/ppermute | solution.py:130
  80.7 2.3 %copy-start.5 = (bf16[512,1792]{1,0:T(8,128)(2,1)}, bf16[512,1792]{1,0:T(8,128)(2,1)S(1)}, u32[]{:S(2)}) copy-start(bf16[512,1792]{1,0:T(8,128)(2,1)S(1)} %collective-permute-done.9.refs_1_) | copy-start | bytes 5505028
  80.7 17.0 %collective-permute-start.16 = (bf16[64,5376]{1,0:T(8,128)(2,1)S(1)}, bf16[64,5376]{1,0:T(8,128)(2,1)S(1)}, u32[]{:S(2)}, u32[]{:S(2)}) collective-permute-start(bf16[64,5376]{1,0:T(8,128)(2,1)S(1)} %slice.27), channel_id=1, source_target_pairs={{0,6},{2,0},{4,2},{6,4},{1,7},{3,1},{5,3},{7,5},{8,14},{10,8},{12,... | collective-permute-start | bytes 2064392 | tf_op jit(solution)/shard_map/ppermute | solution.py:130
  87.1 1.1 copy-start.6
  87.2 1.5 %copy-start.7 = (bf16[128,5376]{1,0:T(8,128)(2,1)}, bf16[128,5376]{1,0:T(8,128)(2,1)S(1)}, u32[]{:S(2)}) copy-start(bf16[128,5376]{1,0:T(8,128)(2,1)S(1)} %collective-permute-done.7.refs_4_) | copy-start | bytes 4128772
  87.2 2.0 %copy-start.8 = (bf16[128,5376]{1,0:T(8,128)(2,1)}, bf16[128,5376]{1,0:T(8,128)(2,1)S(1)}, u32[]{:S(2)}) copy-start(bf16[128,5376]{1,0:T(8,128)(2,1)S(1)} %collective-permute-done.8.refs_5_) | copy-start | bytes 4128772
  97.1 5.8 %copy-start.9 = (bf16[64,5376]{1,0:T(8,128)(2,1)}, bf16[64,5376]{1,0:T(8,128)(2,1)S(1)}, u32[]{:S(2)}) copy-start(bf16[64,5376]{1,0:T(8,128)(2,1)S(1)} %collective-permute-done.15.refs_0_) | copy-start | bytes 2064388
  97.7 5.2 %copy-start.10 = (bf16[64,5376]{1,0:T(8,128)(2,1)}, bf16[64,5376]{1,0:T(8,128)(2,1)S(1)}, u32[]{:S(2)}) copy-start(bf16[64,5376]{1,0:T(8,128)(2,1)S(1)} %collective-permute-done.16.refs_1_) | copy-start | bytes 2064388
  97.7 5.2 %collective-permute-start.17 = (bf16[64,5376]{1,0:T(8,128)(2,1)S(1)}, bf16[64,5376]{1,0:T(8,128)(2,1)S(1)}, u32[]{:S(2)}, u32[]{:S(2)}) collective-permute-start(bf16[64,5376]{1,0:T(8,128)(2,1)S(1)} %collective-permute-done.15.refs_0_), channel_id=1, source_target_pairs={{0,1},{1,0},{2,3},{3,2},{4,5},{5,4},{6,7},{7,6},{8,9},{9,8},{10,11... | collective-permute-start | bytes 2064392 | tf_op jit(solution)/shard_map/ppermute | solution.py:134
  98.8 4.1 %collective-permute-start.18 = (bf16[64,5376]{1,0:T(8,128)(2,1)S(1)}, bf16[64,5376]{1,0:T(8,128)(2,1)S(1)}, u32[]{:S(2)}, u32[]{:S(2)}) collective-permute-start(bf16[64,5376]{1,0:T(8,128)(2,1)S(1)} %collective-permute-done.16.refs_1_), channel_id=1, source_target_pairs={{0,1},{1,0},{2,3},{3,2},{4,5},{5,4},{6,7},{7,6},{8,9},{9,8},{10,11... | collective-permute-start | bytes 2064392 | tf_op jit(solution)/shard_map/ppermute | solution.py:134
  98.8 19.3 %collective-permute-start.10 = (bf16[384,768]{1,0:T(8,128)(2,1)S(1)}, bf16[384,768]{1,0:T(8,128)(2,1)S(1)}, u32[]{:S(2)}, u32[]{:S(2)}) collective-permute-start(bf16[384,768]{1,0:T(8,128)(2,1)S(1)} %get-tuple-element.29.hid_a.refs_0_), channel_id=1, source_target_pairs={{0,2},{2,4},{4,6},{6,0},{1,3},{3,5},{5,7},{7,1},{8,10},{10,12},{12... | collective-permute-start | bytes 1769480 | tf_op jit(solution)/shard_map/ppermute | solution.py:130
  100.3 17.9 %collective-permute-start.11 = (bf16[384,768]{1,0:T(8,128)(2,1)S(1)}, bf16[384,768]{1,0:T(8,128)(2,1)S(1)}, u32[]{:S(2)}, u32[]{:S(2)}) collective-permute-start(bf16[384,768]{1,0:T(8,128)(2,1)S(1)} %get-tuple-element.29.hid_a.refs_0_), channel_id=1, source_target_pairs={{0,6},{2,0},{4,2},{6,4},{1,7},{3,1},{5,3},{7,5},{8,14},{10,8},{12,... | collective-permute-start | bytes 1769480 | tf_op jit(solution)/shard_map/ppermute | solution.py:130
  102.1 20.6 %collective-permute-start.12 = (bf16[384,768]{1,0:T(8,128)(2,1)S(1)}, bf16[384,768]{1,0:T(8,128)(2,1)S(1)}, u32[]{:S(2)}, u32[]{:S(2)}) collective-permute-start(bf16[384,768]{1,0:T(8,128)(2,1)S(1)} %get-tuple-element.29.hid_a.refs_0_), channel_id=1, source_target_pairs={{0,1},{1,0},{2,3},{3,2},{4,5},{5,4},{6,7},{7,6},{8,9},{9,8},{10,11... | collective-permute-start | bytes 1769480 | tf_op jit(solution)/shard_map/ppermute | solution.py:134
  102.9 0.9 copy-start.11
  102.9 1.1 copy-start.12
  118.3 14.9 %collective-permute-start.19 = (bf16[336,768]{1,0:T(8,128)(2,1)S(1)}, bf16[336,768]{1,0:T(8,128)(2,1)S(1)}, u32[]{:S(2)}, u32[]{:S(2)}) collective-permute-start(bf16[336,768]{1,0:T(8,128)(2,1)S(1)} %get-tuple-element.48), channel_id=1, source_target_pairs={{0,2},{2,4},{4,6},{6,0},{1,3},{3,5},{5,7},{7,1},{8,10},{10,12},{12... | collective-permute-start | bytes 1548296 | tf_op jit(solution)/shard_map/ppermute | solution.py:130
  118.4 18.1 %collective-permute-start.20 = (bf16[336,768]{1,0:T(8,128)(2,1)S(1)}, bf16[336,768]{1,0:T(8,128)(2,1)S(1)}, u32[]{:S(2)}, u32[]{:S(2)}) collective-permute-start(bf16[336,768]{1,0:T(8,128)(2,1)S(1)} %get-tuple-element.47), channel_id=1, source_target_pairs={{0,6},{2,0},{4,2},{6,4},{1,7},{3,1},{5,3},{7,5},{8,14},{10,8},{12,... | collective-permute-start | bytes 1548296 | tf_op jit(solution)/shard_map/ppermute | solution.py:130
  121.1 16.7 %collective-permute-start.21 = (bf16[144,768]{1,0:T(8,128)(2,1)S(1)}, bf16[144,768]{1,0:T(8,128)(2,1)S(1)}, u32[]{:S(2)}, u32[]{:S(2)}) collective-permute-start(bf16[144,768]{1,0:T(8,128)(2,1)S(1)} %get-tuple-element.42.refs_6_), channel_id=1, source_target_pairs={{0,4},{2,6},{4,0},{6,2},{1,5},{3,7},{5,1},{7,3},{8,12},{10,14},{12... | collective-permute-start | bytes 663560 | tf_op jit(solution)/shard_map/ppermute | solution.py:130
  121.5 19.8 %collective-permute-start.13 = (bf16[384,768]{1,0:T(8,128)(2,1)S(1)}, bf16[384,768]{1,0:T(8,128)(2,1)S(1)}, u32[]{:S(2)}, u32[]{:S(2)}) collective-permute-start(bf16[384,768]{1,0:T(8,128)(2,1)S(1)} %collective-permute-done.10.refs_1_), channel_id=1, source_target_pairs={{0,1},{1,0},{2,3},{3,2},{4,5},{5,4},{6,7},{7,6},{8,9},{9,8},{10,11... | collective-permute-start | bytes 1769480 | tf_op jit(solution)/shard_map/ppermute | solution.py:134
  122.7 18.6 %collective-permute-start.14 = (bf16[384,768]{1,0:T(8,128)(2,1)S(1)}, bf16[384,768]{1,0:T(8,128)(2,1)S(1)}, u32[]{:S(2)}, u32[]{:S(2)}) collective-permute-start(bf16[384,768]{1,0:T(8,128)(2,1)S(1)} %collective-permute-done.11.refs_2_), channel_id=1, source_target_pairs={{0,1},{1,0},{2,3},{3,2},{4,5},{5,4},{6,7},{7,6},{8,9},{9,8},{10,11... | collective-permute-start | bytes 1769480 | tf_op jit(solution)/shard_map/ppermute | solution.py:134
  133.2 8.1 %collective-permute-start.23 = (bf16[336,768]{1,0:T(8,128)(2,1)S(1)}, bf16[336,768]{1,0:T(8,128)(2,1)S(1)}, u32[]{:S(2)}, u32[]{:S(2)}) collective-permute-start(bf16[336,768]{1,0:T(8,128)(2,1)S(1)} %collective-permute-done.19.refs_7_), channel_id=1, source_target_pairs={{0,1},{1,0},{2,3},{3,2},{4,5},{5,4},{6,7},{7,6},{8,9},{9,8},{10,11... | collective-permute-start | bytes 1548296 | tf_op jit(solution)/shard_map/ppermute | solution.py:134
  136.5 4.8 %collective-permute-start.24 = (bf16[336,768]{1,0:T(8,128)(2,1)S(1)}, bf16[336,768]{1,0:T(8,128)(2,1)S(1)}, u32[]{:S(2)}, u32[]{:S(2)}) collective-permute-start(bf16[336,768]{1,0:T(8,128)(2,1)S(1)} %collective-permute-done.20.refs_8_), channel_id=1, source_target_pairs={{0,1},{1,0},{2,3},{3,2},{4,5},{5,4},{6,7},{7,6},{8,9},{9,8},{10,11... | collective-permute-start | bytes 1548296 | tf_op jit(solution)/shard_map/ppermute | solution.py:134
  137.8 2.0 %collective-permute-start.22 = (bf16[144,768]{1,0:T(8,128)(2,1)S(1)}, bf16[144,768]{1,0:T(8,128)(2,1)S(1)}, u32[]{:S(2)}, u32[]{:S(2)}) collective-permute-start(bf16[144,768]{1,0:T(8,128)(2,1)S(1)} %get-tuple-element.42.refs_6_), channel_id=1, source_target_pairs={{0,1},{1,0},{2,3},{3,2},{4,5},{5,4},{6,7},{7,6},{8,9},{9,8},{10,11... | collective-permute-start | bytes 663560 | tf_op jit(solution)/shard_map/ppermute | solution.py:134
  139.8 1.5 collective-permute-start.25

commit v3 on v2

--- a/solution.py
+++ b/solution.py
@@ -40,13 +40,20 @@
     return lax.broadcasted_iota(jnp.int32, shape, dim)
 
 
-def dispatch_kernel(first, tiles, ids_ref, comb_ref, rank_ref, tok, grad, out_ref, both, sems):
+def dispatch_kernel(first, tiles, *refs):
+    small, (tok, grad, out_ref), refs = refs[:3], refs[3:6], refs[6:]
+    ids_ref, comb_ref, rank_ref = refs[:3]
+    both, sems = refs[3:]
+    for k in range(3):
+        pltpu.make_async_copy(small[k], refs[k], sems.at[tiles + k]).start()
     rows = out_ref.shape[0]
     toks = tok.shape[0]
     for j in range(tiles):
         span = pl.ds((first + j) * TILE, TILE)
         pltpu.make_async_copy(tok.at[:, span], both.at[j, pl.ds(0, toks), :], sems.at[j]).start()
         pltpu.make_async_copy(grad.at[:, span], both.at[j, pl.ds(toks, toks), :], sems.at[j]).start()
+    for k in range(3):
+        pltpu.make_async_copy(small[k], refs[k], sems.at[tiles + k]).wait()
     routed = rank_ref.shape[0]
     ranks = rank_ref[...].reshape(1, routed)
     expert_row = iota((rows, routed), 0) >> ROW_BITS
@@ -80,19 +87,22 @@
     toks = tokens.shape[0]
     return pl.pallas_call(
         functools.partial(dispatch_kernel, first, tiles),
-        in_specs=[VMEM, VMEM, VMEM, HBM, HBM],
+        in_specs=[HBM] * 5,
         out_specs=VMEM,
         out_shape=jax.ShapeDtypeStruct((rows, tiles * TILE), BF16),
         scratch_shapes=[
+            pltpu.VMEM(ids.shape, ids.dtype),
+            pltpu.VMEM(comb.shape, comb.dtype),
+            pltpu.VMEM(ranks.shape, ranks.dtype),
             pltpu.VMEM((tiles, 2 * toks, TILE), BF16),
-            pltpu.SemaphoreType.DMA((tiles,)),
+            pltpu.SemaphoreType.DMA((tiles + 3,)),
         ],
         compiler_params=params(20),
         cost_estimate=pl.CostEstimate(
             flops=tiles * 8 * toks * rows * TILE, bytes_accessed=tiles * 6 * toks * TILE, transcendentals=0
         ),
         name="dispatch",
-    )(ids, comb, ranks, *in_hbm(tokens, out_grad))
+    )(*in_hbm(ids, comb, ranks, tokens, out_grad))
 
 
 def split_kernel(order, in_ref, out_ref):
@@ -159,6 +169,10 @@
     def __init__(self, first, arrays, kind, groups):
         self.first, self.arrays, self.kind, self.groups = first, arrays, kind, groups
         self.width = arrays[0].shape[1]
+
+    def pinned(self):
+        count = len(self.arrays) // 2 if self.kind == "parts" and self.groups[0] == 0 else 0
+        return in_hbm(*self.arrays[:count]) + list(self.arrays[count:])
 
     def sources(self, refs, a, n):
         refs = refs[a * len(refs) // 2 : (a + 1) * len(refs) // 2]
@@ -275,7 +289,7 @@
     extra = [] if before is None else [before]
     return pl.pallas_call(
         functools.partial(acts_kernel, rows_of, skip, last, keep, given),
-        in_specs=[HBM] * len(rows_of.arrays) + [VMEM if given else HBM] * 3 + [VMEM] * len(extra),
+        in_specs=[ANY] * len(rows_of.arrays) + [VMEM if given else HBM] * 3 + [VMEM] * len(extra),
         out_specs=(VMEM,) * len(outs),
         out_shape=in_vmem(*outs),
         scratch_shapes=scratch,
@@ -286,7 +300,7 @@
             transcendentals=0,
         ),
         name="acts",
-    )(*in_hbm(*rows_of.arrays), *(weights if given else in_hbm(*weights)), *extra)
+    )(*rows_of.pinned(), *(weights if given else in_hbm(*weights)), *extra)
 
 
 def squares_kernel(x0, g0, xa, ga, xb, gb, hid_a, hid_b, last_ref, xt_ref, gt_ref, hid_t, parts):
@@ -355,25 +369,70 @@
     )(*rows_of_x, hid_a, hid_b)
 
 
-def final_kernel(entries, copies, sums, *refs):
-    arrays, refs = refs[: -8], refs[-8:]
-    xt_ref, gt_ref, out_ref, hid, coded, stage, in_sems, out_sems = refs
+def start_copies(copies, source, slot, arrays, hid, sems):
+    for owner, i, row, at, n in copies:
+        if owner == source:
+            pltpu.make_async_copy(
+                arrays[i].at[pl.ds(row, n), :], hid.at[slot, pl.ds(at, n), :], sems.at[slot]
+            ).start()
+
+
+def wait_rows(hid, slot, rows, sems):
+    ref = hid.at[slot, pl.ds(0, rows), :]
+    pltpu.make_async_copy(ref, ref, sems.at[slot]).wait()
+
+
+def early_kernel(copies, missing, *refs):
+    arrays, (xt_ref, gt_ref, pre_ref, hid, sems) = refs[:-5], refs[-5:]
+    count, rows = hid.shape[0], hid.shape[1]
+    m = hid.shape[2] // 3
+    for k in range(count):
+        start_copies(copies, k, k, arrays, hid, sems)
+        if missing[k] is not None:
+            at, n = missing[k]
+            hid[k, at : at + n, :] = jnp.zeros((n, 3 * m), BF16)
+    for k in range(count):
+        wait_rows(hid, k, rows - (0 if missing[k] is None else missing[k][1]), sems)
+        for i in range(3):
+            lhs = gt_ref if i == 2 else xt_ref
+            pre_ref[k, i] = jnp.dot(
+                lhs[...], hid[k, :, i * m : (i + 1) * m], preferred_element_type=F32
+            )
+
+
+def early_products(copies, missing, arrays, xt, gt):
+    rows = xt.shape[1]
+    width = arrays[0].shape[1]
+    count = len(missing)
+    return pl.pallas_call(
+        functools.partial(early_kernel, copies, missing),
+        in_specs=[ANY] * len(arrays) + [VMEM] * 2,
+        out_specs=VMEM,
+        out_shape=in_vmem(((count, 3, TILE, width // 3), F32))[0],
+        scratch_shapes=[
+            pltpu.VMEM((count, rows, width), BF16),
+            pltpu.SemaphoreType.DMA((count,)),
+        ],
+        compiler_params=params(12),
+        cost_estimate=pl.CostEstimate(
+            flops=2 * rows * TILE * width * count,
+            bytes_accessed=2 * rows * width * count,
+            transcendentals=0,
+        ),
+        name="early_products",
+    )(*arrays, xt, gt)
+
+
+def final_kernel(entries, plan, copies, sums, *refs):
+    arrays, refs = refs[:-9], refs[-9:]
+    pre_ref, xt_ref, gt_ref, out_ref, hid, coded, stage, in_sems, out_sems = refs
     for k, (i, row) in enumerate(sums):
         pltpu.make_async_copy(
             arrays[i].at[pl.ds(row, 16), pl.ds(0, 128)], coded.at[k], in_sems.at[8]
         ).start()
-
-    def start(source):
-        for owner, i, row, at, n in copies:
-            if owner == source:
-                pltpu.make_async_copy(
-                    arrays[i].at[pl.ds(row, n), :],
-                    hid.at[source, pl.ds(at, n), :],
-                    in_sems.at[source],
-                ).start()
-
-    start(0)
-    start(1)
+    for source, _, _, rows in plan:
+        if rows is not None:
+            start_copies(copies, source, source, arrays, hid, in_sems)
     m = hid.shape[2] // 3
     pltpu.make_async_copy(coded, coded, in_sems.at[8]).wait()
     pieces = jnp.sum(coded[...].astype(F32), axis=0)
@@ -382,61 +441,58 @@
         total = jnp.sum(pieces[3 * i : 3 * i + 3, :], axis=0, keepdims=True)
         factors.append(lax.rsqrt(total[:, 0:1] / entries + EPSILON))
 
-    def store(slot, i):
-        dz = jnp.where(i % 4 == 1, 3, jnp.where(i % 4 == 2, 1, jnp.where(i % 4 == 3, 2, 0)))
-        at = pl.ds(pl.multiple_of(position(i // 4, dz) * m, m), m)
+    def store(slot, source):
+        at = position(source // 4, (0, 3, 1, 2)[source % 4])
+        at = pl.ds(pl.multiple_of(at * m, m), m)
         return pltpu.make_async_copy(stage.at[slot], out_ref.at[:, :, at], out_sems.at[slot])
 
-    @pl.loop(0, 8)
-    def _(i):
-        slot = i % 2
-        pltpu.make_async_copy(hid.at[i], hid.at[i], in_sems.at[i]).wait()
-
-        @pl.when(i == 0)
-        def _():
-            for source in range(2, 8):
-                start(source)
-
-        @pl.when(i >= 2)
-        def _():
-            store(slot, i - 2).wait()
-
-        for k in range(3):
-            lhs = gt_ref if k == 2 else xt_ref
-            grads = jnp.dot(
-                lhs[...], hid[i, :, k * m : (k + 1) * m], preferred_element_type=F32
-            )
-            stage[slot, k] = (grads * factors[k]).astype(BF16)
-        store(slot, i).start()
-
-    store(0, 6).wait()
-    store(1, 7).wait()
-
-
-def final(copies, sums, arrays, xt, gt, entries):
+    slots = stage.shape[0]
+    for step, (source, early, at, rows) in enumerate(plan):
+        slot = step % slots
+        if step >= slots:
+            store(slot, plan[step - slots][0]).wait()
+        if rows is not None:
+            wait_rows(hid, source, rows, in_sems)
+        for i in range(3):
+            lhs = gt_ref if i == 2 else xt_ref
+            grads = None if early is None else pre_ref[early, i]
+            if rows is not None:
+                more = jnp.dot(
+                    lhs[:, at : at + rows],
+                    hid[source, :rows, i * m : (i + 1) * m],
+                    preferred_element_type=F32,
+                )
+                grads = more if grads is None else grads + more
+            stage[slot, i] = (grads * factors[i]).astype(BF16)
+        store(slot, source).start()
+    for step in range(len(plan) - slots, len(plan)):
+        store(step % slots, plan[step][0]).wait()
+
+
+def final(plan, copies, sums, arrays, pre, xt, gt, entries):
     rows = xt.shape[1]
     width = arrays[0].shape[1]
     m = width // 3
     return pl.pallas_call(
-        functools.partial(final_kernel, entries, copies, sums),
-        in_specs=[ANY] * len(arrays) + [VMEM] * 2,
+        functools.partial(final_kernel, entries, plan, copies, sums),
+        in_specs=[ANY] * len(arrays) + [VMEM] * 3,
         out_specs=HBM,
         out_shape=jax.ShapeDtypeStruct((3, TILE, 8 * m), BF16),
         scratch_shapes=[
             pltpu.VMEM((8, rows, width), BF16),
             pltpu.VMEM((8, 16, 128), BF16),
-            pltpu.VMEM((2, 3, TILE, m), BF16),
+            pltpu.VMEM((3, 3, TILE, m), BF16),
             pltpu.SemaphoreType.DMA((9,)),
-            pltpu.SemaphoreType.DMA((2,)),
+            pltpu.SemaphoreType.DMA((3,)),
         ],
-        compiler_params=params(16),
+        compiler_params=params(20),
         cost_estimate=pl.CostEstimate(
-            flops=2 * rows * TILE * width * 8,
+            flops=rows * TILE * width * 8,
             bytes_accessed=4 * TILE * width * 8,
             transcendentals=0,
         ),
         name="final",
-    )(*arrays, xt, gt)
+    )(*arrays, pre, xt, gt)
 
 
 def placed(source, array, row, group, offset, count, z, size):
@@ -468,9 +524,9 @@
     weights = (gate_weight[0], up_weight[0], down_weight[0])
     ids, comb = expert_ids.T, combine.T
     tiles = width // TILE
-    sent = dispatch(ids, comb, expert_rank, tokens, out_grad, 0, EARLY, rows)
-    ranks = after(expert_rank, sent)
-    sent_rest = dispatch(ids, comb, ranks, tokens, out_grad, EARLY, tiles - EARLY, rows)
+    sent_rest = dispatch(ids, comb, expert_rank, tokens, out_grad, EARLY, tiles - EARLY, rows)
+    ranks = after(expert_rank, sent_rest)
+    sent = dispatch(ids, comb, ranks, tokens, out_grad, 0, EARLY, rows)
     early = EARLY * TILE
 
     near = near_z(sent)
@@ -480,6 +536,7 @@
     block = split_rows(got, (0,))
     far = far_z(near[1], near[2], n)
     block = after(block, far)
+    near = list(after(tuple(near), block))
     four = [t.reshape(hot, 2 * CAP, early) for t in near + [jnp.concatenate(far)]]
     got = lax.all_to_all(
         jnp.concatenate(four, axis=1), expert, split_axis=0, concat_axis=0, tiled=True
@@ -508,24 +565,35 @@
         along(jnp.concatenate([down_a[half:], hid_b]), 3),
         along(hid_b, 2),
     ]
-    near_a = with_other(near_a)
-    last = with_other(last)
+    near_a = with_other([hid_a, up_a, down_a])
 
     size = 2 * n
-    copies, sums = [], []
+    other = swap(hid_b)
+    copies, missing = [], []
     for a in range(2):
         for k, z in enumerate(NEAR_Z):
-            copies += placed(4 * a + k, 3 * a + k, 0, 0, 0, 3 * size, z, size)
-        mine, up, down, other = range(6 + 4 * a, 10 + 4 * a)
-        copies += placed(4 * a, mine, 0, 3, 0, size, 0, size)
-        copies += placed(4 * a + 1, up, half, 3, 0, size, 3, size)
-        copies += placed(4 * a + 2, down, half, 3, 0, size, 1, size)
+            copies += placed(3 * a + k, 3 * a + k, 0, 0, 0, 3 * size, z, size)
+            missing.append(None if z == 0 else ((3 + z) % 4 * size, size))
+        copies += placed(3 * a, 6 + a, 0, 3, 0, size, 0, size)
+    pre = early_products(copies, missing, near_a + [hid_b, other], xt, gt)
+
+    last = last[1:]
+    last = [hid_b, other] + last + [swap(t) for t in after(last, pre)]
+    copies, sums, plan = [], [(0, size), (1, size)], []
+    for a in range(2):
+        up, down, far = range(2 + 3 * a, 5 + 3 * a)
+        plan.append((4 * a, 3 * a, 0, None))
+        plan.append((4 * a + 1, 3 * a + 1, 2 * size, size))
+        plan.append((4 * a + 2, 3 * a + 2, 0, size))
+        plan.append((4 * a + 3, None, 0, 4 * size))
+        copies += [(4 * a + 1, up, half, 0, size), (4 * a + 2, down, half, 0, size)]
         copies += placed(4 * a + 3, up, 0, 0, 0, half, 2, size)
         copies += placed(4 * a + 3, down, 0, half // size, half % size, half, 2, size)
-        copies += placed(4 * a + 3, other, 0, 3, 0, size, 2, size)
-        sums += [(mine, size), (up, half + size), (down, half + size), (other, size)]
+        copies += placed(4 * a + 3, far, 0, 3, 0, size, 2, size)
+        sums += [(up, half + size), (down, half + size), (far, size)]
+    plan.sort(key=lambda step: step[0] % 4)
     entries = width * weights[0].shape[1] * 8
-    return final(copies, sums, near_a + last, xt, gt, entries)[None]
+    return final(plan, copies, sums, last, pre, xt, gt, entries)[None]
 
 
 def solution(mesh):

time: 155 us -> 152 us (0.981)
  starting transfers between devices: 48.7 us -> 45.1 us
  Pallas kernels: 46.9 us -> 49.5 us
  local copies, waits for them, and re-layouts: 6.34 us -> 3.88 us
    pallas_call x1 -> x2, Pallas kernels: 13.1 us -> 17.7 us  [the longest x1 9.12 us: final(): pl.pallas_call(functools.partial(final_kernel, entries, plan, copies, sum...]
    ppermute x13, starting transfers between devices: 18.8 us -> 14.4 us  [along(): return lax.ppermute(x, 'z', shift(4, k))]
    ppermute x13, waiting for transfers between devices: 30.3 us -> 26.7 us  [along(): return lax.ppermute(x, 'z', shift(4, k))]
    unnamed x26 -> x12, local copies, waits for them, and re-layouts: 5.08 us -> 1.51 us
    all_to_all x1, waiting for transfers between devices: 18.1 us -> 20.6 us  [body(): lax.all_to_all(jnp.concatenate(four, axis=1), expert, split_axis=0, conca...]
  transfers between devices with their start and end apart: 28 -> 28, of which waited for: 9 -> 11; matrix products, arithmetic and copies ran while one was open for 2% -> 2% of each run, Pallas kernels for 18% -> 24%
where the time goes in v3:
time: 152 us
  waiting for transfers between devices  50.8 us (33%)
  Pallas kernels  49.5 us (33%)
  starting transfers between devices  45.1 us (30%)
  local copies, waits for them, and re-layouts  3.88 us (3%)
  other arithmetic  2.32 us (2%)
    ppermute x13, waiting for transfers between devices, along(): return lax.ppermute(x, 'z', shift(4, k))  26.7 us
    all_to_all x1, waiting for transfers between devices, body(): lax.all_to_all(jnp.concatenate(four, axis=1), expert, split_axis=0, conca...  20.6 us
    ppermute x13, starting transfers between devices, swap(): return lax.ppermute(x, 'core', shift(2, 1))  16.7 us
    pallas_call x3, Pallas kernels, acts(): pl.pallas_call(functools.partial(acts_kernel, rows_of, skip, last, keep,...  15.5 us
    ppermute x13, starting transfers between devices, along(): return lax.ppermute(x, 'z', shift(4, k))  14.4 us
    pallas_call x1, Pallas kernels, squares(): pl.pallas_call(squares_kernel, in_specs=[VMEM] * 8, out_specs=(VMEM,) * 3...  9.82 us
    pallas_call x1, Pallas kernels, final(): pl.pallas_call(functools.partial(final_kernel, entries, plan, copies, sum...  9.12 us
    pallas_call x1, Pallas kernels, early_products(): pl.pallas_call(functools.partial(early_kernel, copies, missing), in_specs...  8.58 us
  transfers between devices with their start and end apart: 28, of which 11 were waited for; matrix products, arithmetic and copies ran while one was open for 2% of the time, Pallas kernels for 24%

profile of v3, /device:TPU:1, one launch (start us, length us, event | category | flops | bytes accessed | tf_op | source)
XLA Modules:
  0.0 151.9 jit_solution(16066198841576093490)
XLA Ops:
  0.0 3.7 %dispatch.2 = bf16[128,5376]{1,0:T(8,128)(2,1)} custom-call(s32[8,128]{1,0:T(8,128)} %bitcast.21, f32[8,128]{1,0:T(8,128)} %bitcast.23, s32[384]{0:T(512)} %refs_2_.2, bf16[128,7168]{1,0:T(8,128)(2,1)} %refs_3_.3, bf16[128,7168]{1,0:T(8,128)(2,1)} %refs_4_.3), custom_call_target="tpu_custom_call" | custom-call | flops 704643072 | bytes 4128768 | tf_op jit(solution)/shard_map/dispatch/pallas_call | solution.py:88
  3.7 7.6 %all-to-all-start = ((bf16[16,8,5376]{2,1,0:T(8,128)(2,1)}), bf16[16,8,5376]{2,1,0:T(8,128)(2,1)S(1)}, u32[]{:S(2)}, u32[]{:S(2)}) async-start(bf16[16,8,5376]{2,1,0:T(8,128)(2,1)} %bitcast.2), calls=%async_computation | async-start | bytes 2752512 | tf_op jit(solution)/shard_map/all_to_all | solution.py:533
  11.3 1.6 %dispatch.3 = bf16[128,1792]{1,0:T(8,128)(2,1)S(1)} custom-call(s32[8,128]{1,0:T(8,128)} %bitcast.22, f32[8,128]{1,0:T(8,128)} %bitcast.24, s32[384]{0:T(512)} %refs_2_.2, bf16[128,7168]{1,0:T(8,128)(2,1)} %refs_3_.3, bf16[128,7168]{1,0:T(8,128)(2,1)} %refs_4_.3), custom_call_target="tpu_custom_call" | custom-call | flops 234881024 | bytes 1376256 | tf_op jit(solution)/shard_map/dispatch/pallas_call | solution.py:88
  12.9 3.8 %collective-permute-start.1 = (bf16[128,1792]{1,0:T(8,128)(2,1)S(1)}, bf16[128,1792]{1,0:T(8,128)(2,1)S(1)}, u32[]{:S(2)}, u32[]{:S(2)}) collective-permute-start(bf16[128,1792]{1,0:T(8,128)(2,1)S(1)} %dispatch.3), channel_id=1, source_target_pairs={{0,6},{2,0},{4,2},{6,4},{1,7},{3,1},{5,3},{7,5},{8,14},{10,8},{12,... | collective-permute-start | bytes 1376264 | tf_op jit(solution)/shard_map/ppermute | solution.py:140
  16.8 8.9 %collective-permute-done.1 = bf16[128,1792]{1,0:T(8,128)(2,1)S(1)} collective-permute-done((bf16[128,1792]{1,0:T(8,128)(2,1)S(1)}, bf16[128,1792]{1,0:T(8,128)(2,1)S(1)}, u32[]{:S(2)}, u32[]{:S(2)}) %collective-permute-start.1) | collective-permute-done | bytes 458784 | tf_op jit(solution)/shard_map/ppermute | solution.py:140
  25.7 3.5 %collective-permute-start.3 = (bf16[64,1792]{1,0:T(8,128)(2,1)S(1)}, bf16[64,1792]{1,0:T(8,128)(2,1)S(1)}, u32[]{:S(2)}, u32[]{:S(2)}) collective-permute-start(bf16[64,1792]{1,0:T(8,128)(2,1)S(1)} %slice.25), channel_id=1, source_target_pairs={{0,6},{2,0},{4,2},{6,4},{1,7},{3,1},{5,3},{7,5},{8,14},{10,8},{12,... | collective-permute-start | bytes 688136 | tf_op jit(solution)/shard_map/ppermute | solution.py:140
  29.2 0.7 copy-done.4
  29.9 2.2 %collective-permute-done.3 = bf16[64,1792]{1,0:T(8,128)(2,1)S(1)} collective-permute-done((bf16[64,1792]{1,0:T(8,128)(2,1)S(1)}, bf16[64,1792]{1,0:T(8,128)(2,1)S(1)}, u32[]{:S(2)}, u32[]{:S(2)}) %collective-permute-start.3) | collective-permute-done | bytes 229408 | tf_op jit(solution)/shard_map/ppermute | solution.py:140
  32.1 3.9 %collective-permute-done.2 = bf16[64,1792]{1,0:T(8,128)(2,1)S(1)} collective-permute-done((bf16[64,1792]{1,0:T(8,128)(2,1)S(1)}, bf16[64,1792]{1,0:T(8,128)(2,1)S(1)}, u32[]{:S(2)}, u32[]{:S(2)}) %collective-permute-start.2) | collective-permute-done | bytes 229408 | tf_op jit(solution)/shard_map/ppermute | solution.py:140
  36.0 0.8 maximum_bitcast_fusion
  36.8 0.5 split_rows.2.refs_0_
  37.3 0.5 copy-done.1
  37.8 0.1 copy-done.3
  38.0 0.1 copy-done.5
  38.1 1.4 pad_maximum_fusion
  39.5 6.4 %all-to-all-start.1 = ((bf16[16,32,1792]{2,1,0:T(8,128)(2,1)}), bf16[16,32,1792]{2,1,0:T(8,128)(2,1)S(1)}, u32[]{:S(2)}, u32[]{:S(2)}) async-start(bf16[16,32,1792]{2,1,0:T(8,128)(2,1)} %pad_maximum_fusion), calls=%async_computation.1 | async-start | bytes 3670016 | tf_op jit(solution)/shard_map/all_to_all | solution.py:541
  46.0 1.5 collective-permute-start.5
  47.4 20.6 %all-to-all-done.1.in_ref = bf16[16,32,1792]{2,1,0:T(8,128)(2,1)S(1)} async-done(((bf16[16,32,1792]{2,1,0:T(8,128)(2,1)}), bf16[16,32,1792]{2,1,0:T(8,128)(2,1)S(1)}, u32[]{:S(2)}, u32[]{:S(2)}) %all-to-all-start.1) | async-done | bytes 1835040 | tf_op jit(solution)/shard_map/all_to_all | solution.py:541
  68.0 0.6 split_rows.3.refs_0_
  68.6 6.4 %collective-permute-start.4 = (bf16[512,1792]{1,0:T(8,128)(2,1)S(1)}, bf16[512,1792]{1,0:T(8,128)(2,1)S(1)}, u32[]{:S(2)}, u32[]{:S(2)}) collective-permute-start(bf16[512,1792]{1,0:T(8,128)(2,1)S(1)} %split_rows.3.refs_0_), channel_id=1, source_target_pairs={{0,1},{1,0},{2,3},{3,2},{4,5},{5,4},{6,7},{7,6},{8,9},{9,8},{10,11... | collective-permute-start | bytes 5505032 | tf_op jit(solution)/shard_map/ppermute | solution.py:144
  75.1 0.1 collective-permute-start.7
  75.2 3.5 %collective-permute-start.9 = (bf16[128,5376]{1,0:T(8,128)(2,1)}, bf16[128,5376]{1,0:T(8,128)(2,1)S(1)}, u32[]{:S(2)}, u32[]{:S(2)}) collective-permute-start(bf16[128,5376]{1,0:T(8,128)(2,1)} %collective-permute-done.6.refs_2_), channel_id=1, source_target_pairs={{0,1},{1,0},{2,3},{3,2},{4,5},{5,4},{6,7},{7,6},{8,9},{9,8},{10,11... | collective-permute-start | bytes 4128776 | tf_op jit(solution)/shard_map/ppermute | solution.py:144
  78.7 1.3 collective-permute-start.8
  80.0 1.1 slice.27
  81.2 1.1 slice.26
  82.4 1.7 %collective-permute-start.10 = (bf16[64,5376]{1,0:T(8,128)(2,1)S(1)}, bf16[64,5376]{1,0:T(8,128)(2,1)S(1)}, u32[]{:S(2)}, u32[]{:S(2)}) collective-permute-start(bf16[64,5376]{1,0:T(8,128)(2,1)S(1)} %slice.26), channel_id=1, source_target_pairs={{0,2},{2,4},{4,6},{6,0},{1,3},{3,5},{5,7},{7,1},{8,10},{10,12},{12... | collective-permute-start | bytes 2064392 | tf_op jit(solution)/shard_map/ppermute | solution.py:140
  84.1 3.6 %acts.3 = (f32[3,512,256]{2,1,0:T(8,128)S(1)}, bf16[512,1792]{1,0:T(8,128)(2,1)S(1)}, bf16[512,1792]{1,0:T(8,128)(2,1)S(1)}) custom-call(bf16[512,1792]{1,0:T(8,128)(2,1)S(1)} %split_rows.3.refs_0_, bf16[512,1792]{1,0:T(8,128)(2,1)S(1)} %collective-permute-done.4.refs_1_, bf16[7168,256]{1,0:T(8,128)(2,1)} %bitcast.13, bf16[7168,256]{1,0:T(8,128)(2,1)} %bitcast.15, ...), custom_call_target="tpu_custom_call" | custom-call | flops 1409286144 | bytes 6422528 | tf_op jit(solution)/shard_map/acts/pallas_call | solution.py:290
  87.7 8.2 %acts.4 = (bf16[384,768]{1,0:T(8,128)(2,1)S(1)}, bf16[384,5376]{1,0:T(8,128)(2,1)S(1)}, bf16[384,5376]{1,0:T(8,128)(2,1)S(1)}, bf16[5376,256]{1,0:T(8,128)(2,1)S...) custom-call(bf16[128,5376]{1,0:T(8,128)(2,1)} %copy-done, ...), custom_call_target="tpu_custom_call" | custom-call | flops 3170893824 | bytes 16515072 | tf_op jit(solution)/shard_map/acts/pallas_call | solution.py:290
  95.9 2.4 %collective-permute-done.11.refs_1_ = bf16[64,5376]{1,0:T(8,128)(2,1)S(1)} collective-permute-done((bf16[64,5376]{1,0:T(8,128)(2,1)S(1)}, bf16[64,5376]{1,0:T(8,128)(2,1)S(1)}, u32[]{:S(2)}, u32[]{:S(2)}) %collective-permute-start.11) | collective-permute-done | bytes 688160 | tf_op jit(solution)/shard_map/ppermute | solution.py:140
  98.3 1.8 %collective-permute-done.10.refs_0_ = bf16[64,5376]{1,0:T(8,128)(2,1)S(1)} collective-permute-done((bf16[64,5376]{1,0:T(8,128)(2,1)S(1)}, bf16[64,5376]{1,0:T(8,128)(2,1)S(1)}, u32[]{:S(2)}, u32[]{:S(2)}) %collective-permute-start.10) | collective-permute-done | bytes 688160 | tf_op jit(solution)/shard_map/ppermute | solution.py:140
  100.1 1.6 %collective-permute-start.12 = (bf16[64,5376]{1,0:T(8,128)(2,1)S(1)}, bf16[64,5376]{1,0:T(8,128)(2,1)S(1)}, u32[]{:S(2)}, u32[]{:S(2)}) collective-permute-start(bf16[64,5376]{1,0:T(8,128)(2,1)S(1)} %collective-permute-done.10.refs_0_), channel_id=1, source_target_pairs={{0,1},{1,0},{2,3},{3,2},{4,5},{5,4},{6,7},{7,6},{8,9},{9,8},{10,11... | collective-permute-start | bytes 2064392 | tf_op jit(solution)/shard_map/ppermute | solution.py:144
  101.7 0.5 collective-permute-start.20
  102.2 1.5 collective-permute-start.15
  103.6 0.8 collective-permute-done.13.refs_3_
  104.4 3.7 %acts.5 = (bf16[128,768]{1,0:T(8,128)(2,1)S(1)}, bf16[128,5376]{1,0:T(8,128)(2,1)S(1)}, bf16[128,5376]{1,0:T(8,128)(2,1)S(1)}) custom-call(bf16[64,5376]{1,0:T(8,128)(2,1)S(1)} %collective-permute-done.10.refs_0_, bf16[64,5376]{1,0:T(8,128)(2,1)S(1)} %collective-permute-done.11.refs_1_, bf16[64,5376]{1,0:T(8,128)(2,1)S(1)} %collective-permute-done.12.refs_2_, ...), custom_call_target="tpu_custom_call" | custom-call | flops 1056964608 | bytes 11010048 | tf_op jit(solution)/shard_map/acts/pallas_call | solution.py:290
  108.1 9.8 %squares.1 = (bf16[144,768]{1,0:T(8,128)(2,1)S(1)}, bf16[896,512]{1,0:T(8,128)(2,1)S(1)}, bf16[896,512]{1,0:T(8,128)(2,1)S(1)}) custom-call(bf16[512,1792]{1,0:T(8,128)(2,1)S(1)} %get-tuple-element.37.x0, bf16[512,1792]{1,0:T(8,128)(2,1)S(1)} %get-tuple-element.38.g0, bf16[384,5376]{1,0:T(8,128)(2,1)S(1)} %get-tuple-element.40.xa, ...), custom_call_target="tpu_custom_call" | custom-call | flops 5637144576 | bytes 14680064 | tf_op jit(solution)/shard_map/squares/pallas_call | solution.py:356
  118.0 0.4 collective-permute-done.15.refs_1_
  118.4 0.8 collective-permute-start.21
  119.1 0.5 collective-permute-start.14
  119.9 1.4 collective-permute-start.17
  121.3 0.6 collective-permute-done.14.refs_7_.refs_1_
  121.9 0.8 collective-permute-start.19
  122.7 8.6 %early_products.1.refs_8_ = f32[6,3,896,256]{3,2,1,0:T(8,128)S(1)} custom-call(bf16[384,768]{1,0:T(8,128)(2,1)S(1)} %get-tuple-element.42.hid_a.refs_0_, bf16[384,768]{1,0:T(8,128)(2,1)S(1)} %collective-permute-done.15.refs_1_, bf16[384,768]{1,0:T(8,128)(2,1)S(1)} %collective-permute-done.16.refs_2_, bf16[384,768]{1,0:T(8,128)(2,1)S(1)} %collective-permute-done.20.refs_3_, ...), custom_call_target="tpu_custom_call" | custom-call | flops 4227858432 | bytes 4718592 | tf_op jit(solution)/shard_map/early_products/pallas_call | solution.py:407
  131.3 7.2 %collective-permute-done.19.refs_4_ = bf16[144,768]{1,0:T(8,128)(2,1)S(1)} collective-permute-done((bf16[144,768]{1,0:T(8,128)(2,1)S(1)}, bf16[144,768]{1,0:T(8,128)(2,1)S(1)}, u32[]{:S(2)}, u32[]{:S(2)}) %collective-permute-start.19) | collective-permute-done | bytes 221216 | tf_op jit(solution)/shard_map/ppermute | solution.py:140
  138.5 1.5 %collective-permute-start.23 = (bf16[336,768]{1,0:T(8,128)(2,1)S(1)}, bf16[336,768]{1,0:T(8,128)(2,1)S(1)}, u32[]{:S(2)}, u32[]{:S(2)}) collective-permute-start(bf16[336,768]{1,0:T(8,128)(2,1)S(1)} %collective-permute-done.17.refs_2_), channel_id=1, source_target_pairs={{0,1},{1,0},{2,3},{3,2},{4,5},{5,4},{6,7},{7,6},{8,9},{9,8},{10,11... | collective-permute-start | bytes 1548296 | tf_op jit(solution)/shard_map/ppermute | solution.py:144
  140.1 0.5 collective-permute-start.25
  140.6 2.1 %collective-permute-done.25.refs_7_ = bf16[144,768]{1,0:T(8,128)(2,1)S(1)} collective-permute-done((bf16[144,768]{1,0:T(8,128)(2,1)S(1)}, bf16[144,768]{1,0:T(8,128)(2,1)S(1)}, u32[]{:S(2)}, u32[]{:S(2)}) %collective-permute-start.25) | collective-permute-done | bytes 221216 | tf_op jit(solution)/shard_map/ppermute | solution.py:144
  142.6 9.1 %final.1 = bf16[3,896,2048]{2,1,0:T(8,128)(2,1)} custom-call(bf16[144,768]{1,0:T(8,128)(2,1)S(1)} %get-tuple-element.51.refs_6_.refs_0_, bf16[144,768]{1,0:T(8,128)(2,1)S(1)} %collective-permute-done.14.refs_7_.refs_1_, bf16[336,768]{1,0:T(8,128)(2,1)S(1)} %collective-permute-done.17.refs_2_, bf16[336,768]{1,0:T(8,128)(2,1)S(1)} %collective-permute-done.18.refs_3_, ...), custom_call_target="tpu_custom_call" | custom-call | flops 2818572288 | bytes 22020096 | tf_op jit(solution)/shard_map/final/pallas_call | solution.py:476
  (39 shorter events, 0.4 us)
Async XLA Ops:
  3.7 33.1 %all-to-all-start = ((bf16[16,8,5376]{2,1,0:T(8,128)(2,1)}), bf16[16,8,5376]{2,1,0:T(8,128)(2,1)S(1)}, u32[]{:S(2)}, u32[]{:S(2)}) async-start(bf16[16,8,5376]{2,1,0:T(8,128)(2,1)} %bitcast.2), calls=%async_computation | async-start | bytes 2752512 | tf_op jit(solution)/shard_map/all_to_all | solution.py:533
  12.9 12.7 %collective-permute-start.1 = (bf16[128,1792]{1,0:T(8,128)(2,1)S(1)}, bf16[128,1792]{1,0:T(8,128)(2,1)S(1)}, u32[]{:S(2)}, u32[]{:S(2)}) collective-permute-start(bf16[128,1792]{1,0:T(8,128)(2,1)S(1)} %dispatch.3), channel_id=1, source_target_pairs={{0,6},{2,0},{4,2},{6,4},{1,7},{3,1},{5,3},{7,5},{8,14},{10,8},{12,... | collective-permute-start | bytes 1376264 | tf_op jit(solution)/shard_map/ppermute | solution.py:140
  16.8 12.4 %collective-permute-start = (bf16[128,1792]{1,0:T(8,128)(2,1)S(1)}, bf16[128,1792]{1,0:T(8,128)(2,1)S(1)}, u32[]{:S(2)}, u32[]{:S(2)}) collective-permute-start(bf16[128,1792]{1,0:T(8,128)(2,1)S(1)} %dispatch.3), channel_id=1, source_target_pairs={{0,2},{2,4},{4,6},{6,0},{1,3},{3,5},{5,7},{7,1},{8,10},{10,12},{12... | collective-permute-start | bytes 1376264 | tf_op jit(solution)/shard_map/ppermute | solution.py:140
  25.6 3.5 %copy-start.2 = (bf16[128,1792]{1,0:T(8,128)(2,1)}, bf16[128,1792]{1,0:T(8,128)(2,1)S(1)}, u32[]{:S(2)}) copy-start(bf16[128,1792]{1,0:T(8,128)(2,1)S(1)} %collective-permute-done.1) | copy-start | bytes 1376260
  25.7 6.4 %collective-permute-start.3 = (bf16[64,1792]{1,0:T(8,128)(2,1)S(1)}, bf16[64,1792]{1,0:T(8,128)(2,1)S(1)}, u32[]{:S(2)}, u32[]{:S(2)}) collective-permute-start(bf16[64,1792]{1,0:T(8,128)(2,1)S(1)} %slice.25), channel_id=1, source_target_pairs={{0,6},{2,0},{4,2},{6,4},{1,7},{3,1},{5,3},{7,5},{8,14},{10,8},{12,... | collective-permute-start | bytes 688136 | tf_op jit(solution)/shard_map/ppermute | solution.py:140
  29.1 0.8 copy-start.4
  29.9 6.1 %collective-permute-start.2 = (bf16[64,1792]{1,0:T(8,128)(2,1)S(1)}, bf16[64,1792]{1,0:T(8,128)(2,1)S(1)}, u32[]{:S(2)}, u32[]{:S(2)}) collective-permute-start(bf16[64,1792]{1,0:T(8,128)(2,1)S(1)} %slice.24), channel_id=1, source_target_pairs={{0,2},{2,4},{4,6},{6,0},{1,3},{3,5},{5,7},{7,1},{8,10},{10,12},{12... | collective-permute-start | bytes 688136 | tf_op jit(solution)/shard_map/ppermute | solution.py:140
  36.8 1.0 copy-start.1
  36.8 1.2 copy-start.3
  36.8 1.3 copy-start.5
  37.3 37.7 %copy-start = (bf16[128,5376]{1,0:T(8,128)(2,1)}, bf16[128,5376]{1,0:T(8,128)(2,1)S(1)}, u32[]{:S(2)}) copy-start(bf16[128,5376]{1,0:T(8,128)(2,1)S(1)} %split_rows.2.refs_0_) | copy-start | bytes 4128772
  39.5 28.5 %all-to-all-start.1 = ((bf16[16,32,1792]{2,1,0:T(8,128)(2,1)}), bf16[16,32,1792]{2,1,0:T(8,128)(2,1)S(1)}, u32[]{:S(2)}, u32[]{:S(2)}) async-start(bf16[16,32,1792]{2,1,0:T(8,128)(2,1)} %pad_maximum_fusion), calls=%async_computation.1 | async-start | bytes 3670016 | tf_op jit(solution)/shard_map/all_to_all | solution.py:541
  45.9 29.3 %collective-permute-start.6 = (bf16[128,5376]{1,0:T(8,128)(2,1)S(1)}, bf16[128,5376]{1,0:T(8,128)(2,1)}, u32[]{:S(2)}, u32[]{:S(2)}) collective-permute-start(bf16[128,5376]{1,0:T(8,128)(2,1)S(1)} %split_rows.2.refs_0_), channel_id=1, source_target_pairs={{0,6},{2,0},{4,2},{6,4},{1,7},{3,1},{5,3},{7,5},{8,14},{10,8},{12,... | collective-permute-start | bytes 4128776 | tf_op jit(solution)/shard_map/ppermute | solution.py:140
  46.0 32.7 %collective-permute-start.5 = (bf16[128,5376]{1,0:T(8,128)(2,1)S(1)}, bf16[128,5376]{1,0:T(8,128)(2,1)}, u32[]{:S(2)}, u32[]{:S(2)}) collective-permute-start(bf16[128,5376]{1,0:T(8,128)(2,1)S(1)} %split_rows.2.refs_0_), channel_id=1, source_target_pairs={{0,2},{2,4},{4,6},{6,0},{1,3},{3,5},{5,7},{7,1},{8,10},{10,12},{12... | collective-permute-start | bytes 4128776 | tf_op jit(solution)/shard_map/ppermute | solution.py:140
  68.6 13.7 %collective-permute-start.4 = (bf16[512,1792]{1,0:T(8,128)(2,1)S(1)}, bf16[512,1792]{1,0:T(8,128)(2,1)S(1)}, u32[]{:S(2)}, u32[]{:S(2)}) collective-permute-start(bf16[512,1792]{1,0:T(8,128)(2,1)S(1)} %split_rows.3.refs_0_), channel_id=1, source_target_pairs={{0,1},{1,0},{2,3},{3,2},{4,5},{5,4},{6,7},{7,6},{8,9},{9,8},{10,11... | collective-permute-start | bytes 5505032 | tf_op jit(solution)/shard_map/ppermute | solution.py:144
  75.1 12.6 %collective-permute-start.7 = (bf16[128,5376]{1,0:T(8,128)(2,1)S(1)}, bf16[128,5376]{1,0:T(8,128)(2,1)S(1)}, u32[]{:S(2)}, u32[]{:S(2)}) collective-permute-start(bf16[128,5376]{1,0:T(8,128)(2,1)S(1)} %split_rows.2.refs_0_), channel_id=1, source_target_pairs={{0,1},{1,0},{2,3},{3,2},{4,5},{5,4},{6,7},{7,6},{8,9},{9,8},{10,11... | collective-permute-start | bytes 4128776 | tf_op jit(solution)/shard_map/ppermute | solution.py:144
  75.2 12.5 %collective-permute-start.9 = (bf16[128,5376]{1,0:T(8,128)(2,1)}, bf16[128,5376]{1,0:T(8,128)(2,1)S(1)}, u32[]{:S(2)}, u32[]{:S(2)}) collective-permute-start(bf16[128,5376]{1,0:T(8,128)(2,1)} %collective-permute-done.6.refs_2_), channel_id=1, source_target_pairs={{0,1},{1,0},{2,3},{3,2},{4,5},{5,4},{6,7},{7,6},{8,9},{9,8},{10,11... | collective-permute-start | bytes 4128776 | tf_op jit(solution)/shard_map/ppermute | solution.py:144
  78.7 9.0 %collective-permute-start.8 = (bf16[128,5376]{1,0:T(8,128)(2,1)}, bf16[128,5376]{1,0:T(8,128)(2,1)S(1)}, u32[]{:S(2)}, u32[]{:S(2)}) collective-permute-start(bf16[128,5376]{1,0:T(8,128)(2,1)} %collective-permute-done.5.refs_1_), channel_id=1, source_target_pairs={{0,1},{1,0},{2,3},{3,2},{4,5},{5,4},{6,7},{7,6},{8,9},{9,8},{10,11... | collective-permute-start | bytes 4128776 | tf_op jit(solution)/shard_map/ppermute | solution.py:144
  81.1 17.1 %collective-permute-start.11 = (bf16[64,5376]{1,0:T(8,128)(2,1)S(1)}, bf16[64,5376]{1,0:T(8,128)(2,1)S(1)}, u32[]{:S(2)}, u32[]{:S(2)}) collective-permute-start(bf16[64,5376]{1,0:T(8,128)(2,1)S(1)} %slice.27), channel_id=1, source_target_pairs={{0,6},{2,0},{4,2},{6,4},{1,7},{3,1},{5,3},{7,5},{8,14},{10,8},{12,... | collective-permute-start | bytes 2064392 | tf_op jit(solution)/shard_map/ppermute | solution.py:140
  82.4 17.7 %collective-permute-start.10 = (bf16[64,5376]{1,0:T(8,128)(2,1)S(1)}, bf16[64,5376]{1,0:T(8,128)(2,1)S(1)}, u32[]{:S(2)}, u32[]{:S(2)}) collective-permute-start(bf16[64,5376]{1,0:T(8,128)(2,1)S(1)} %slice.26), channel_id=1, source_target_pairs={{0,2},{2,4},{4,6},{6,0},{1,3},{3,5},{5,7},{7,1},{8,10},{10,12},{12... | collective-permute-start | bytes 2064392 | tf_op jit(solution)/shard_map/ppermute | solution.py:140
  100.1 3.6 %collective-permute-start.12 = (bf16[64,5376]{1,0:T(8,128)(2,1)S(1)}, bf16[64,5376]{1,0:T(8,128)(2,1)S(1)}, u32[]{:S(2)}, u32[]{:S(2)}) collective-permute-start(bf16[64,5376]{1,0:T(8,128)(2,1)S(1)} %collective-permute-done.10.refs_0_), channel_id=1, source_target_pairs={{0,1},{1,0},{2,3},{3,2},{4,5},{5,4},{6,7},{7,6},{8,9},{9,8},{10,11... | collective-permute-start | bytes 2064392 | tf_op jit(solution)/shard_map/ppermute | solution.py:144
  101.7 2.8 %collective-permute-start.13 = (bf16[64,5376]{1,0:T(8,128)(2,1)S(1)}, bf16[64,5376]{1,0:T(8,128)(2,1)S(1)}, u32[]{:S(2)}, u32[]{:S(2)}) collective-permute-start(bf16[64,5376]{1,0:T(8,128)(2,1)S(1)} %collective-permute-done.11.refs_1_), channel_id=1, source_target_pairs={{0,1},{1,0},{2,3},{3,2},{4,5},{5,4},{6,7},{7,6},{8,9},{9,8},{10,11... | collective-permute-start | bytes 2064392 | tf_op jit(solution)/shard_map/ppermute | solution.py:144
  101.7 18.2 %collective-permute-start.20 = (bf16[384,768]{1,0:T(8,128)(2,1)S(1)}, bf16[384,768]{1,0:T(8,128)(2,1)S(1)}, u32[]{:S(2)}, u32[]{:S(2)}) collective-permute-start(bf16[384,768]{1,0:T(8,128)(2,1)S(1)} %get-tuple-element.42.hid_a.refs_0_), channel_id=1, source_target_pairs={{0,1},{1,0},{2,3},{3,2},{4,5},{5,4},{6,7},{7,6},{8,9},{9,8},{10,11... | collective-permute-start | bytes 1769480 | tf_op jit(solution)/shard_map/ppermute | solution.py:144
  102.2 15.8 %collective-permute-start.16 = (bf16[384,768]{1,0:T(8,128)(2,1)S(1)}, bf16[384,768]{1,0:T(8,128)(2,1)S(1)}, u32[]{:S(2)}, u32[]{:S(2)}) collective-permute-start(bf16[384,768]{1,0:T(8,128)(2,1)S(1)} %get-tuple-element.42.hid_a.refs_0_), channel_id=1, source_target_pairs={{0,6},{2,0},{4,2},{6,4},{1,7},{3,1},{5,3},{7,5},{8,14},{10,8},{12,... | collective-permute-start | bytes 1769480 | tf_op jit(solution)/shard_map/ppermute | solution.py:140
  102.2 16.2 %collective-permute-start.15 = (bf16[384,768]{1,0:T(8,128)(2,1)S(1)}, bf16[384,768]{1,0:T(8,128)(2,1)S(1)}, u32[]{:S(2)}, u32[]{:S(2)}) collective-permute-start(bf16[384,768]{1,0:T(8,128)(2,1)S(1)} %get-tuple-element.42.hid_a.refs_0_), channel_id=1, source_target_pairs={{0,2},{2,4},{4,6},{6,0},{1,3},{3,5},{5,7},{7,1},{8,10},{10,12},{12... | collective-permute-start | bytes 1769480 | tf_op jit(solution)/shard_map/ppermute | solution.py:140
  118.4 4.4 %collective-permute-start.21 = (bf16[384,768]{1,0:T(8,128)(2,1)S(1)}, bf16[384,768]{1,0:T(8,128)(2,1)S(1)}, u32[]{:S(2)}, u32[]{:S(2)}) collective-permute-start(bf16[384,768]{1,0:T(8,128)(2,1)S(1)} %collective-permute-done.15.refs_1_), channel_id=1, source_target_pairs={{0,1},{1,0},{2,3},{3,2},{4,5},{5,4},{6,7},{7,6},{8,9},{9,8},{10,11... | collective-permute-start | bytes 1769480 | tf_op jit(solution)/shard_map/ppermute | solution.py:144
  119.1 3.6 %collective-permute-start.22 = (bf16[384,768]{1,0:T(8,128)(2,1)S(1)}, bf16[384,768]{1,0:T(8,128)(2,1)S(1)}, u32[]{:S(2)}, u32[]{:S(2)}) collective-permute-start(bf16[384,768]{1,0:T(8,128)(2,1)S(1)} %collective-permute-done.16.refs_2_), channel_id=1, source_target_pairs={{0,1},{1,0},{2,3},{3,2},{4,5},{5,4},{6,7},{7,6},{8,9},{9,8},{10,11... | collective-permute-start | bytes 1769480 | tf_op jit(solution)/shard_map/ppermute | solution.py:144
  119.1 2.8 %collective-permute-start.14 = (bf16[144,768]{1,0:T(8,128)(2,1)S(1)}, bf16[144,768]{1,0:T(8,128)(2,1)S(1)}, u32[]{:S(2)}, u32[]{:S(2)}) collective-permute-start(bf16[144,768]{1,0:T(8,128)(2,1)S(1)} %get-tuple-element.51.refs_6_.refs_0_), channel_id=1, source_target_pairs={{0,1},{1,0},{2,3},{3,2},{4,5},{5,4},{6,7},{7,6},{8,9},{9,8},{10,11... | collective-permute-start | bytes 663560 | tf_op jit(solution)/shard_map/ppermute | solution.py:144
  119.8 18.7 %collective-permute-start.18 = (bf16[336,768]{1,0:T(8,128)(2,1)S(1)}, bf16[336,768]{1,0:T(8,128)(2,1)S(1)}, u32[]{:S(2)}, u32[]{:S(2)}) collective-permute-start(bf16[336,768]{1,0:T(8,128)(2,1)S(1)} %get-tuple-element.59), channel_id=1, source_target_pairs={{0,6},{2,0},{4,2},{6,4},{1,7},{3,1},{5,3},{7,5},{8,14},{10,8},{12,... | collective-permute-start | bytes 1548296 | tf_op jit(solution)/shard_map/ppermute | solution.py:140
  119.9 18.6 %collective-permute-start.17 = (bf16[336,768]{1,0:T(8,128)(2,1)S(1)}, bf16[336,768]{1,0:T(8,128)(2,1)S(1)}, u32[]{:S(2)}, u32[]{:S(2)}) collective-permute-start(bf16[336,768]{1,0:T(8,128)(2,1)S(1)} %get-tuple-element.60), channel_id=1, source_target_pairs={{0,2},{2,4},{4,6},{6,0},{1,3},{3,5},{5,7},{7,1},{8,10},{10,12},{12... | collective-permute-start | bytes 1548296 | tf_op jit(solution)/shard_map/ppermute | solution.py:140
  121.9 16.6 %collective-permute-start.19 = (bf16[144,768]{1,0:T(8,128)(2,1)S(1)}, bf16[144,768]{1,0:T(8,128)(2,1)S(1)}, u32[]{:S(2)}, u32[]{:S(2)}) collective-permute-start(bf16[144,768]{1,0:T(8,128)(2,1)S(1)} %get-tuple-element.51.refs_6_.refs_0_), channel_id=1, source_target_pairs={{0,4},{2,6},{4,0},{6,2},{1,5},{3,7},{5,1},{7,3},{8,12},{10,14},{12... | collective-permute-start | bytes 663560 | tf_op jit(solution)/shard_map/ppermute | solution.py:140
  138.5 4.1 %collective-permute-start.23 = (bf16[336,768]{1,0:T(8,128)(2,1)S(1)}, bf16[336,768]{1,0:T(8,128)(2,1)S(1)}, u32[]{:S(2)}, u32[]{:S(2)}) collective-permute-start(bf16[336,768]{1,0:T(8,128)(2,1)S(1)} %collective-permute-done.17.refs_2_), channel_id=1, source_target_pairs={{0,1},{1,0},{2,3},{3,2},{4,5},{5,4},{6,7},{7,6},{8,9},{9,8},{10,11... | collective-permute-start | bytes 1548296 | tf_op jit(solution)/shard_map/ppermute | solution.py:144
  140.1 2.6 %collective-permute-start.24 = (bf16[336,768]{1,0:T(8,128)(2,1)S(1)}, bf16[336,768]{1,0:T(8,128)(2,1)S(1)}, u32[]{:S(2)}, u32[]{:S(2)}) collective-permute-start(bf16[336,768]{1,0:T(8,128)(2,1)S(1)} %collective-permute-done.18.refs_3_), channel_id=1, source_target_pairs={{0,1},{1,0},{2,3},{3,2},{4,5},{5,4},{6,7},{7,6},{8,9},{9,8},{10,11... | collective-permute-start | bytes 1548296 | tf_op jit(solution)/shard_map/ppermute | solution.py:144
  140.1 2.6 %collective-permute-start.25 = (bf16[144,768]{1,0:T(8,128)(2,1)S(1)}, bf16[144,768]{1,0:T(8,128)(2,1)S(1)}, u32[]{:S(2)}, u32[]{:S(2)}) collective-permute-start(bf16[144,768]{1,0:T(8,128)(2,1)S(1)} %collective-permute-done.19.refs_4_), channel_id=1, source_target_pairs={{0,1},{1,0},{2,3},{3,2},{4,5},{5,4},{6,7},{7,6},{8,9},{9,8},{10,11... | collective-permute-start | bytes 663560 | tf_op jit(solution)/shard_map/ppermute | solution.py:144

commit v4 on v3

--- a/solution.py
+++ b/solution.py
@@ -132,6 +132,29 @@
     )(block)
 
 
+def pack_kernel(*refs):
+    blocks, first, second, out = refs[:-3], refs[-3], refs[-2], refs[-1]
+    hot, _, width = out.shape
+    per = 2 * CAP
+    for i, ref in enumerate(blocks):
+        out[:, i * per : (i + 1) * per, :] = ref[...].reshape(hot, per, width)
+    at = len(blocks) * per
+    out[: hot // 2, at:, :] = first[...].reshape(hot // 2, per, width)
+    out[hot // 2 :, at:, :] = second[...].reshape(hot // 2, per, width)
+
+
+def pack(blocks, first, second, hot):
+    per, width = 2 * CAP, first.shape[1]
+    return pl.pallas_call(
+        pack_kernel,
+        in_specs=[VMEM] * (len(blocks) + 2),
+        out_specs=VMEM,
+        out_shape=jax.ShapeDtypeStruct((hot, (len(blocks) + 1) * per, width), BF16),
+        compiler_params=params(16),
+        name="pack",
+    )(*blocks, first, second)
+
+
 def shift(n, k):
     return [(i, (i + k) % n) for i in range(n)]
 
@@ -423,19 +446,11 @@
     )(*arrays, xt, gt)
 
 
-def final_kernel(entries, plan, copies, sums, *refs):
-    arrays, refs = refs[:-9], refs[-9:]
-    pre_ref, xt_ref, gt_ref, out_ref, hid, coded, stage, in_sems, out_sems = refs
-    for k, (i, row) in enumerate(sums):
-        pltpu.make_async_copy(
-            arrays[i].at[pl.ds(row, 16), pl.ds(0, 128)], coded.at[k], in_sems.at[8]
-        ).start()
-    for source, _, _, rows in plan:
-        if rows is not None:
-            start_copies(copies, source, source, arrays, hid, in_sems)
-    m = hid.shape[2] // 3
-    pltpu.make_async_copy(coded, coded, in_sems.at[8]).wait()
-    pieces = jnp.sum(coded[...].astype(F32), axis=0)
+def final_kernel(entries, plan, sums, *refs):
+    arrays, refs = refs[:-6], refs[-6:]
+    pre_ref, xt_ref, gt_ref, out_ref, stage, out_sems = refs
+    m = stage.shape[3]
+    pieces = sum(arrays[i][row : row + 16, 0:128].astype(F32) for i, row in sums)
     factors = []
     for i in range(3):
         total = jnp.sum(pieces[3 * i : 3 * i + 3, :], axis=0, keepdims=True)
@@ -447,20 +462,18 @@
         return pltpu.make_async_copy(stage.at[slot], out_ref.at[:, :, at], out_sems.at[slot])
 
     slots = stage.shape[0]
-    for step, (source, early, at, rows) in enumerate(plan):
+    for step, (source, early, at, parts) in enumerate(plan):
         slot = step % slots
         if step >= slots:
             store(slot, plan[step - slots][0]).wait()
-        if rows is not None:
-            wait_rows(hid, source, rows, in_sems)
         for i in range(3):
             lhs = gt_ref if i == 2 else xt_ref
             grads = None if early is None else pre_ref[early, i]
-            if rows is not None:
+            if parts:
+                rows = [arrays[k][row : row + n, i * m : (i + 1) * m] for k, row, n in parts]
+                rows = rows[0] if len(rows) == 1 else jnp.concatenate(rows, axis=0)
                 more = jnp.dot(
-                    lhs[:, at : at + rows],
-                    hid[source, :rows, i * m : (i + 1) * m],
-                    preferred_element_type=F32,
+                    lhs[:, at : at + rows.shape[0]], rows, preferred_element_type=F32
                 )
                 grads = more if grads is None else grads + more
             stage[slot, i] = (grads * factors[i]).astype(BF16)
@@ -469,23 +482,21 @@
         store(step % slots, plan[step][0]).wait()
 
 
-def final(plan, copies, sums, arrays, pre, xt, gt, entries):
+def final(plan, sums, arrays, pre, xt, gt, entries):
     rows = xt.shape[1]
     width = arrays[0].shape[1]
     m = width // 3
+    arrays = [pltpu.with_memory_space_constraint(t, pltpu.VMEM) for t in arrays]
     return pl.pallas_call(
-        functools.partial(final_kernel, entries, plan, copies, sums),
-        in_specs=[ANY] * len(arrays) + [VMEM] * 3,
+        functools.partial(final_kernel, entries, plan, sums),
+        in_specs=[VMEM] * (len(arrays) + 3),
         out_specs=HBM,
         out_shape=jax.ShapeDtypeStruct((3, TILE, 8 * m), BF16),
         scratch_shapes=[
-            pltpu.VMEM((8, rows, width), BF16),
-            pltpu.VMEM((8, 16, 128), BF16),
             pltpu.VMEM((3, 3, TILE, m), BF16),
-            pltpu.SemaphoreType.DMA((9,)),
             pltpu.SemaphoreType.DMA((3,)),
         ],
-        compiler_params=params(20),
+        compiler_params=params(16),
         cost_estimate=pl.CostEstimate(
             flops=rows * TILE * width * 8,
             bytes_accessed=4 * TILE * width * 8,
@@ -537,9 +548,8 @@
     far = far_z(near[1], near[2], n)
     block = after(block, far)
     near = list(after(tuple(near), block))
-    four = [t.reshape(hot, 2 * CAP, early) for t in near + [jnp.concatenate(far)]]
     got = lax.all_to_all(
-        jnp.concatenate(four, axis=1), expert, split_axis=0, concat_axis=0, tiled=True
+        pack(near, far[0], far[1], hot), expert, split_axis=0, concat_axis=0, tiled=True
     )
     whole = with_other([split_rows(got, (1, 0, 2, 3))])
 
@@ -568,32 +578,32 @@
     near_a = with_other([hid_a, up_a, down_a])
 
     size = 2 * n
-    other = swap(hid_b)
     copies, missing = [], []
     for a in range(2):
         for k, z in enumerate(NEAR_Z):
             copies += placed(3 * a + k, 3 * a + k, 0, 0, 0, 3 * size, z, size)
-            missing.append(None if z == 0 else ((3 + z) % 4 * size, size))
-        copies += placed(3 * a, 6 + a, 0, 3, 0, size, 0, size)
-    pre = early_products(copies, missing, near_a + [hid_b, other], xt, gt)
-
-    last = last[1:]
-    last = [hid_b, other] + last + [swap(t) for t in after(last, pre)]
-    copies, sums, plan = [], [(0, size), (1, size)], []
+            missing.append(((3 + z) % 4 * size, size))
+    copies += placed(0, 6, 0, 3, 0, size, 0, size)
+    missing[0] = None
+    pre = early_products(copies, missing, near_a + [hid_b], xt, gt)
+
+    swapped = [swap(t) for t in after(last, pre)]
+    last = [last[0], swapped[0]] + last[1:] + swapped[1:]
+    sums, plan = [(0, size), (1, size)], []
     for a in range(2):
         up, down, far = range(2 + 3 * a, 5 + 3 * a)
-        plan.append((4 * a, 3 * a, 0, None))
-        plan.append((4 * a + 1, 3 * a + 1, 2 * size, size))
-        plan.append((4 * a + 2, 3 * a + 2, 0, size))
-        plan.append((4 * a + 3, None, 0, 4 * size))
-        copies += [(4 * a + 1, up, half, 0, size), (4 * a + 2, down, half, 0, size)]
-        copies += placed(4 * a + 3, up, 0, 0, 0, half, 2, size)
-        copies += placed(4 * a + 3, down, 0, half // size, half % size, half, 2, size)
-        copies += placed(4 * a + 3, far, 0, 3, 0, size, 2, size)
+        plan.append((4 * a, 3 * a, 3 * size, [(1, 0, size)] if a else []))
+        plan.append((4 * a + 1, 3 * a + 1, 2 * size, [(up, half, size)]))
+        plan.append((4 * a + 2, 3 * a + 2, 0, [(down, half, size)]))
+        parts = placed(0, up, 0, 0, 0, half, 2, size)
+        parts += placed(0, down, 0, half // size, half % size, half, 2, size)
+        parts += placed(0, far, 0, 3, 0, size, 2, size)
+        parts.sort(key=lambda part: part[3])
+        plan.append((4 * a + 3, None, 0, [(k, row, n) for _, k, row, _, n in parts]))
         sums += [(up, half + size), (down, half + size), (far, size)]
     plan.sort(key=lambda step: step[0] % 4)
     entries = width * weights[0].shape[1] * 8
-    return final(plan, copies, sums, last, pre, xt, gt, entries)[None]
+    return final(plan, sums, last, pre, xt, gt, entries)[None]
 
 
 def solution(mesh):

time: 152 us -> 150 us (0.987)
  other arithmetic: 2.32 us -> 0.07 us
    pallas_call x1 -> x2, Pallas kernels: 9.12 us -> 8.98 us  [the longest x1 6.69 us: final(): pl.pallas_call(functools.partial(final_kernel, entries, plan, sums), in_s...]
  transfers between devices with their start and end apart: 28 -> 28, of which waited for: 11 -> 12; matrix products, arithmetic and copies ran while one was open for 2% -> 3% of each run, Pallas kernels for 24% -> 24%
where the time goes in v4:
time: 150 us; the launch traced here: 149 us
  waiting for transfers between devices  50.6 us (34%)
  Pallas kernels  49 us (33%)
  starting transfers between devices  45.1 us (30%)
  local copies, waits for them, and re-layouts  3.96 us (3%)
    ppermute x13, waiting for transfers between devices, along(): return lax.ppermute(x, 'z', shift(4, k))  26.5 us
    all_to_all x1, waiting for transfers between devices, body(): lax.all_to_all(pack(near, far[0], far[1], hot), expert, split_axis=0, con...  20.6 us
    ppermute x13, starting transfers between devices, swap(): return lax.ppermute(x, 'core', shift(2, 1))  16.8 us
    pallas_call x3, Pallas kernels, acts(): pl.pallas_call(functools.partial(acts_kernel, rows_of, skip, last, keep,...  15.4 us
    ppermute x13, starting transfers between devices, along(): return lax.ppermute(x, 'z', shift(4, k))  14.4 us
    pallas_call x1, Pallas kernels, squares(): pl.pallas_call(squares_kernel, in_specs=[VMEM] * 8, out_specs=(VMEM,) * 3...  9.81 us
    pallas_call x1, Pallas kernels, early_products(): pl.pallas_call(functools.partial(early_kernel, copies, missing), in_specs...  8.34 us
    all_to_all x1, starting transfers between devices, body(): lax.all_to_all(sent_rest.reshape(hot, 2 * CAP, width - early), expert, sp...  7.6 us
  transfers between devices with their start and end apart: 28, of which 12 were waited for; matrix products, arithmetic and copies ran while one was open for 3% of the time, Pallas kernels for 24%

profile of v4, /device:TPU:1, one launch (start us, length us, event | category | flops | bytes accessed | tf_op | source)
XLA Modules:
  0.0 149.1 jit_solution(14790948060029048997)
XLA Ops:
  0.0 3.7 %dispatch.2 = bf16[128,5376]{1,0:T(8,128)(2,1)} custom-call(s32[8,128]{1,0:T(8,128)} %bitcast.13, f32[8,128]{1,0:T(8,128)} %bitcast.15, s32[384]{0:T(512)} %refs_2_.2, bf16[128,7168]{1,0:T(8,128)(2,1)} %refs_3_.3, bf16[128,7168]{1,0:T(8,128)(2,1)} %refs_4_.3), custom_call_target="tpu_custom_call" | custom-call | flops 704643072 | bytes 4128768 | tf_op jit(solution)/shard_map/dispatch/pallas_call | solution.py:88
  3.7 7.6 %all-to-all-start = ((bf16[16,8,5376]{2,1,0:T(8,128)(2,1)}), bf16[16,8,5376]{2,1,0:T(8,128)(2,1)S(1)}, u32[]{:S(2)}, u32[]{:S(2)}) async-start(bf16[16,8,5376]{2,1,0:T(8,128)(2,1)} %bitcast.2), calls=%async_computation | async-start | bytes 2752512 | tf_op jit(solution)/shard_map/all_to_all | solution.py:544
  11.3 1.6 %dispatch.3.refs_0_ = bf16[128,1792]{1,0:T(8,128)(2,1)S(1)} custom-call(s32[8,128]{1,0:T(8,128)} %bitcast.14, f32[8,128]{1,0:T(8,128)} %bitcast.16, s32[384]{0:T(512)} %refs_2_.2, bf16[128,7168]{1,0:T(8,128)(2,1)} %refs_3_.3, bf16[128,7168]{1,0:T(8,128)(2,1)} %refs_4_.3), custom_call_target="tpu_custom_call" | custom-call | flops 234881024 | bytes 1376256 | tf_op jit(solution)/shard_map/dispatch/pallas_call | solution.py:88
  12.9 3.8 %collective-permute-start.1 = (bf16[128,1792]{1,0:T(8,128)(2,1)S(1)}, bf16[128,1792]{1,0:T(8,128)(2,1)S(1)}, u32[]{:S(2)}, u32[]{:S(2)}) collective-permute-start(bf16[128,1792]{1,0:T(8,128)(2,1)S(1)} %dispatch.3.refs_0_), channel_id=1, source_target_pairs={{0,6},{2,0},{4,2},{6,4},{1,7},{3,1},{5,3},{7,5},{8,14},{10,8},{12,... | collective-permute-start | bytes 1376264 | tf_op jit(solution)/shard_map/ppermute | solution.py:163
  16.8 8.9 %collective-permute-done.1.refs_2_ = bf16[128,1792]{1,0:T(8,128)(2,1)S(1)} collective-permute-done((bf16[128,1792]{1,0:T(8,128)(2,1)S(1)}, bf16[128,1792]{1,0:T(8,128)(2,1)S(1)}, u32[]{:S(2)}, u32[]{:S(2)}) %collective-permute-start.1) | collective-permute-done | bytes 458784 | tf_op jit(solution)/shard_map/ppermute | solution.py:163
  25.6 0.8 slice.25
  26.4 3.4 %collective-permute-start.3 = (bf16[64,1792]{1,0:T(8,128)(2,1)}, bf16[64,1792]{1,0:T(8,128)(2,1)S(1)}, u32[]{:S(2)}, u32[]{:S(2)}) collective-permute-start(bf16[64,1792]{1,0:T(8,128)(2,1)} %slice.25), channel_id=1, source_target_pairs={{0,6},{2,0},{4,2},{6,4},{1,7},{3,1},{5,3},{7,5},{8,14},{10,8},{12,... | collective-permute-start | bytes 688136 | tf_op jit(solution)/shard_map/ppermute | solution.py:163
  29.8 0.7 slice.24
  30.5 0.1 copy-done.3
  30.7 0.3 all-to-all-done.in_ref
  31.0 0.5 split_rows.2.refs_0_
  31.5 1.6 %collective-permute-done.3.refs_4_ = bf16[64,1792]{1,0:T(8,128)(2,1)S(1)} collective-permute-done((bf16[64,1792]{1,0:T(8,128)(2,1)}, bf16[64,1792]{1,0:T(8,128)(2,1)S(1)}, u32[]{:S(2)}, u32[]{:S(2)}) %collective-permute-start.3) | collective-permute-done | bytes 229408 | tf_op jit(solution)/shard_map/ppermute | solution.py:163
  33.1 4.0 %collective-permute-done.2.refs_3_ = bf16[64,1792]{1,0:T(8,128)(2,1)} collective-permute-done((bf16[64,1792]{1,0:T(8,128)(2,1)}, bf16[64,1792]{1,0:T(8,128)(2,1)}, u32[]{:S(2)}, u32[]{:S(2)}) %collective-permute-start.2) | collective-permute-done | bytes 229408 | tf_op jit(solution)/shard_map/ppermute | solution.py:163
  37.1 2.3 %pack.1 = bf16[16,32,1792]{2,1,0:T(8,128)(2,1)} custom-call(bf16[128,1792]{1,0:T(8,128)(2,1)S(1)} %dispatch.3.refs_0_, bf16[128,1792]{1,0:T(8,128)(2,1)S(1)} %copy-done.4, bf16[128,1792]{1,0:T(8,128)(2,1)S(1)} %copy-done.2, bf16[64,1792]{1,0:T(8,128)(2,1)} %collective-permute-done.2.refs_3_, bf16[64,1792]{1,0:T(8,128)(2,1)S(1)} %collective-permute-done.3.refs_4_), custom_call_target="tpu_custom_call" | custom-call | tf_op jit(solution)/shard_map/pack/pallas_call | solution.py:148
  39.4 6.4 %all-to-all-start.1 = ((bf16[16,32,1792]{2,1,0:T(8,128)(2,1)}), bf16[16,32,1792]{2,1,0:T(8,128)(2,1)S(1)}, u32[]{:S(2)}, u32[]{:S(2)}) async-start(bf16[16,32,1792]{2,1,0:T(8,128)(2,1)} %pack.1), calls=%async_computation.1 | async-start | bytes 3670016 | tf_op jit(solution)/shard_map/all_to_all | solution.py:551
  45.7 0.1 collective-permute-start.6
  45.8 1.5 collective-permute-start.5
  47.3 20.6 %all-to-all-done.1.in_ref = bf16[16,32,1792]{2,1,0:T(8,128)(2,1)S(1)} async-done(((bf16[16,32,1792]{2,1,0:T(8,128)(2,1)}), bf16[16,32,1792]{2,1,0:T(8,128)(2,1)S(1)}, u32[]{:S(2)}, u32[]{:S(2)}) %all-to-all-start.1) | async-done | bytes 1835040 | tf_op jit(solution)/shard_map/all_to_all | solution.py:551
  67.8 0.6 split_rows.3.refs_0_
  68.5 6.4 %collective-permute-start.4 = (bf16[512,1792]{1,0:T(8,128)(2,1)S(1)}, bf16[512,1792]{1,0:T(8,128)(2,1)S(1)}, u32[]{:S(2)}, u32[]{:S(2)}) collective-permute-start(bf16[512,1792]{1,0:T(8,128)(2,1)S(1)} %split_rows.3.refs_0_), channel_id=1, source_target_pairs={{0,1},{1,0},{2,3},{3,2},{4,5},{5,4},{6,7},{7,6},{8,9},{9,8},{10,11... | collective-permute-start | bytes 5505032 | tf_op jit(solution)/shard_map/ppermute | solution.py:167
  74.9 0.1 collective-permute-start.7
  75.0 3.5 %collective-permute-start.9 = (bf16[128,5376]{1,0:T(8,128)(2,1)}, bf16[128,5376]{1,0:T(8,128)(2,1)S(1)}, u32[]{:S(2)}, u32[]{:S(2)}) collective-permute-start(bf16[128,5376]{1,0:T(8,128)(2,1)} %collective-permute-done.6.refs_2_), channel_id=1, source_target_pairs={{0,1},{1,0},{2,3},{3,2},{4,5},{5,4},{6,7},{7,6},{8,9},{9,8},{10,11... | collective-permute-start | bytes 4128776 | tf_op jit(solution)/shard_map/ppermute | solution.py:167
  78.5 1.3 collective-permute-start.8
  79.8 1.1 slice.27
  81.0 1.1 slice.26
  82.2 1.7 %collective-permute-start.10 = (bf16[64,5376]{1,0:T(8,128)(2,1)S(1)}, bf16[64,5376]{1,0:T(8,128)(2,1)S(1)}, u32[]{:S(2)}, u32[]{:S(2)}) collective-permute-start(bf16[64,5376]{1,0:T(8,128)(2,1)S(1)} %slice.26), channel_id=1, source_target_pairs={{0,2},{2,4},{4,6},{6,0},{1,3},{3,5},{5,7},{7,1},{8,10},{10,12},{12... | collective-permute-start | bytes 2064392 | tf_op jit(solution)/shard_map/ppermute | solution.py:163
  83.9 3.6 %acts.3 = (f32[3,512,256]{2,1,0:T(8,128)S(1)}, bf16[512,1792]{1,0:T(8,128)(2,1)S(1)}, bf16[512,1792]{1,0:T(8,128)(2,1)S(1)}) custom-call(bf16[512,1792]{1,0:T(8,128)(2,1)S(1)} %split_rows.3.refs_0_, bf16[512,1792]{1,0:T(8,128)(2,1)S(1)} %collective-permute-done.4.refs_1_, bf16[7168,256]{1,0:T(8,128)(2,1)} %bitcast.7, bf16[7168,256]{1,0:T(8,128)(2,1)} %bitcast.9, ...), custom_call_target="tpu_custom_call" | custom-call | flops 1409286144 | bytes 6422528 | tf_op jit(solution)/shard_map/acts/pallas_call | solution.py:313
  87.5 8.2 %acts.4 = (bf16[384,768]{1,0:T(8,128)(2,1)S(1)}, bf16[384,5376]{1,0:T(8,128)(2,1)S(1)}, bf16[384,5376]{1,0:T(8,128)(2,1)S(1)}, bf16[5376,256]{1,0:T(8,128)(2,1)S...) custom-call(bf16[128,5376]{1,0:T(8,128)(2,1)} %copy-done, ...), custom_call_target="tpu_custom_call" | custom-call | flops 3170893824 | bytes 16515072 | tf_op jit(solution)/shard_map/acts/pallas_call | solution.py:313
  95.7 2.4 %collective-permute-done.11.refs_1_ = bf16[64,5376]{1,0:T(8,128)(2,1)S(1)} collective-permute-done((bf16[64,5376]{1,0:T(8,128)(2,1)S(1)}, bf16[64,5376]{1,0:T(8,128)(2,1)S(1)}, u32[]{:S(2)}, u32[]{:S(2)}) %collective-permute-start.11) | collective-permute-done | bytes 688160 | tf_op jit(solution)/shard_map/ppermute | solution.py:163
  98.1 1.8 %collective-permute-done.10.refs_0_ = bf16[64,5376]{1,0:T(8,128)(2,1)S(1)} collective-permute-done((bf16[64,5376]{1,0:T(8,128)(2,1)S(1)}, bf16[64,5376]{1,0:T(8,128)(2,1)S(1)}, u32[]{:S(2)}, u32[]{:S(2)}) %collective-permute-start.10) | collective-permute-done | bytes 688160 | tf_op jit(solution)/shard_map/ppermute | solution.py:163
  99.9 1.6 %collective-permute-start.12 = (bf16[64,5376]{1,0:T(8,128)(2,1)S(1)}, bf16[64,5376]{1,0:T(8,128)(2,1)S(1)}, u32[]{:S(2)}, u32[]{:S(2)}) collective-permute-start(bf16[64,5376]{1,0:T(8,128)(2,1)S(1)} %collective-permute-done.10.refs_0_), channel_id=1, source_target_pairs={{0,1},{1,0},{2,3},{3,2},{4,5},{5,4},{6,7},{7,6},{8,9},{9,8},{10,11... | collective-permute-start | bytes 2064392 | tf_op jit(solution)/shard_map/ppermute | solution.py:167
  101.5 0.5 collective-permute-start.19
  102.0 1.5 collective-permute-start.14
  103.5 0.8 collective-permute-done.13.refs_3_
  104.2 3.7 %acts.5 = (bf16[128,768]{1,0:T(8,128)(2,1)S(1)}, bf16[128,5376]{1,0:T(8,128)(2,1)S(1)}, bf16[128,5376]{1,0:T(8,128)(2,1)S(1)}) custom-call(bf16[64,5376]{1,0:T(8,128)(2,1)S(1)} %collective-permute-done.10.refs_0_, bf16[64,5376]{1,0:T(8,128)(2,1)S(1)} %collective-permute-done.11.refs_1_, bf16[64,5376]{1,0:T(8,128)(2,1)S(1)} %collective-permute-done.12.refs_2_, ...), custom_call_target="tpu_custom_call" | custom-call | flops 1056964608 | bytes 11010048 | tf_op jit(solution)/shard_map/acts/pallas_call | solution.py:313
  108.0 9.8 %squares.1 = (bf16[144,768]{1,0:T(8,128)(2,1)S(1)}, bf16[896,512]{1,0:T(8,128)(2,1)S(1)}, bf16[896,512]{1,0:T(8,128)(2,1)S(1)}) custom-call(bf16[512,1792]{1,0:T(8,128)(2,1)S(1)} %get-tuple-element.38.x0, bf16[512,1792]{1,0:T(8,128)(2,1)S(1)} %get-tuple-element.39.g0, bf16[384,5376]{1,0:T(8,128)(2,1)S(1)} %get-tuple-element.41.xa, ...), custom_call_target="tpu_custom_call" | custom-call | flops 5637144576 | bytes 14680064 | tf_op jit(solution)/shard_map/squares/pallas_call | solution.py:379
  117.8 0.4 collective-permute-done.14.refs_1_
  118.2 0.8 collective-permute-start.20
  119.1 0.1 collective-permute-start.17
  119.2 1.4 collective-permute-start.16
  120.6 0.8 collective-permute-start.18
  121.5 8.3 %early_products.1.refs_8_ = f32[6,3,896,256]{3,2,1,0:T(8,128)S(1)} custom-call(bf16[384,768]{1,0:T(8,128)(2,1)S(1)} %get-tuple-element.43.hid_a.refs_0_, bf16[384,768]{1,0:T(8,128)(2,1)S(1)} %collective-permute-done.14.refs_1_, bf16[384,768]{1,0:T(8,128)(2,1)S(1)} %collective-permute-done.15.refs_2_, bf16[384,768]{1,0:T(8,128)(2,1)S(1)} %collective-permute-done.19.refs_3_, ...), custom_call_target="tpu_custom_call" | custom-call | flops 4227858432 | bytes 4718592 | tf_op jit(solution)/shard_map/early_products/pallas_call | solution.py:430
  129.8 7.4 %collective-permute-done.18.refs_4_ = bf16[144,768]{1,0:T(8,128)(2,1)S(1)} collective-permute-done((bf16[144,768]{1,0:T(8,128)(2,1)S(1)}, bf16[144,768]{1,0:T(8,128)(2,1)S(1)}, u32[]{:S(2)}, u32[]{:S(2)}) %collective-permute-start.18) | collective-permute-done | bytes 221216 | tf_op jit(solution)/shard_map/ppermute | solution.py:163
  137.3 2.1 %collective-permute-start.23 = (bf16[336,768]{1,0:T(8,128)(2,1)S(1)}, bf16[336,768]{1,0:T(8,128)(2,1)S(1)}, u32[]{:S(2)}, u32[]{:S(2)}) collective-permute-start(bf16[336,768]{1,0:T(8,128)(2,1)S(1)} %collective-permute-done.16.refs_2_), channel_id=1, source_target_pairs={{0,1},{1,0},{2,3},{3,2},{4,5},{5,4},{6,7},{7,6},{8,9},{9,8},{10,11... | collective-permute-start | bytes 1548296 | tf_op jit(solution)/shard_map/ppermute | solution.py:167
  139.4 0.5 collective-permute-start.22
  139.9 2.1 %collective-permute-done.22.refs_1_ = bf16[144,768]{1,0:T(8,128)(2,1)S(1)} collective-permute-done((bf16[144,768]{1,0:T(8,128)(2,1)S(1)}, bf16[144,768]{1,0:T(8,128)(2,1)S(1)}, u32[]{:S(2)}, u32[]{:S(2)}) %collective-permute-start.22) | collective-permute-done | bytes 221216 | tf_op jit(solution)/shard_map/ppermute | solution.py:167
  141.9 0.3 collective-permute-done.25.refs_7_
  142.3 6.7 %final.1 = bf16[3,896,2048]{2,1,0:T(8,128)(2,1)} custom-call(bf16[144,768]{1,0:T(8,128)(2,1)S(1)} %get-tuple-element.57.refs_6_.refs_0_, bf16[144,768]{1,0:T(8,128)(2,1)S(1)} %collective-permute-done.22.refs_1_, bf16[336,768]{1,0:T(8,128)(2,1)S(1)} %collective-permute-done.16.refs_2_, bf16[336,768]{1,0:T(8,128)(2,1)S(1)} %collective-permute-done.17.refs_3_, ...), custom_call_target="tpu_custom_call" | custom-call | flops 2818572288 | bytes 22020096 | tf_op jit(solution)/shard_map/final/pallas_call | solution.py:490
  (36 shorter events, 0.3 us)
Async XLA Ops:
  3.7 27.3 %all-to-all-start = ((bf16[16,8,5376]{2,1,0:T(8,128)(2,1)}), bf16[16,8,5376]{2,1,0:T(8,128)(2,1)S(1)}, u32[]{:S(2)}, u32[]{:S(2)}) async-start(bf16[16,8,5376]{2,1,0:T(8,128)(2,1)} %bitcast.2), calls=%async_computation | async-start | bytes 2752512 | tf_op jit(solution)/shard_map/all_to_all | solution.py:544
  12.9 12.7 %collective-permute-start.1 = (bf16[128,1792]{1,0:T(8,128)(2,1)S(1)}, bf16[128,1792]{1,0:T(8,128)(2,1)S(1)}, u32[]{:S(2)}, u32[]{:S(2)}) collective-permute-start(bf16[128,1792]{1,0:T(8,128)(2,1)S(1)} %dispatch.3.refs_0_), channel_id=1, source_target_pairs={{0,6},{2,0},{4,2},{6,4},{1,7},{3,1},{5,3},{7,5},{8,14},{10,8},{12,... | collective-permute-start | bytes 1376264 | tf_op jit(solution)/shard_map/ppermute | solution.py:163
  16.8 13.0 %collective-permute-start = (bf16[128,1792]{1,0:T(8,128)(2,1)S(1)}, bf16[128,1792]{1,0:T(8,128)(2,1)S(1)}, u32[]{:S(2)}, u32[]{:S(2)}) collective-permute-start(bf16[128,1792]{1,0:T(8,128)(2,1)S(1)} %dispatch.3.refs_0_), channel_id=1, source_target_pairs={{0,2},{2,4},{4,6},{6,0},{1,3},{3,5},{5,7},{7,1},{8,10},{10,12},{12... | collective-permute-start | bytes 1376264 | tf_op jit(solution)/shard_map/ppermute | solution.py:163
  25.6 4.9 %copy-start.1 = (bf16[128,1792]{1,0:T(8,128)(2,1)}, bf16[128,1792]{1,0:T(8,128)(2,1)S(1)}, u32[]{:S(2)}) copy-start(bf16[128,1792]{1,0:T(8,128)(2,1)S(1)} %collective-permute-done.1.refs_2_) | copy-start | bytes 1376260
  26.4 6.7 %collective-permute-start.3 = (bf16[64,1792]{1,0:T(8,128)(2,1)}, bf16[64,1792]{1,0:T(8,128)(2,1)S(1)}, u32[]{:S(2)}, u32[]{:S(2)}) collective-permute-start(bf16[64,1792]{1,0:T(8,128)(2,1)} %slice.25), channel_id=1, source_target_pairs={{0,6},{2,0},{4,2},{6,4},{1,7},{3,1},{5,3},{7,5},{8,14},{10,8},{12,... | collective-permute-start | bytes 688136 | tf_op jit(solution)/shard_map/ppermute | solution.py:163
  29.8 0.9 copy-start.3
  30.7 6.4 %collective-permute-start.2 = (bf16[64,1792]{1,0:T(8,128)(2,1)}, bf16[64,1792]{1,0:T(8,128)(2,1)}, u32[]{:S(2)}, u32[]{:S(2)}) collective-permute-start(bf16[64,1792]{1,0:T(8,128)(2,1)} %slice.24), channel_id=1, source_target_pairs={{0,2},{2,4},{4,6},{6,0},{1,3},{3,5},{5,7},{7,1},{8,10},{10,12},{12... | collective-permute-start | bytes 688136 | tf_op jit(solution)/shard_map/ppermute | solution.py:163
  31.0 6.1 %copy-start.2 = (bf16[128,1792]{1,0:T(8,128)(2,1)S(1)}, bf16[128,1792]{1,0:T(8,128)(2,1)}, u32[]{:S(2)}) copy-start(bf16[128,1792]{1,0:T(8,128)(2,1)} %copy-done.1) | copy-start | bytes 1376260
  31.0 6.1 %copy-start.4 = (bf16[128,1792]{1,0:T(8,128)(2,1)S(1)}, bf16[128,1792]{1,0:T(8,128)(2,1)}, u32[]{:S(2)}) copy-start(bf16[128,1792]{1,0:T(8,128)(2,1)} %copy-done.3) | copy-start | bytes 1376260
  31.5 43.4 %copy-start = (bf16[128,5376]{1,0:T(8,128)(2,1)}, bf16[128,5376]{1,0:T(8,128)(2,1)S(1)}, u32[]{:S(2)}) copy-start(bf16[128,5376]{1,0:T(8,128)(2,1)S(1)} %split_rows.2.refs_0_) | copy-start | bytes 4128772
  39.4 28.5 %all-to-all-start.1 = ((bf16[16,32,1792]{2,1,0:T(8,128)(2,1)}), bf16[16,32,1792]{2,1,0:T(8,128)(2,1)S(1)}, u32[]{:S(2)}, u32[]{:S(2)}) async-start(bf16[16,32,1792]{2,1,0:T(8,128)(2,1)} %pack.1), calls=%async_computation.1 | async-start | bytes 3670016 | tf_op jit(solution)/shard_map/all_to_all | solution.py:551
  45.7 29.3 %collective-permute-start.6 = (bf16[128,5376]{1,0:T(8,128)(2,1)S(1)}, bf16[128,5376]{1,0:T(8,128)(2,1)}, u32[]{:S(2)}, u32[]{:S(2)}) collective-permute-start(bf16[128,5376]{1,0:T(8,128)(2,1)S(1)} %split_rows.2.refs_0_), channel_id=1, source_target_pairs={{0,6},{2,0},{4,2},{6,4},{1,7},{3,1},{5,3},{7,5},{8,14},{10,8},{12,... | collective-permute-start | bytes 4128776 | tf_op jit(solution)/shard_map/ppermute | solution.py:163
  45.8 32.7 %collective-permute-start.5 = (bf16[128,5376]{1,0:T(8,128)(2,1)S(1)}, bf16[128,5376]{1,0:T(8,128)(2,1)}, u32[]{:S(2)}, u32[]{:S(2)}) collective-permute-start(bf16[128,5376]{1,0:T(8,128)(2,1)S(1)} %split_rows.2.refs_0_), channel_id=1, source_target_pairs={{0,2},{2,4},{4,6},{6,0},{1,3},{3,5},{5,7},{7,1},{8,10},{10,12},{12... | collective-permute-start | bytes 4128776 | tf_op jit(solution)/shard_map/ppermute | solution.py:163
  68.5 13.7 %collective-permute-start.4 = (bf16[512,1792]{1,0:T(8,128)(2,1)S(1)}, bf16[512,1792]{1,0:T(8,128)(2,1)S(1)}, u32[]{:S(2)}, u32[]{:S(2)}) collective-permute-start(bf16[512,1792]{1,0:T(8,128)(2,1)S(1)} %split_rows.3.refs_0_), channel_id=1, source_target_pairs={{0,1},{1,0},{2,3},{3,2},{4,5},{5,4},{6,7},{7,6},{8,9},{9,8},{10,11... | collective-permute-start | bytes 5505032 | tf_op jit(solution)/shard_map/ppermute | solution.py:167
  74.9 12.6 %collective-permute-start.7 = (bf16[128,5376]{1,0:T(8,128)(2,1)S(1)}, bf16[128,5376]{1,0:T(8,128)(2,1)S(1)}, u32[]{:S(2)}, u32[]{:S(2)}) collective-permute-start(bf16[128,5376]{1,0:T(8,128)(2,1)S(1)} %split_rows.2.refs_0_), channel_id=1, source_target_pairs={{0,1},{1,0},{2,3},{3,2},{4,5},{5,4},{6,7},{7,6},{8,9},{9,8},{10,11... | collective-permute-start | bytes 4128776 | tf_op jit(solution)/shard_map/ppermute | solution.py:167
  75.0 12.5 %collective-permute-start.9 = (bf16[128,5376]{1,0:T(8,128)(2,1)}, bf16[128,5376]{1,0:T(8,128)(2,1)S(1)}, u32[]{:S(2)}, u32[]{:S(2)}) collective-permute-start(bf16[128,5376]{1,0:T(8,128)(2,1)} %collective-permute-done.6.refs_2_), channel_id=1, source_target_pairs={{0,1},{1,0},{2,3},{3,2},{4,5},{5,4},{6,7},{7,6},{8,9},{9,8},{10,11... | collective-permute-start | bytes 4128776 | tf_op jit(solution)/shard_map/ppermute | solution.py:167
  78.5 9.0 %collective-permute-start.8 = (bf16[128,5376]{1,0:T(8,128)(2,1)}, bf16[128,5376]{1,0:T(8,128)(2,1)S(1)}, u32[]{:S(2)}, u32[]{:S(2)}) collective-permute-start(bf16[128,5376]{1,0:T(8,128)(2,1)} %collective-permute-done.5.refs_1_), channel_id=1, source_target_pairs={{0,1},{1,0},{2,3},{3,2},{4,5},{5,4},{6,7},{7,6},{8,9},{9,8},{10,11... | collective-permute-start | bytes 4128776 | tf_op jit(solution)/shard_map/ppermute | solution.py:167
  80.9 17.1 %collective-permute-start.11 = (bf16[64,5376]{1,0:T(8,128)(2,1)S(1)}, bf16[64,5376]{1,0:T(8,128)(2,1)S(1)}, u32[]{:S(2)}, u32[]{:S(2)}) collective-permute-start(bf16[64,5376]{1,0:T(8,128)(2,1)S(1)} %slice.27), channel_id=1, source_target_pairs={{0,6},{2,0},{4,2},{6,4},{1,7},{3,1},{5,3},{7,5},{8,14},{10,8},{12,... | collective-permute-start | bytes 2064392 | tf_op jit(solution)/shard_map/ppermute | solution.py:163
  82.2 17.7 %collective-permute-start.10 = (bf16[64,5376]{1,0:T(8,128)(2,1)S(1)}, bf16[64,5376]{1,0:T(8,128)(2,1)S(1)}, u32[]{:S(2)}, u32[]{:S(2)}) collective-permute-start(bf16[64,5376]{1,0:T(8,128)(2,1)S(1)} %slice.26), channel_id=1, source_target_pairs={{0,2},{2,4},{4,6},{6,0},{1,3},{3,5},{5,7},{7,1},{8,10},{10,12},{12... | collective-permute-start | bytes 2064392 | tf_op jit(solution)/shard_map/ppermute | solution.py:163
  99.9 3.6 %collective-permute-start.12 = (bf16[64,5376]{1,0:T(8,128)(2,1)S(1)}, bf16[64,5376]{1,0:T(8,128)(2,1)S(1)}, u32[]{:S(2)}, u32[]{:S(2)}) collective-permute-start(bf16[64,5376]{1,0:T(8,128)(2,1)S(1)} %collective-permute-done.10.refs_0_), channel_id=1, source_target_pairs={{0,1},{1,0},{2,3},{3,2},{4,5},{5,4},{6,7},{7,6},{8,9},{9,8},{10,11... | collective-permute-start | bytes 2064392 | tf_op jit(solution)/shard_map/ppermute | solution.py:167
  101.5 2.8 %collective-permute-start.13 = (bf16[64,5376]{1,0:T(8,128)(2,1)S(1)}, bf16[64,5376]{1,0:T(8,128)(2,1)S(1)}, u32[]{:S(2)}, u32[]{:S(2)}) collective-permute-start(bf16[64,5376]{1,0:T(8,128)(2,1)S(1)} %collective-permute-done.11.refs_1_), channel_id=1, source_target_pairs={{0,1},{1,0},{2,3},{3,2},{4,5},{5,4},{6,7},{7,6},{8,9},{9,8},{10,11... | collective-permute-start | bytes 2064392 | tf_op jit(solution)/shard_map/ppermute | solution.py:167
  101.5 19.1 %collective-permute-start.19 = (bf16[384,768]{1,0:T(8,128)(2,1)S(1)}, bf16[384,768]{1,0:T(8,128)(2,1)S(1)}, u32[]{:S(2)}, u32[]{:S(2)}) collective-permute-start(bf16[384,768]{1,0:T(8,128)(2,1)S(1)} %get-tuple-element.43.hid_a.refs_0_), channel_id=1, source_target_pairs={{0,1},{1,0},{2,3},{3,2},{4,5},{5,4},{6,7},{7,6},{8,9},{9,8},{10,11... | collective-permute-start | bytes 1769480 | tf_op jit(solution)/shard_map/ppermute | solution.py:167
  102.0 15.8 %collective-permute-start.15 = (bf16[384,768]{1,0:T(8,128)(2,1)S(1)}, bf16[384,768]{1,0:T(8,128)(2,1)S(1)}, u32[]{:S(2)}, u32[]{:S(2)}) collective-permute-start(bf16[384,768]{1,0:T(8,128)(2,1)S(1)} %get-tuple-element.43.hid_a.refs_0_), channel_id=1, source_target_pairs={{0,6},{2,0},{4,2},{6,4},{1,7},{3,1},{5,3},{7,5},{8,14},{10,8},{12,... | collective-permute-start | bytes 1769480 | tf_op jit(solution)/shard_map/ppermute | solution.py:163
  102.0 16.2 %collective-permute-start.14 = (bf16[384,768]{1,0:T(8,128)(2,1)S(1)}, bf16[384,768]{1,0:T(8,128)(2,1)S(1)}, u32[]{:S(2)}, u32[]{:S(2)}) collective-permute-start(bf16[384,768]{1,0:T(8,128)(2,1)S(1)} %get-tuple-element.43.hid_a.refs_0_), channel_id=1, source_target_pairs={{0,2},{2,4},{4,6},{6,0},{1,3},{3,5},{5,7},{7,1},{8,10},{10,12},{12... | collective-permute-start | bytes 1769480 | tf_op jit(solution)/shard_map/ppermute | solution.py:163
  118.2 3.3 %collective-permute-start.20 = (bf16[384,768]{1,0:T(8,128)(2,1)S(1)}, bf16[384,768]{1,0:T(8,128)(2,1)S(1)}, u32[]{:S(2)}, u32[]{:S(2)}) collective-permute-start(bf16[384,768]{1,0:T(8,128)(2,1)S(1)} %collective-permute-done.14.refs_1_), channel_id=1, source_target_pairs={{0,1},{1,0},{2,3},{3,2},{4,5},{5,4},{6,7},{7,6},{8,9},{9,8},{10,11... | collective-permute-start | bytes 1769480 | tf_op jit(solution)/shard_map/ppermute | solution.py:167
  119.0 2.5 %collective-permute-start.21 = (bf16[384,768]{1,0:T(8,128)(2,1)S(1)}, bf16[384,768]{1,0:T(8,128)(2,1)S(1)}, u32[]{:S(2)}, u32[]{:S(2)}) collective-permute-start(bf16[384,768]{1,0:T(8,128)(2,1)S(1)} %collective-permute-done.15.refs_2_), channel_id=1, source_target_pairs={{0,1},{1,0},{2,3},{3,2},{4,5},{5,4},{6,7},{7,6},{8,9},{9,8},{10,11... | collective-permute-start | bytes 1769480 | tf_op jit(solution)/shard_map/ppermute | solution.py:167
  119.1 18.2 %collective-permute-start.17 = (bf16[336,768]{1,0:T(8,128)(2,1)S(1)}, bf16[336,768]{1,0:T(8,128)(2,1)S(1)}, u32[]{:S(2)}, u32[]{:S(2)}) collective-permute-start(bf16[336,768]{1,0:T(8,128)(2,1)S(1)} %get-tuple-element.61), channel_id=1, source_target_pairs={{0,6},{2,0},{4,2},{6,4},{1,7},{3,1},{5,3},{7,5},{8,14},{10,8},{12,... | collective-permute-start | bytes 1548296 | tf_op jit(solution)/shard_map/ppermute | solution.py:163
  119.2 18.0 %collective-permute-start.16 = (bf16[336,768]{1,0:T(8,128)(2,1)S(1)}, bf16[336,768]{1,0:T(8,128)(2,1)S(1)}, u32[]{:S(2)}, u32[]{:S(2)}) collective-permute-start(bf16[336,768]{1,0:T(8,128)(2,1)S(1)} %get-tuple-element.62), channel_id=1, source_target_pairs={{0,2},{2,4},{4,6},{6,0},{1,3},{3,5},{5,7},{7,1},{8,10},{10,12},{12... | collective-permute-start | bytes 1548296 | tf_op jit(solution)/shard_map/ppermute | solution.py:163
  120.6 16.6 %collective-permute-start.18 = (bf16[144,768]{1,0:T(8,128)(2,1)S(1)}, bf16[144,768]{1,0:T(8,128)(2,1)S(1)}, u32[]{:S(2)}, u32[]{:S(2)}) collective-permute-start(bf16[144,768]{1,0:T(8,128)(2,1)S(1)} %get-tuple-element.57.refs_6_.refs_0_), channel_id=1, source_target_pairs={{0,4},{2,6},{4,0},{6,2},{1,5},{3,7},{5,1},{7,3},{8,12},{10,14},{12... | collective-permute-start | bytes 663560 | tf_op jit(solution)/shard_map/ppermute | solution.py:163
  137.3 5.0 %collective-permute-start.23 = (bf16[336,768]{1,0:T(8,128)(2,1)S(1)}, bf16[336,768]{1,0:T(8,128)(2,1)S(1)}, u32[]{:S(2)}, u32[]{:S(2)}) collective-permute-start(bf16[336,768]{1,0:T(8,128)(2,1)S(1)} %collective-permute-done.16.refs_2_), channel_id=1, source_target_pairs={{0,1},{1,0},{2,3},{3,2},{4,5},{5,4},{6,7},{7,6},{8,9},{9,8},{10,11... | collective-permute-start | bytes 1548296 | tf_op jit(solution)/shard_map/ppermute | solution.py:167
  139.4 2.9 %collective-permute-start.24 = (bf16[336,768]{1,0:T(8,128)(2,1)S(1)}, bf16[336,768]{1,0:T(8,128)(2,1)S(1)}, u32[]{:S(2)}, u32[]{:S(2)}) collective-permute-start(bf16[336,768]{1,0:T(8,128)(2,1)S(1)} %collective-permute-done.17.refs_3_), channel_id=1, source_target_pairs={{0,1},{1,0},{2,3},{3,2},{4,5},{5,4},{6,7},{7,6},{8,9},{9,8},{10,11... | collective-permute-start | bytes 1548296 | tf_op jit(solution)/shard_map/ppermute | solution.py:167
  139.4 2.6 %collective-permute-start.22 = (bf16[144,768]{1,0:T(8,128)(2,1)S(1)}, bf16[144,768]{1,0:T(8,128)(2,1)S(1)}, u32[]{:S(2)}, u32[]{:S(2)}) collective-permute-start(bf16[144,768]{1,0:T(8,128)(2,1)S(1)} %get-tuple-element.57.refs_6_.refs_0_), channel_id=1, source_target_pairs={{0,1},{1,0},{2,3},{3,2},{4,5},{5,4},{6,7},{7,6},{8,9},{9,8},{10,11... | collective-permute-start | bytes 663560 | tf_op jit(solution)/shard_map/ppermute | solution.py:167
  139.9 2.4 %collective-permute-start.25 = (bf16[144,768]{1,0:T(8,128)(2,1)S(1)}, bf16[144,768]{1,0:T(8,128)(2,1)S(1)}, u32[]{:S(2)}, u32[]{:S(2)}) collective-permute-start(bf16[144,768]{1,0:T(8,128)(2,1)S(1)} %collective-permute-done.18.refs_4_), channel_id=1, source_target_pairs={{0,1},{1,0},{2,3},{3,2},{4,5},{5,4},{6,7},{7,6},{8,9},{9,8},{10,11... | collective-permute-start | bytes 663560 | tf_op jit(solution)/shard_map/ppermute | solution.py:167

commit v5 on v4

--- a/solution.py
+++ b/solution.py
@@ -152,7 +152,7 @@
         out_shape=jax.ShapeDtypeStruct((hot, (len(blocks) + 1) * per, width), BF16),
         compiler_params=params(16),
         name="pack",
-    )(*blocks, first, second)
+    )(*[pltpu.with_memory_space_constraint(t, pltpu.VMEM) for t in (*blocks, first, second)])
 
 
 def shift(n, k):

time: 150 us -> 150 us (level)
  no operation moved by 1% of the time
where the time goes in v5:
time: 150 us; the launch traced here: 149 us
  waiting for transfers between devices  50.6 us (34%)
  Pallas kernels  49 us (33%)
  starting transfers between devices  45.1 us (30%)
  local copies, waits for them, and re-layouts  3.96 us (3%)
    ppermute x13, waiting for transfers between devices, along(): return lax.ppermute(x, 'z', shift(4, k))  26.5 us
    all_to_all x1, waiting for transfers between devices, body(): lax.all_to_all(pack(near, far[0], far[1], hot), expert, split_axis=0, con...  20.6 us
    ppermute x13, starting transfers between devices, swap(): return lax.ppermute(x, 'core', shift(2, 1))  16.8 us
    pallas_call x3, Pallas kernels, acts(): pl.pallas_call(functools.partial(acts_kernel, rows_of, skip, last, keep,...  15.4 us
    ppermute x13, starting transfers between devices, along(): return lax.ppermute(x, 'z', shift(4, k))  14.4 us
    pallas_call x1, Pallas kernels, squares(): pl.pallas_call(squares_kernel, in_specs=[VMEM] * 8, out_specs=(VMEM,) * 3...  9.81 us
    pallas_call x1, Pallas kernels, early_products(): pl.pallas_call(functools.partial(early_kernel, copies, missing), in_specs...  8.34 us
    all_to_all x1, starting transfers between devices, body(): lax.all_to_all(sent_rest.reshape(hot, 2 * CAP, width - early), expert, sp...  7.6 us
  transfers between devices with their start and end apart: 28, of which 12 were waited for; matrix products, arithmetic and copies ran while one was open for 3% of the time, Pallas kernels for 24%

profile of v5, /device:TPU:1, one launch (start us, length us, event | category | flops | bytes accessed | tf_op | source)
XLA Modules:
  0.0 149.1 jit_solution(14790948060029048997)
XLA Ops:
  0.0 3.7 %dispatch.2 = bf16[128,5376]{1,0:T(8,128)(2,1)} custom-call(s32[8,128]{1,0:T(8,128)} %bitcast.13, f32[8,128]{1,0:T(8,128)} %bitcast.15, s32[384]{0:T(512)} %refs_2_.2, bf16[128,7168]{1,0:T(8,128)(2,1)} %refs_3_.3, bf16[128,7168]{1,0:T(8,128)(2,1)} %refs_4_.3), custom_call_target="tpu_custom_call" | custom-call | flops 704643072 | bytes 4128768 | tf_op jit(solution)/shard_map/dispatch/pallas_call | solution.py:88
  3.7 7.6 %all-to-all-start = ((bf16[16,8,5376]{2,1,0:T(8,128)(2,1)}), bf16[16,8,5376]{2,1,0:T(8,128)(2,1)S(1)}, u32[]{:S(2)}, u32[]{:S(2)}) async-start(bf16[16,8,5376]{2,1,0:T(8,128)(2,1)} %bitcast.2), calls=%async_computation | async-start | bytes 2752512 | tf_op jit(solution)/shard_map/all_to_all | solution.py:544
  11.3 1.6 %dispatch.3.refs_0_ = bf16[128,1792]{1,0:T(8,128)(2,1)S(1)} custom-call(s32[8,128]{1,0:T(8,128)} %bitcast.14, f32[8,128]{1,0:T(8,128)} %bitcast.16, s32[384]{0:T(512)} %refs_2_.2, bf16[128,7168]{1,0:T(8,128)(2,1)} %refs_3_.3, bf16[128,7168]{1,0:T(8,128)(2,1)} %refs_4_.3), custom_call_target="tpu_custom_call" | custom-call | flops 234881024 | bytes 1376256 | tf_op jit(solution)/shard_map/dispatch/pallas_call | solution.py:88
  12.9 3.8 %collective-permute-start.1 = (bf16[128,1792]{1,0:T(8,128)(2,1)S(1)}, bf16[128,1792]{1,0:T(8,128)(2,1)S(1)}, u32[]{:S(2)}, u32[]{:S(2)}) collective-permute-start(bf16[128,1792]{1,0:T(8,128)(2,1)S(1)} %dispatch.3.refs_0_), channel_id=1, source_target_pairs={{0,6},{2,0},{4,2},{6,4},{1,7},{3,1},{5,3},{7,5},{8,14},{10,8},{12,... | collective-permute-start | bytes 1376264 | tf_op jit(solution)/shard_map/ppermute | solution.py:163
  16.8 8.9 %collective-permute-done.1.refs_2_ = bf16[128,1792]{1,0:T(8,128)(2,1)S(1)} collective-permute-done((bf16[128,1792]{1,0:T(8,128)(2,1)S(1)}, bf16[128,1792]{1,0:T(8,128)(2,1)S(1)}, u32[]{:S(2)}, u32[]{:S(2)}) %collective-permute-start.1) | collective-permute-done | bytes 458784 | tf_op jit(solution)/shard_map/ppermute | solution.py:163
  25.6 0.8 slice.25
  26.4 3.4 %collective-permute-start.3 = (bf16[64,1792]{1,0:T(8,128)(2,1)}, bf16[64,1792]{1,0:T(8,128)(2,1)S(1)}, u32[]{:S(2)}, u32[]{:S(2)}) collective-permute-start(bf16[64,1792]{1,0:T(8,128)(2,1)} %slice.25), channel_id=1, source_target_pairs={{0,6},{2,0},{4,2},{6,4},{1,7},{3,1},{5,3},{7,5},{8,14},{10,8},{12,... | collective-permute-start | bytes 688136 | tf_op jit(solution)/shard_map/ppermute | solution.py:163
  29.8 0.7 slice.24
  30.5 0.1 copy-done.3
  30.7 0.3 all-to-all-done.in_ref
  31.0 0.5 split_rows.2.refs_0_
  31.5 1.6 %collective-permute-done.3.refs_4_ = bf16[64,1792]{1,0:T(8,128)(2,1)S(1)} collective-permute-done((bf16[64,1792]{1,0:T(8,128)(2,1)}, bf16[64,1792]{1,0:T(8,128)(2,1)S(1)}, u32[]{:S(2)}, u32[]{:S(2)}) %collective-permute-start.3) | collective-permute-done | bytes 229408 | tf_op jit(solution)/shard_map/ppermute | solution.py:163
  33.1 4.0 %collective-permute-done.2.refs_3_ = bf16[64,1792]{1,0:T(8,128)(2,1)} collective-permute-done((bf16[64,1792]{1,0:T(8,128)(2,1)}, bf16[64,1792]{1,0:T(8,128)(2,1)}, u32[]{:S(2)}, u32[]{:S(2)}) %collective-permute-start.2) | collective-permute-done | bytes 229408 | tf_op jit(solution)/shard_map/ppermute | solution.py:163
  37.1 2.3 %pack.1 = bf16[16,32,1792]{2,1,0:T(8,128)(2,1)} custom-call(bf16[128,1792]{1,0:T(8,128)(2,1)S(1)} %dispatch.3.refs_0_, bf16[128,1792]{1,0:T(8,128)(2,1)S(1)} %copy-done.4, bf16[128,1792]{1,0:T(8,128)(2,1)S(1)} %copy-done.2, bf16[64,1792]{1,0:T(8,128)(2,1)} %collective-permute-done.2.refs_3_, bf16[64,1792]{1,0:T(8,128)(2,1)S(1)} %collective-permute-done.3.refs_4_), custom_call_target="tpu_custom_call" | custom-call | tf_op jit(solution)/shard_map/pack/pallas_call | solution.py:148
  39.4 6.4 %all-to-all-start.1 = ((bf16[16,32,1792]{2,1,0:T(8,128)(2,1)}), bf16[16,32,1792]{2,1,0:T(8,128)(2,1)S(1)}, u32[]{:S(2)}, u32[]{:S(2)}) async-start(bf16[16,32,1792]{2,1,0:T(8,128)(2,1)} %pack.1), calls=%async_computation.1 | async-start | bytes 3670016 | tf_op jit(solution)/shard_map/all_to_all | solution.py:551
  45.7 0.1 collective-permute-start.6
  45.8 1.5 collective-permute-start.5
  47.3 20.6 %all-to-all-done.1.in_ref = bf16[16,32,1792]{2,1,0:T(8,128)(2,1)S(1)} async-done(((bf16[16,32,1792]{2,1,0:T(8,128)(2,1)}), bf16[16,32,1792]{2,1,0:T(8,128)(2,1)S(1)}, u32[]{:S(2)}, u32[]{:S(2)}) %all-to-all-start.1) | async-done | bytes 1835040 | tf_op jit(solution)/shard_map/all_to_all | solution.py:551
  67.8 0.6 split_rows.3.refs_0_
  68.5 6.4 %collective-permute-start.4 = (bf16[512,1792]{1,0:T(8,128)(2,1)S(1)}, bf16[512,1792]{1,0:T(8,128)(2,1)S(1)}, u32[]{:S(2)}, u32[]{:S(2)}) collective-permute-start(bf16[512,1792]{1,0:T(8,128)(2,1)S(1)} %split_rows.3.refs_0_), channel_id=1, source_target_pairs={{0,1},{1,0},{2,3},{3,2},{4,5},{5,4},{6,7},{7,6},{8,9},{9,8},{10,11... | collective-permute-start | bytes 5505032 | tf_op jit(solution)/shard_map/ppermute | solution.py:167
  74.9 0.1 collective-permute-start.7
  75.0 3.5 %collective-permute-start.9 = (bf16[128,5376]{1,0:T(8,128)(2,1)}, bf16[128,5376]{1,0:T(8,128)(2,1)S(1)}, u32[]{:S(2)}, u32[]{:S(2)}) collective-permute-start(bf16[128,5376]{1,0:T(8,128)(2,1)} %collective-permute-done.6.refs_2_), channel_id=1, source_target_pairs={{0,1},{1,0},{2,3},{3,2},{4,5},{5,4},{6,7},{7,6},{8,9},{9,8},{10,11... | collective-permute-start | bytes 4128776 | tf_op jit(solution)/shard_map/ppermute | solution.py:167
  78.5 1.3 collective-permute-start.8
  79.8 1.1 slice.27
  81.0 1.1 slice.26
  82.2 1.7 %collective-permute-start.10 = (bf16[64,5376]{1,0:T(8,128)(2,1)S(1)}, bf16[64,5376]{1,0:T(8,128)(2,1)S(1)}, u32[]{:S(2)}, u32[]{:S(2)}) collective-permute-start(bf16[64,5376]{1,0:T(8,128)(2,1)S(1)} %slice.26), channel_id=1, source_target_pairs={{0,2},{2,4},{4,6},{6,0},{1,3},{3,5},{5,7},{7,1},{8,10},{10,12},{12... | collective-permute-start | bytes 2064392 | tf_op jit(solution)/shard_map/ppermute | solution.py:163
  83.9 3.6 %acts.3 = (f32[3,512,256]{2,1,0:T(8,128)S(1)}, bf16[512,1792]{1,0:T(8,128)(2,1)S(1)}, bf16[512,1792]{1,0:T(8,128)(2,1)S(1)}) custom-call(bf16[512,1792]{1,0:T(8,128)(2,1)S(1)} %split_rows.3.refs_0_, bf16[512,1792]{1,0:T(8,128)(2,1)S(1)} %collective-permute-done.4.refs_1_, bf16[7168,256]{1,0:T(8,128)(2,1)} %bitcast.7, bf16[7168,256]{1,0:T(8,128)(2,1)} %bitcast.9, ...), custom_call_target="tpu_custom_call" | custom-call | flops 1409286144 | bytes 6422528 | tf_op jit(solution)/shard_map/acts/pallas_call | solution.py:313
  87.5 8.2 %acts.4 = (bf16[384,768]{1,0:T(8,128)(2,1)S(1)}, bf16[384,5376]{1,0:T(8,128)(2,1)S(1)}, bf16[384,5376]{1,0:T(8,128)(2,1)S(1)}, bf16[5376,256]{1,0:T(8,128)(2,1)S...) custom-call(bf16[128,5376]{1,0:T(8,128)(2,1)} %copy-done, ...), custom_call_target="tpu_custom_call" | custom-call | flops 3170893824 | bytes 16515072 | tf_op jit(solution)/shard_map/acts/pallas_call | solution.py:313
  95.7 2.4 %collective-permute-done.11.refs_1_ = bf16[64,5376]{1,0:T(8,128)(2,1)S(1)} collective-permute-done((bf16[64,5376]{1,0:T(8,128)(2,1)S(1)}, bf16[64,5376]{1,0:T(8,128)(2,1)S(1)}, u32[]{:S(2)}, u32[]{:S(2)}) %collective-permute-start.11) | collective-permute-done | bytes 688160 | tf_op jit(solution)/shard_map/ppermute | solution.py:163
  98.1 1.8 %collective-permute-done.10.refs_0_ = bf16[64,5376]{1,0:T(8,128)(2,1)S(1)} collective-permute-done((bf16[64,5376]{1,0:T(8,128)(2,1)S(1)}, bf16[64,5376]{1,0:T(8,128)(2,1)S(1)}, u32[]{:S(2)}, u32[]{:S(2)}) %collective-permute-start.10) | collective-permute-done | bytes 688160 | tf_op jit(solution)/shard_map/ppermute | solution.py:163
  99.9 1.6 %collective-permute-start.12 = (bf16[64,5376]{1,0:T(8,128)(2,1)S(1)}, bf16[64,5376]{1,0:T(8,128)(2,1)S(1)}, u32[]{:S(2)}, u32[]{:S(2)}) collective-permute-start(bf16[64,5376]{1,0:T(8,128)(2,1)S(1)} %collective-permute-done.10.refs_0_), channel_id=1, source_target_pairs={{0,1},{1,0},{2,3},{3,2},{4,5},{5,4},{6,7},{7,6},{8,9},{9,8},{10,11... | collective-permute-start | bytes 2064392 | tf_op jit(solution)/shard_map/ppermute | solution.py:167
  101.5 0.5 collective-permute-start.19
  102.0 1.5 collective-permute-start.14
  103.5 0.8 collective-permute-done.13.refs_3_
  104.2 3.7 %acts.5 = (bf16[128,768]{1,0:T(8,128)(2,1)S(1)}, bf16[128,5376]{1,0:T(8,128)(2,1)S(1)}, bf16[128,5376]{1,0:T(8,128)(2,1)S(1)}) custom-call(bf16[64,5376]{1,0:T(8,128)(2,1)S(1)} %collective-permute-done.10.refs_0_, bf16[64,5376]{1,0:T(8,128)(2,1)S(1)} %collective-permute-done.11.refs_1_, bf16[64,5376]{1,0:T(8,128)(2,1)S(1)} %collective-permute-done.12.refs_2_, ...), custom_call_target="tpu_custom_call" | custom-call | flops 1056964608 | bytes 11010048 | tf_op jit(solution)/shard_map/acts/pallas_call | solution.py:313
  108.0 9.8 %squares.1 = (bf16[144,768]{1,0:T(8,128)(2,1)S(1)}, bf16[896,512]{1,0:T(8,128)(2,1)S(1)}, bf16[896,512]{1,0:T(8,128)(2,1)S(1)}) custom-call(bf16[512,1792]{1,0:T(8,128)(2,1)S(1)} %get-tuple-element.38.x0, bf16[512,1792]{1,0:T(8,128)(2,1)S(1)} %get-tuple-element.39.g0, bf16[384,5376]{1,0:T(8,128)(2,1)S(1)} %get-tuple-element.41.xa, ...), custom_call_target="tpu_custom_call" | custom-call | flops 5637144576 | bytes 14680064 | tf_op jit(solution)/shard_map/squares/pallas_call | solution.py:379
  117.8 0.4 collective-permute-done.14.refs_1_
  118.2 0.8 collective-permute-start.20
  119.1 0.1 collective-permute-start.17
  119.2 1.4 collective-permute-start.16
  120.6 0.8 collective-permute-start.18
  121.5 8.3 %early_products.1.refs_8_ = f32[6,3,896,256]{3,2,1,0:T(8,128)S(1)} custom-call(bf16[384,768]{1,0:T(8,128)(2,1)S(1)} %get-tuple-element.43.hid_a.refs_0_, bf16[384,768]{1,0:T(8,128)(2,1)S(1)} %collective-permute-done.14.refs_1_, bf16[384,768]{1,0:T(8,128)(2,1)S(1)} %collective-permute-done.15.refs_2_, bf16[384,768]{1,0:T(8,128)(2,1)S(1)} %collective-permute-done.19.refs_3_, ...), custom_call_target="tpu_custom_call" | custom-call | flops 4227858432 | bytes 4718592 | tf_op jit(solution)/shard_map/early_products/pallas_call | solution.py:430
  129.8 7.4 %collective-permute-done.18.refs_4_ = bf16[144,768]{1,0:T(8,128)(2,1)S(1)} collective-permute-done((bf16[144,768]{1,0:T(8,128)(2,1)S(1)}, bf16[144,768]{1,0:T(8,128)(2,1)S(1)}, u32[]{:S(2)}, u32[]{:S(2)}) %collective-permute-start.18) | collective-permute-done | bytes 221216 | tf_op jit(solution)/shard_map/ppermute | solution.py:163
  137.3 2.1 %collective-permute-start.23 = (bf16[336,768]{1,0:T(8,128)(2,1)S(1)}, bf16[336,768]{1,0:T(8,128)(2,1)S(1)}, u32[]{:S(2)}, u32[]{:S(2)}) collective-permute-start(bf16[336,768]{1,0:T(8,128)(2,1)S(1)} %collective-permute-done.16.refs_2_), channel_id=1, source_target_pairs={{0,1},{1,0},{2,3},{3,2},{4,5},{5,4},{6,7},{7,6},{8,9},{9,8},{10,11... | collective-permute-start | bytes 1548296 | tf_op jit(solution)/shard_map/ppermute | solution.py:167
  139.4 0.5 collective-permute-start.22
  139.9 2.1 %collective-permute-done.22.refs_1_ = bf16[144,768]{1,0:T(8,128)(2,1)S(1)} collective-permute-done((bf16[144,768]{1,0:T(8,128)(2,1)S(1)}, bf16[144,768]{1,0:T(8,128)(2,1)S(1)}, u32[]{:S(2)}, u32[]{:S(2)}) %collective-permute-start.22) | collective-permute-done | bytes 221216 | tf_op jit(solution)/shard_map/ppermute | solution.py:167
  141.9 0.3 collective-permute-done.25.refs_7_
  142.3 6.7 %final.1 = bf16[3,896,2048]{2,1,0:T(8,128)(2,1)} custom-call(bf16[144,768]{1,0:T(8,128)(2,1)S(1)} %get-tuple-element.57.refs_6_.refs_0_, bf16[144,768]{1,0:T(8,128)(2,1)S(1)} %collective-permute-done.22.refs_1_, bf16[336,768]{1,0:T(8,128)(2,1)S(1)} %collective-permute-done.16.refs_2_, bf16[336,768]{1,0:T(8,128)(2,1)S(1)} %collective-permute-done.17.refs_3_, ...), custom_call_target="tpu_custom_call" | custom-call | flops 2818572288 | bytes 22020096 | tf_op jit(solution)/shard_map/final/pallas_call | solution.py:490
  (36 shorter events, 0.3 us)
Async XLA Ops:
  3.7 27.3 %all-to-all-start = ((bf16[16,8,5376]{2,1,0:T(8,128)(2,1)}), bf16[16,8,5376]{2,1,0:T(8,128)(2,1)S(1)}, u32[]{:S(2)}, u32[]{:S(2)}) async-start(bf16[16,8,5376]{2,1,0:T(8,128)(2,1)} %bitcast.2), calls=%async_computation | async-start | bytes 2752512 | tf_op jit(solution)/shard_map/all_to_all | solution.py:544
  12.9 12.7 %collective-permute-start.1 = (bf16[128,1792]{1,0:T(8,128)(2,1)S(1)}, bf16[128,1792]{1,0:T(8,128)(2,1)S(1)}, u32[]{:S(2)}, u32[]{:S(2)}) collective-permute-start(bf16[128,1792]{1,0:T(8,128)(2,1)S(1)} %dispatch.3.refs_0_), channel_id=1, source_target_pairs={{0,6},{2,0},{4,2},{6,4},{1,7},{3,1},{5,3},{7,5},{8,14},{10,8},{12,... | collective-permute-start | bytes 1376264 | tf_op jit(solution)/shard_map/ppermute | solution.py:163
  16.8 13.0 %collective-permute-start = (bf16[128,1792]{1,0:T(8,128)(2,1)S(1)}, bf16[128,1792]{1,0:T(8,128)(2,1)S(1)}, u32[]{:S(2)}, u32[]{:S(2)}) collective-permute-start(bf16[128,1792]{1,0:T(8,128)(2,1)S(1)} %dispatch.3.refs_0_), channel_id=1, source_target_pairs={{0,2},{2,4},{4,6},{6,0},{1,3},{3,5},{5,7},{7,1},{8,10},{10,12},{12... | collective-permute-start | bytes 1376264 | tf_op jit(solution)/shard_map/ppermute | solution.py:163
  25.6 4.9 %copy-start.1 = (bf16[128,1792]{1,0:T(8,128)(2,1)}, bf16[128,1792]{1,0:T(8,128)(2,1)S(1)}, u32[]{:S(2)}) copy-start(bf16[128,1792]{1,0:T(8,128)(2,1)S(1)} %collective-permute-done.1.refs_2_) | copy-start | bytes 1376260
  26.4 6.7 %collective-permute-start.3 = (bf16[64,1792]{1,0:T(8,128)(2,1)}, bf16[64,1792]{1,0:T(8,128)(2,1)S(1)}, u32[]{:S(2)}, u32[]{:S(2)}) collective-permute-start(bf16[64,1792]{1,0:T(8,128)(2,1)} %slice.25), channel_id=1, source_target_pairs={{0,6},{2,0},{4,2},{6,4},{1,7},{3,1},{5,3},{7,5},{8,14},{10,8},{12,... | collective-permute-start | bytes 688136 | tf_op jit(solution)/shard_map/ppermute | solution.py:163
  29.8 0.9 copy-start.3
  30.7 6.4 %collective-permute-start.2 = (bf16[64,1792]{1,0:T(8,128)(2,1)}, bf16[64,1792]{1,0:T(8,128)(2,1)}, u32[]{:S(2)}, u32[]{:S(2)}) collective-permute-start(bf16[64,1792]{1,0:T(8,128)(2,1)} %slice.24), channel_id=1, source_target_pairs={{0,2},{2,4},{4,6},{6,0},{1,3},{3,5},{5,7},{7,1},{8,10},{10,12},{12... | collective-permute-start | bytes 688136 | tf_op jit(solution)/shard_map/ppermute | solution.py:163
  31.0 6.1 %copy-start.2 = (bf16[128,1792]{1,0:T(8,128)(2,1)S(1)}, bf16[128,1792]{1,0:T(8,128)(2,1)}, u32[]{:S(2)}) copy-start(bf16[128,1792]{1,0:T(8,128)(2,1)} %copy-done.1) | copy-start | bytes 1376260
  31.0 6.1 %copy-start.4 = (bf16[128,1792]{1,0:T(8,128)(2,1)S(1)}, bf16[128,1792]{1,0:T(8,128)(2,1)}, u32[]{:S(2)}) copy-start(bf16[128,1792]{1,0:T(8,128)(2,1)} %copy-done.3) | copy-start | bytes 1376260
  31.5 43.4 %copy-start = (bf16[128,5376]{1,0:T(8,128)(2,1)}, bf16[128,5376]{1,0:T(8,128)(2,1)S(1)}, u32[]{:S(2)}) copy-start(bf16[128,5376]{1,0:T(8,128)(2,1)S(1)} %split_rows.2.refs_0_) | copy-start | bytes 4128772
  39.4 28.5 %all-to-all-start.1 = ((bf16[16,32,1792]{2,1,0:T(8,128)(2,1)}), bf16[16,32,1792]{2,1,0:T(8,128)(2,1)S(1)}, u32[]{:S(2)}, u32[]{:S(2)}) async-start(bf16[16,32,1792]{2,1,0:T(8,128)(2,1)} %pack.1), calls=%async_computation.1 | async-start | bytes 3670016 | tf_op jit(solution)/shard_map/all_to_all | solution.py:551
  45.7 29.3 %collective-permute-start.6 = (bf16[128,5376]{1,0:T(8,128)(2,1)S(1)}, bf16[128,5376]{1,0:T(8,128)(2,1)}, u32[]{:S(2)}, u32[]{:S(2)}) collective-permute-start(bf16[128,5376]{1,0:T(8,128)(2,1)S(1)} %split_rows.2.refs_0_), channel_id=1, source_target_pairs={{0,6},{2,0},{4,2},{6,4},{1,7},{3,1},{5,3},{7,5},{8,14},{10,8},{12,... | collective-permute-start | bytes 4128776 | tf_op jit(solution)/shard_map/ppermute | solution.py:163
  45.8 32.7 %collective-permute-start.5 = (bf16[128,5376]{1,0:T(8,128)(2,1)S(1)}, bf16[128,5376]{1,0:T(8,128)(2,1)}, u32[]{:S(2)}, u32[]{:S(2)}) collective-permute-start(bf16[128,5376]{1,0:T(8,128)(2,1)S(1)} %split_rows.2.refs_0_), channel_id=1, source_target_pairs={{0,2},{2,4},{4,6},{6,0},{1,3},{3,5},{5,7},{7,1},{8,10},{10,12},{12... | collective-permute-start | bytes 4128776 | tf_op jit(solution)/shard_map/ppermute | solution.py:163
  68.5 13.7 %collective-permute-start.4 = (bf16[512,1792]{1,0:T(8,128)(2,1)S(1)}, bf16[512,1792]{1,0:T(8,128)(2,1)S(1)}, u32[]{:S(2)}, u32[]{:S(2)}) collective-permute-start(bf16[512,1792]{1,0:T(8,128)(2,1)S(1)} %split_rows.3.refs_0_), channel_id=1, source_target_pairs={{0,1},{1,0},{2,3},{3,2},{4,5},{5,4},{6,7},{7,6},{8,9},{9,8},{10,11... | collective-permute-start | bytes 5505032 | tf_op jit(solution)/shard_map/ppermute | solution.py:167
  74.9 12.6 %collective-permute-start.7 = (bf16[128,5376]{1,0:T(8,128)(2,1)S(1)}, bf16[128,5376]{1,0:T(8,128)(2,1)S(1)}, u32[]{:S(2)}, u32[]{:S(2)}) collective-permute-start(bf16[128,5376]{1,0:T(8,128)(2,1)S(1)} %split_rows.2.refs_0_), channel_id=1, source_target_pairs={{0,1},{1,0},{2,3},{3,2},{4,5},{5,4},{6,7},{7,6},{8,9},{9,8},{10,11... | collective-permute-start | bytes 4128776 | tf_op jit(solution)/shard_map/ppermute | solution.py:167
  75.0 12.5 %collective-permute-start.9 = (bf16[128,5376]{1,0:T(8,128)(2,1)}, bf16[128,5376]{1,0:T(8,128)(2,1)S(1)}, u32[]{:S(2)}, u32[]{:S(2)}) collective-permute-start(bf16[128,5376]{1,0:T(8,128)(2,1)} %collective-permute-done.6.refs_2_), channel_id=1, source_target_pairs={{0,1},{1,0},{2,3},{3,2},{4,5},{5,4},{6,7},{7,6},{8,9},{9,8},{10,11... | collective-permute-start | bytes 4128776 | tf_op jit(solution)/shard_map/ppermute | solution.py:167
  78.5 9.0 %collective-permute-start.8 = (bf16[128,5376]{1,0:T(8,128)(2,1)}, bf16[128,5376]{1,0:T(8,128)(2,1)S(1)}, u32[]{:S(2)}, u32[]{:S(2)}) collective-permute-start(bf16[128,5376]{1,0:T(8,128)(2,1)} %collective-permute-done.5.refs_1_), channel_id=1, source_target_pairs={{0,1},{1,0},{2,3},{3,2},{4,5},{5,4},{6,7},{7,6},{8,9},{9,8},{10,11... | collective-permute-start | bytes 4128776 | tf_op jit(solution)/shard_map/ppermute | solution.py:167
  80.9 17.1 %collective-permute-start.11 = (bf16[64,5376]{1,0:T(8,128)(2,1)S(1)}, bf16[64,5376]{1,0:T(8,128)(2,1)S(1)}, u32[]{:S(2)}, u32[]{:S(2)}) collective-permute-start(bf16[64,5376]{1,0:T(8,128)(2,1)S(1)} %slice.27), channel_id=1, source_target_pairs={{0,6},{2,0},{4,2},{6,4},{1,7},{3,1},{5,3},{7,5},{8,14},{10,8},{12,... | collective-permute-start | bytes 2064392 | tf_op jit(solution)/shard_map/ppermute | solution.py:163
  82.2 17.7 %collective-permute-start.10 = (bf16[64,5376]{1,0:T(8,128)(2,1)S(1)}, bf16[64,5376]{1,0:T(8,128)(2,1)S(1)}, u32[]{:S(2)}, u32[]{:S(2)}) collective-permute-start(bf16[64,5376]{1,0:T(8,128)(2,1)S(1)} %slice.26), channel_id=1, source_target_pairs={{0,2},{2,4},{4,6},{6,0},{1,3},{3,5},{5,7},{7,1},{8,10},{10,12},{12... | collective-permute-start | bytes 2064392 | tf_op jit(solution)/shard_map/ppermute | solution.py:163
  99.9 3.6 %collective-permute-start.12 = (bf16[64,5376]{1,0:T(8,128)(2,1)S(1)}, bf16[64,5376]{1,0:T(8,128)(2,1)S(1)}, u32[]{:S(2)}, u32[]{:S(2)}) collective-permute-start(bf16[64,5376]{1,0:T(8,128)(2,1)S(1)} %collective-permute-done.10.refs_0_), channel_id=1, source_target_pairs={{0,1},{1,0},{2,3},{3,2},{4,5},{5,4},{6,7},{7,6},{8,9},{9,8},{10,11... | collective-permute-start | bytes 2064392 | tf_op jit(solution)/shard_map/ppermute | solution.py:167
  101.5 2.8 %collective-permute-start.13 = (bf16[64,5376]{1,0:T(8,128)(2,1)S(1)}, bf16[64,5376]{1,0:T(8,128)(2,1)S(1)}, u32[]{:S(2)}, u32[]{:S(2)}) collective-permute-start(bf16[64,5376]{1,0:T(8,128)(2,1)S(1)} %collective-permute-done.11.refs_1_), channel_id=1, source_target_pairs={{0,1},{1,0},{2,3},{3,2},{4,5},{5,4},{6,7},{7,6},{8,9},{9,8},{10,11... | collective-permute-start | bytes 2064392 | tf_op jit(solution)/shard_map/ppermute | solution.py:167
  101.5 19.1 %collective-permute-start.19 = (bf16[384,768]{1,0:T(8,128)(2,1)S(1)}, bf16[384,768]{1,0:T(8,128)(2,1)S(1)}, u32[]{:S(2)}, u32[]{:S(2)}) collective-permute-start(bf16[384,768]{1,0:T(8,128)(2,1)S(1)} %get-tuple-element.43.hid_a.refs_0_), channel_id=1, source_target_pairs={{0,1},{1,0},{2,3},{3,2},{4,5},{5,4},{6,7},{7,6},{8,9},{9,8},{10,11... | collective-permute-start | bytes 1769480 | tf_op jit(solution)/shard_map/ppermute | solution.py:167
  102.0 15.8 %collective-permute-start.15 = (bf16[384,768]{1,0:T(8,128)(2,1)S(1)}, bf16[384,768]{1,0:T(8,128)(2,1)S(1)}, u32[]{:S(2)}, u32[]{:S(2)}) collective-permute-start(bf16[384,768]{1,0:T(8,128)(2,1)S(1)} %get-tuple-element.43.hid_a.refs_0_), channel_id=1, source_target_pairs={{0,6},{2,0},{4,2},{6,4},{1,7},{3,1},{5,3},{7,5},{8,14},{10,8},{12,... | collective-permute-start | bytes 1769480 | tf_op jit(solution)/shard_map/ppermute | solution.py:163
  102.0 16.2 %collective-permute-start.14 = (bf16[384,768]{1,0:T(8,128)(2,1)S(1)}, bf16[384,768]{1,0:T(8,128)(2,1)S(1)}, u32[]{:S(2)}, u32[]{:S(2)}) collective-permute-start(bf16[384,768]{1,0:T(8,128)(2,1)S(1)} %get-tuple-element.43.hid_a.refs_0_), channel_id=1, source_target_pairs={{0,2},{2,4},{4,6},{6,0},{1,3},{3,5},{5,7},{7,1},{8,10},{10,12},{12... | collective-permute-start | bytes 1769480 | tf_op jit(solution)/shard_map/ppermute | solution.py:163
  118.2 3.3 %collective-permute-start.20 = (bf16[384,768]{1,0:T(8,128)(2,1)S(1)}, bf16[384,768]{1,0:T(8,128)(2,1)S(1)}, u32[]{:S(2)}, u32[]{:S(2)}) collective-permute-start(bf16[384,768]{1,0:T(8,128)(2,1)S(1)} %collective-permute-done.14.refs_1_), channel_id=1, source_target_pairs={{0,1},{1,0},{2,3},{3,2},{4,5},{5,4},{6,7},{7,6},{8,9},{9,8},{10,11... | collective-permute-start | bytes 1769480 | tf_op jit(solution)/shard_map/ppermute | solution.py:167
  119.0 2.5 %collective-permute-start.21 = (bf16[384,768]{1,0:T(8,128)(2,1)S(1)}, bf16[384,768]{1,0:T(8,128)(2,1)S(1)}, u32[]{:S(2)}, u32[]{:S(2)}) collective-permute-start(bf16[384,768]{1,0:T(8,128)(2,1)S(1)} %collective-permute-done.15.refs_2_), channel_id=1, source_target_pairs={{0,1},{1,0},{2,3},{3,2},{4,5},{5,4},{6,7},{7,6},{8,9},{9,8},{10,11... | collective-permute-start | bytes 1769480 | tf_op jit(solution)/shard_map/ppermute | solution.py:167
  119.1 18.2 %collective-permute-start.17 = (bf16[336,768]{1,0:T(8,128)(2,1)S(1)}, bf16[336,768]{1,0:T(8,128)(2,1)S(1)}, u32[]{:S(2)}, u32[]{:S(2)}) collective-permute-start(bf16[336,768]{1,0:T(8,128)(2,1)S(1)} %get-tuple-element.61), channel_id=1, source_target_pairs={{0,6},{2,0},{4,2},{6,4},{1,7},{3,1},{5,3},{7,5},{8,14},{10,8},{12,... | collective-permute-start | bytes 1548296 | tf_op jit(solution)/shard_map/ppermute | solution.py:163
  119.2 18.0 %collective-permute-start.16 = (bf16[336,768]{1,0:T(8,128)(2,1)S(1)}, bf16[336,768]{1,0:T(8,128)(2,1)S(1)}, u32[]{:S(2)}, u32[]{:S(2)}) collective-permute-start(bf16[336,768]{1,0:T(8,128)(2,1)S(1)} %get-tuple-element.62), channel_id=1, source_target_pairs={{0,2},{2,4},{4,6},{6,0},{1,3},{3,5},{5,7},{7,1},{8,10},{10,12},{12... | collective-permute-start | bytes 1548296 | tf_op jit(solution)/shard_map/ppermute | solution.py:163
  120.6 16.6 %collective-permute-start.18 = (bf16[144,768]{1,0:T(8,128)(2,1)S(1)}, bf16[144,768]{1,0:T(8,128)(2,1)S(1)}, u32[]{:S(2)}, u32[]{:S(2)}) collective-permute-start(bf16[144,768]{1,0:T(8,128)(2,1)S(1)} %get-tuple-element.57.refs_6_.refs_0_), channel_id=1, source_target_pairs={{0,4},{2,6},{4,0},{6,2},{1,5},{3,7},{5,1},{7,3},{8,12},{10,14},{12... | collective-permute-start | bytes 663560 | tf_op jit(solution)/shard_map/ppermute | solution.py:163
  137.3 5.0 %collective-permute-start.23 = (bf16[336,768]{1,0:T(8,128)(2,1)S(1)}, bf16[336,768]{1,0:T(8,128)(2,1)S(1)}, u32[]{:S(2)}, u32[]{:S(2)}) collective-permute-start(bf16[336,768]{1,0:T(8,128)(2,1)S(1)} %collective-permute-done.16.refs_2_), channel_id=1, source_target_pairs={{0,1},{1,0},{2,3},{3,2},{4,5},{5,4},{6,7},{7,6},{8,9},{9,8},{10,11... | collective-permute-start | bytes 1548296 | tf_op jit(solution)/shard_map/ppermute | solution.py:167
  139.4 2.9 %collective-permute-start.24 = (bf16[336,768]{1,0:T(8,128)(2,1)S(1)}, bf16[336,768]{1,0:T(8,128)(2,1)S(1)}, u32[]{:S(2)}, u32[]{:S(2)}) collective-permute-start(bf16[336,768]{1,0:T(8,128)(2,1)S(1)} %collective-permute-done.17.refs_3_), channel_id=1, source_target_pairs={{0,1},{1,0},{2,3},{3,2},{4,5},{5,4},{6,7},{7,6},{8,9},{9,8},{10,11... | collective-permute-start | bytes 1548296 | tf_op jit(solution)/shard_map/ppermute | solution.py:167
  139.4 2.6 %collective-permute-start.22 = (bf16[144,768]{1,0:T(8,128)(2,1)S(1)}, bf16[144,768]{1,0:T(8,128)(2,1)S(1)}, u32[]{:S(2)}, u32[]{:S(2)}) collective-permute-start(bf16[144,768]{1,0:T(8,128)(2,1)S(1)} %get-tuple-element.57.refs_6_.refs_0_), channel_id=1, source_target_pairs={{0,1},{1,0},{2,3},{3,2},{4,5},{5,4},{6,7},{7,6},{8,9},{9,8},{10,11... | collective-permute-start | bytes 663560 | tf_op jit(solution)/shard_map/ppermute | solution.py:167
  139.9 2.4 %collective-permute-start.25 = (bf16[144,768]{1,0:T(8,128)(2,1)S(1)}, bf16[144,768]{1,0:T(8,128)(2,1)S(1)}, u32[]{:S(2)}, u32[]{:S(2)}) collective-permute-start(bf16[144,768]{1,0:T(8,128)(2,1)S(1)} %collective-permute-done.18.refs_4_), channel_id=1, source_target_pairs={{0,1},{1,0},{2,3},{3,2},{4,5},{5,4},{6,7},{7,6},{8,9},{9,8},{10,11... | collective-permute-start | bytes 663560 | tf_op jit(solution)/shard_map/ppermute | solution.py:167
